TPU v7x, 32 devices: a whole 2x2x4 slice. The times are simulated.
32 devices in a mesh: row: 4 (over z), col: 8 (over y, x, core).
Axes of the slice: x: 2, y: 2, z: 4, core: 2. Of those that a mesh axis runs over, the one named last changes fastest.
Arguments:
- trailing: float32 [16384, 16384], P('row', 'col'), may hold values from -6 to 6
- panel_factors: float32 [1024, 16384], P('col', 'row'), may hold values from -1.2 to 1.2
- vectors_t: float32 [16, 64, 512], P('col'), may hold values from -0.25 to 0.25
- inverse_lower_factors: float32 [16, 512, 512], P('col', 'row'), as said below
- slot_of_panel: int32 [16], replicated, may hold values from 0 to 15, each once
Outputs:
- updated: float32 [16384, 16384], P('row', 'col')
Inputs may be any that keep to these rules, and one draw needn't show every extreme that they name: `slot_of_panel`: a permutation of the panels' slots. `inverse_lower_factors`: each slot's matrix is lower triangular with a positive diagonal.
All inputs are finite; a program needn't handle non-finite values.
Results may differ from a plain program's by a relative error of at most 0.000075.
Values sent between devices are 32-bit elements; how exact they have to be, the bound alone decides.
No kernel may reach another device: no remote copies, remote signals or barrier semaphores. Data moves between devices by JAX's collectives and lax.ppermute only.
A program may use at most 256 MiB of HBM per device.

v0:
```python
import functools

import jax
import jax.numpy as jnp
from jax import lax
from jax.experimental import pallas as pl
from jax.experimental.pallas import tpu as pltpu
from jax.sharding import PartitionSpec as P

HOPPED = (6, 2)
GATHERED = ((0, 3), (3, 3))
ORDER = ((1, 0, 3), (0, 6, 2), (2, 4, 2), (2, 3, 1))
HIGHEST = lax.Precision.HIGHEST
SCALE_VMEM = 48 * 1024 * 1024
UPDATE_VMEM = 48 * 1024 * 1024
EARLY = pl.CostEstimate(flops=1, bytes_accessed=1, transcendentals=0)


def split(x):
    hi = x.astype(jnp.bfloat16)
    return hi, (x - hi.astype(jnp.float32)).astype(jnp.bfloat16)


def dot3(a_hi, a_lo, b_hi, b_lo):
    dot = functools.partial(jnp.dot, preferred_element_type=jnp.float32)
    return dot(a_hi, b_hi) + (dot(a_hi, b_lo) + dot(a_lo, b_hi))


def scale_kernel(place, *refs):
    parts, cores, (hi, lo) = refs[:4], refs[4], refs[-2:]
    group = jnp.concatenate([part[...] for part in parts], axis=0)
    scaled = dot3(*split(cores[0]), *split(group))
    hi[...], lo[...] = split(scaled.T)


def scale_into(place, parts, cores, line, previous, depth):
    width = parts[0][0].shape[1]
    rows = cores.shape[1]
    half = rows // 4
    tile = min(width, 1024)
    block = pl.BlockSpec((tile, rows), lambda i, place: (i, place[0]))
    shape = jax.ShapeDtypeStruct((width, depth), jnp.bfloat16)
    held = [] if previous is None else list(previous)
    return pl.pallas_call(
        scale_kernel,
        grid_spec=pltpu.PrefetchScalarGridSpec(
            num_scalar_prefetch=1,
            grid=(width // tile,),
            in_specs=[
                pl.BlockSpec((half, tile), functools.partial(lambda at, i, place: (at, i), at))
                for _, at in parts
            ]
            + [pl.BlockSpec((1, rows, rows), lambda i, place: (line, 0, 0))]
            + [pl.BlockSpec(memory_space=pl.ANY)] * len(held),
            out_specs=[block, block],
        ),
        out_shape=[shape, shape],
        input_output_aliases={} if previous is None else {6: 0, 7: 1},
        compiler_params=pltpu.CompilerParams(vmem_limit_bytes=SCALE_VMEM),
        cost_estimate=EARLY,
    )(place, *(a for a, _ in parts), cores, *held)


def blocks_kernel(per_col, col, slots, *refs):
    near, far, (out, held) = refs[:-3], refs[-3], refs[-2:]
    lines = len(near)
    rank = held.shape[1]
    together = 2 * per_col
    for s in range(lines):
        held[s * together : s * together + per_col] = near[s][...]
        held[s * together + per_col : (s + 1) * together] = far[s * per_col : (s + 1) * per_col]
    out[...] = jnp.zeros_like(out)
    me = col[0]
    for s in range(lines):
        for t in range(together):
            owner = me ^ (2 * s + t // per_col)
            slot = slots[owner * per_col + t % per_col]
            block = held[((slot // per_col) ^ me) * per_col + slot % per_col]
            row = (t + (me % 2) * per_col) % together
            out[s, pl.ds(pl.multiple_of(row * rank, rank), rank), t * rank : (t + 1) * rank] = block


def diagonal_blocks(col, slots, near, far):
    per_col, rank, _ = near[0].shape
    lines = len(near)
    size = 2 * per_col * rank
    return pl.pallas_call(
        functools.partial(blocks_kernel, per_col),
        grid_spec=pltpu.PrefetchScalarGridSpec(
            num_scalar_prefetch=2,
            grid=(1,),
            in_specs=[pl.BlockSpec(x.shape, lambda i, col, slots: (0, 0, 0)) for x in (*near, far)],
            out_specs=pl.BlockSpec((lines, size, size), lambda i, col, slots: (0, 0, 0)),
            scratch_shapes=[pltpu.VMEM((2 * lines * per_col, rank, rank), jnp.float32)],
        ),
        out_shape=jax.ShapeDtypeStruct((lines, size, size), jnp.float32),
        compiler_params=pltpu.CompilerParams(vmem_limit_bytes=SCALE_VMEM),
        cost_estimate=EARLY,
    )(col, slots, *near, far)


def lay_kernel(planes, plane, *refs):
    sources, out, sems = refs[: 2 * planes - 1], refs[-2], refs[-1]
    blocks = out.shape[0] // planes
    for z in range(planes):

        @pl.when(plane[0] == z)
        def _():
            copies = [
                pltpu.make_async_copy(
                    sources[planes - 1 + q - z], out.at[pl.ds(q * blocks, blocks)], sems.at[q]
                )
                for q in range(planes)
            ]
            for copy in copies:
                copy.start()
            for copy in copies:
                copy.wait()


def lay(plane, sources):
    planes = (len(sources) + 1) // 2
    shape = sources[0].shape
    return pl.pallas_call(
        functools.partial(lay_kernel, planes),
        grid_spec=pltpu.PrefetchScalarGridSpec(
            num_scalar_prefetch=1,
            grid=(1,),
            in_specs=[pl.BlockSpec(memory_space=pl.ANY)] * len(sources),
            out_specs=pl.BlockSpec((planes * shape[0], *shape[1:]), lambda i, plane: (0, 0, 0)),
            scratch_shapes=[pltpu.SemaphoreType.DMA((planes,))],
        ),
        out_shape=jax.ShapeDtypeStruct((planes * shape[0], *shape[1:]), jnp.float32),
        compiler_params=pltpu.CompilerParams(vmem_limit_bytes=SCALE_VMEM),
        cost_estimate=EARLY,
    )(plane, *sources)


def update_kernel(trailing, hi, lo, right, *refs):
    out, right_hi, right_lo = refs[-3:]

    @pl.when(pl.program_id(0) == 0)
    def _():
        right_hi[...], right_lo[...] = split(right[...])

    out[...] = trailing[...] - dot3(hi[...], lo[...], right_hi[...], right_lo[...])


def update_chunk(start, trailing, left, right, previous):
    height = trailing.shape[0]
    depth, wide = right.shape
    tile = min(height, 512)
    here = pl.BlockSpec((tile, wide), lambda i: (i, start // wide))
    side = pl.BlockSpec((tile, depth), lambda i: (i, 0))
    held = [] if previous is None else [previous]
    return pl.pallas_call(
        update_kernel,
        grid=(height // tile,),
        in_specs=[here, side, side, pl.BlockSpec((depth, wide), lambda i: (0, 0))]
        + [pl.BlockSpec(memory_space=pl.ANY)] * len(held),
        out_specs=here,
        out_shape=jax.ShapeDtypeStruct(trailing.shape, jnp.float32),
        scratch_shapes=[pltpu.VMEM((depth, wide), jnp.bfloat16)] * 2,
        input_output_aliases={} if previous is None else {4: 0},
        compiler_params=pltpu.CompilerParams(vmem_limit_bytes=UPDATE_VMEM),
        cost_estimate=EARLY,
    )(trailing, *left, right, *held)


def body(planes, columns, trailing, panel_factors, vectors_t, inverse_lower_factors, slot_of_panel):
    lines = columns // 2
    rows = panel_factors.shape[0]
    width = trailing.shape[1]
    depth = rows * columns
    halves = columns // planes
    col = lax.axis_index("col")
    line = col // 2

    def across(x, bits):
        return lax.ppermute(x, "col", [(i, i ^ bits) for i in range(columns)])

    def along(x, moves):
        return lax.ppermute(x, "row", moves)

    eighth = width // 8

    def column_chunk(first, count):
        parts = []
        for h in range(halves):
            at = h * width + first * eighth
            parts.append(panel_factors[:, at : at + count * eighth])
        return jnp.stack(parts)

    after = lax.optimization_barrier

    everywhere = [None] + [
        lax.all_gather(column_chunk(*columns_of), "row", axis=0, tiled=True) for columns_of in GATHERED
    ]
    solved = lax.dot_general(
        vectors_t, inverse_lower_factors, (((2,), (2,)), ((0,), (0,))), precision=HIGHEST
    )
    cores = jnp.einsum("fdv,fpv->fdp", solved, solved, precision=HIGHEST)
    bit = 1
    while bit < planes:
        cores = cores + along(cores, [(i, i ^ bit) for i in range(planes)])
        bit *= 2
    bulk, cores = after((panel_factors, cores))
    near = [cores] + [across(cores, 2 * s) for s in range(1, lines)]

    cut = rows // 2
    gathered = [[[bulk], None]] + [[None, None] for _ in range(lines - 1)]
    single = [1 << i for i in range(lines.bit_length() - 1)]
    for s in single:
        gathered[s][0] = [across(bulk, 2 * s)]

    mine, near = after((column_chunk(*HOPPED), near))
    from_above, from_below = [mine], [mine]

    def hop(d):
        from_above.append(along(from_above[-1], [(p, p - 1) for p in range(1, planes - d + 1)]))
        from_below.append(along(from_below[-1], [(p, p + 1) for p in range(d - 1, planes - 1)]))

    hop(1)
    far = across(jnp.concatenate(near), 1)
    gathered[0][1] = [across(bulk, 1)]

    arrived, hopped, far, gathered[0][1] = after(
        ([gathered[s][0] for s in single], (from_above[-1], from_below[-1]), far, gathered[0][1])
    )
    from_above[-1], from_below[-1] = hopped
    for s, x in zip(single, arrived):
        gathered[s][0] = x
    several = sorted((s for s in range(1, lines) if s not in single), key=lambda s: bin(s).count("1"))
    for s in several:
        low, high = s & -s, 1 << (s.bit_length() - 1)
        upper, lower = gathered[s ^ high][0], gathered[s ^ low][0]
        gathered[s][0] = [
            across(upper[0][:cut], 2 * high),
            across(lower[-1][-cut:], 2 * low),
        ]
    hop(2)
    for s in single:
        gathered[s][1] = [across(x, 1) for x in gathered[s][0]]

    arrived, hopped, swapped, everywhere[1] = after(
        (
            [gathered[s][0] for s in several],
            (from_above[-1], from_below[-1]),
            [gathered[s][1] for s in single],
            everywhere[1],
        )
    )
    from_above[-1], from_below[-1] = hopped
    for s, x in zip(several, arrived):
        gathered[s][0] = x
        gathered[s][1] = [across(part, 1) for part in x]
    for s, x in zip(single, swapped):
        gathered[s][1] = x
    for d in range(3, planes):
        hop(d)

    def exchange(number):
        source, first, count = ORDER[number]
        sent = everywhere[source]
        if source and GATHERED[source - 1][1] != count:
            at = (first - GATHERED[source - 1][0]) * eighth
            sent = sent[:, :, at : at + count * eighth]
        chunk = lax.all_to_all(sent, "col", split_axis=0, concat_axis=0, tiled=True)
        return chunk.reshape(depth, -1)

    chunks = [exchange(0)]
    blocks = diagonal_blocks(col.astype(jnp.int32).reshape(1), slot_of_panel, near, far)

    left = None
    for s in range(lines):
        place = (line ^ s).astype(jnp.int32).reshape(1)
        parts = []
        for group in gathered[s]:
            parts += [(group[0], 0), (group[0], 1)] if len(group) == 1 else [(x, 0) for x in group]
        left = scale_into(place, parts, blocks, s, left, depth)

    plane = lax.axis_index("row").astype(jnp.int32).reshape(1)
    everywhere[0] = lay(plane, from_below[:0:-1] + [mine] + from_above[1:])
    everywhere[0], left = after((everywhere[0], left))
    chunks.append(exchange(1))
    updated = None
    for number, (_, first, _) in enumerate(ORDER):
        updated = update_chunk(first * eighth, trailing, left, chunks[number], updated)
        if number + 2 < len(ORDER):
            source = ORDER[number + 2][0]
            everywhere[source], updated = after((everywhere[source], updated))
            chunks.append(exchange(number + 2))
    return updated


def solution(mesh):
    planes, columns = mesh.shape["row"], mesh.shape["col"]
    if columns != 2 * planes or planes & (planes - 1):
        raise ValueError("unsupported mesh")
    return jax.shard_map(
        functools.partial(body, planes, columns),
        mesh=mesh,
        in_specs=(
            P("row", "col"),
            P("col", "row"),
            P("col", None, None),
            P("col", "row", None),
            P(),
        ),
        out_specs=P("row", "col"),
        check_vma=False,
    )
```

profile of v0, /device:TPU:0, one launch (start us, length us, event | category | flops | bytes accessed | tf_op | source)
XLA Modules:
  0.0 307.7 jit_solution(16677705617104491859)
XLA Ops:
  6.5 2.6 slice_bitcast_fusion.1
  9.1 0.9 pad_maximum_fusion
  11.0 3.1 %collective-permute-start = (f32[2,64,64]{2,1,0:T(8,128)S(1)}, f32[2,64,64]{2,1,0:T(8,128)S(1)}, u32[]{:S(2)}, u32[]{:S(2)}) collective-permute-start(f32[2,64,64]{2,1,0:T(8,128)S(1)} %fusion.1), channel_id=1, source_target_pairs={{0,8},{8,0},{16,24},{24,16},{1,9},{9,1},{17,25},{25,17},{2,10},{10... | collective-permute-start | bytes 98312 | tf_op jit(solution)/shard_map/ppermute | solution.py:183
  14.1 2.2 collective-permute-done
  16.4 3.1 %collective-permute-start.1 = (f32[2,64,64]{2,1,0:T(8,128)S(1)}, f32[2,64,64]{2,1,0:T(8,128)S(1)}, u32[]{:S(2)}, u32[]{:S(2)}) collective-permute-start(f32[2,64,64]{2,1,0:T(8,128)S(1)} %add.7), channel_id=1, source_target_pairs={{0,16},{8,24},{16,0},{24,8},{1,17},{9,25},{17,1},{25,9},{2,18},{10... | collective-permute-start | bytes 98312 | tf_op jit(solution)/shard_map/ppermute | solution.py:183
  19.5 2.2 collective-permute-done.1
  21.8 1.9 collective-permute-start.3
  23.8 1.5 collective-permute-start.2
  25.5 1.9 collective-permute-start.5
  27.4 45.3 %collective-permute-done.6.refs_3_ = f32[2,64,64]{2,1,0:T(8,128)S(1)} collective-permute-done((f32[2,64,64]{2,1,0:T(8,128)S(1)}, f32[2,64,64]{2,1,0:T(8,128)S(1)}, u32[]{:S(2)}, u32[]{:S(2)}) %collective-permute-start.6) | collective-permute-done | bytes 32800 | tf_op jit(solution)/shard_map/ppermute | solution.py:180
  72.7 1.7 collective-permute-start.4
  74.4 2.5 collective-permute-done.4.refs_1_
  78.2 6.7 %collective-permute-start.8 = (f32[2,128,512]{2,1,0:T(8,128)S(1)}, f32[2,128,512]{2,1,0:T(8,128)S(1)}, u32[]{:S(2)}, u32[]{:S(2)}) collective-permute-start(f32[2,128,512]{2,1,0:T(8,128)S(1)} %pad_maximum_fusion.2.refs_3_), channel_id=1, source_target_pairs={{0,8},{8,16},{16,24},{1,9},{9,17},{17,25},{2,10},{10,18},{18,26},{... | collective-permute-start | bytes 1572872 | tf_op jit(solution)/shard_map/ppermute | solution.py:183
  85.0 1.3 collective-permute-start.7
  86.3 10.5 %collective-permute-done.8.refs_2_ = f32[2,128,512]{2,1,0:T(8,128)S(1)} collective-permute-done((f32[2,128,512]{2,1,0:T(8,128)S(1)}, f32[2,128,512]{2,1,0:T(8,128)S(1)}, u32[]{:S(2)}, u32[]{:S(2)}) %collective-permute-start.8) | collective-permute-done | bytes 524320 | tf_op jit(solution)/shard_map/ppermute | solution.py:183
  96.8 4.2 %collective-permute-done.7.refs_4_ = f32[2,128,512]{2,1,0:T(8,128)S(1)} collective-permute-done((f32[2,128,512]{2,1,0:T(8,128)S(1)}, f32[2,128,512]{2,1,0:T(8,128)S(1)}, u32[]{:S(2)}, u32[]{:S(2)}) %collective-permute-start.7) | collective-permute-done | bytes 524320 | tf_op jit(solution)/shard_map/ppermute | solution.py:183
  100.9 1.3 copy-done.3
  102.8 1.3 collective-permute-start.13
  104.8 2.3 slice.32
  107.1 2.3 slice.33
  110.0 1.6 collective-permute-start.11
  111.7 7.5 %collective-permute-done.13.refs_5_ = f32[2,128,512]{2,1,0:T(8,128)} collective-permute-done((f32[2,128,512]{2,1,0:T(8,128)S(1)}, f32[2,128,512]{2,1,0:T(8,128)}, u32[]{:S(2)}, u32[]{:S(2)}) %collective-permute-start.13) | collective-permute-done | bytes 524320 | tf_op jit(solution)/shard_map/ppermute | solution.py:183
  119.2 1.5 collective-permute-start.14
  120.6 0.8 copy-done.6
  121.4 1.0 pad_maximum_fusion.1
  122.5 12.5 %collective-permute-done.12.refs_1_ = f32[64,4096]{1,0:T(8,128)} collective-permute-done((f32[64,4096]{1,0:T(8,128)}, f32[64,4096]{1,0:T(8,128)}, u32[]{:S(2)}, u32[]{:S(2)}) %collective-permute-start.12) | collective-permute-done | bytes 1048608 | tf_op jit(solution)/shard_map/ppermute | solution.py:180
  135.2 4.5 %all-to-all-start = ((f32[8,128,768]{2,1,0:T(8,128)}), f32[8,128,768]{2,1,0:T(8,128)}, u32[]{:S(2)}, u32[]{:S(2)}) async-start(f32[8,128,768]{2,1,0:T(8,128)} %all-gather.3.cloned.1.call-done), calls=%async_computation | async-start | bytes 6291456 | tf_op jit(solution)/shard_map/all_to_all | solution.py:268
  140.3 1.5 collective-permute-start.17
  141.7 1.3 collective-permute-start.18
  143.1 0.8 shard_map.56.refs_4_
  143.9 1.6 copy-done.4
  145.5 4.7 %shard_map.57 = (bf16[4096,1024]{1,0:T(8,128)(2,1)}, bf16[4096,1024]{1,0:T(8,128)(2,1)}) custom-call(s32[1]{0:T(128)} %bitcast.9.place, f32[128,4096]{1,0:T(8,128)S(1)} %copy-done.2, f32[128,4096]{1,0:T(8,128)S(1)} %copy-done.2, f32[128,4096]{1,0:T(8,128)S(1)} %copy-done.4, f32[128,4096]{1,0:T(8,128)S(1)} %copy-done.4, f32[4,256,256]{2,1,0:T(8,128)S(1)} %shard_map.56.refs_4_), custom_call_target="tpu_custom_call" | custom-call | flops 1 | bytes 1 | tf_op jit(solution)/shard_map/pallas_call | solution.py:44
  150.2 6.3 %shard_map.58 = (bf16[4096,1024]{1,0:T(8,128)(2,1)}, bf16[4096,1024]{1,0:T(8,128)(2,1)}) custom-call(s32[1]{0:T(128)} %bitcast.8.place, f32[128,4096]{1,0:T(8,128)} %collective-permute-done.2.refs_0_.refs_1_, f32[128,4096]{1,0:T(8,128)} %collective-permute-done.2.refs_0_.refs_1_, ...), custom_call_target="tpu_custom_call", output_to_operand_aliasing={{0}: (6, {}), {1}: (7, {})} | custom-call | flops 1 | bytes 1 | tf_op jit(solution)/shard_map/pallas_call | solution.py:44
  156.5 6.4 %shard_map.59 = (bf16[4096,1024]{1,0:T(8,128)(2,1)}, bf16[4096,1024]{1,0:T(8,128)(2,1)}) custom-call(s32[1]{0:T(128)} %bitcast.7.place, f32[128,4096]{1,0:T(8,128)} %collective-permute-done.3.refs_0_.refs_1_, f32[128,4096]{1,0:T(8,128)} %collective-permute-done.3.refs_0_.refs_1_, ...), custom_call_target="tpu_custom_call", output_to_operand_aliasing={{0}: (6, {}), {1}: (7, {})} | custom-call | flops 1 | bytes 1 | tf_op jit(solution)/shard_map/pallas_call | solution.py:44
  162.9 26.0 %collective-permute-done.18.refs_6_ = f32[2,128,512]{2,1,0:T(8,128)} collective-permute-done((f32[2,128,512]{2,1,0:T(8,128)}, f32[2,128,512]{2,1,0:T(8,128)}, u32[]{:S(2)}, u32[]{:S(2)}) %collective-permute-start.18) | collective-permute-done | bytes 524320 | tf_op jit(solution)/shard_map/ppermute | solution.py:183
  188.9 1.3 shard_map.55
  190.2 1.3 copy-done.5
  191.5 6.3 %shard_map.60 = (bf16[4096,1024]{1,0:T(8,128)(2,1)}, bf16[4096,1024]{1,0:T(8,128)(2,1)}) custom-call(s32[1]{0:T(128)} %bitcast.5.place, f32[64,4096]{1,0:T(8,128)} %collective-permute-done.11.refs_0_, f32[64,4096]{1,0:T(8,128)} %collective-permute-done.12.refs_1_, ...), custom_call_target="tpu_custom_call", output_to_operand_aliasing={{0}: (6, {}), {1}: (7, {})} | custom-call | flops 1 | bytes 1 | tf_op jit(solution)/shard_map/pallas_call | solution.py:44
  197.8 4.0 %all-to-all-start.1 = ((f32[8,128,512]{2,1,0:T(8,128)}), f32[8,128,512]{2,1,0:T(8,128)S(1)}, u32[]{:S(2)}, u32[]{:S(2)}) async-start(f32[8,128,512]{2,1,0:T(8,128)} %copy-done.5), calls=%async_computation.1 | async-start | bytes 4194304 | tf_op jit(solution)/shard_map/all_to_all | solution.py:268
  201.7 26.1 %shard_map.61.refs_0_ = f32[4096,2048]{1,0:T(8,128)} custom-call(f32[4096,2048]{1,0:T(8,128)} %trailing.7, bf16[4096,1024]{1,0:T(8,128)(2,1)} %get-tuple-element.67.hi, bf16[4096,1024]{1,0:T(8,128)(2,1)} %get-tuple-element.68.lo, f32[1024,768]{1,0:T(8,128)} %bitcast.12.right), custom_call_target="tpu_custom_call" | custom-call | flops 1 | bytes 1 | tf_op jit(solution)/shard_map/pallas_call | solution.py:156
  227.8 3.1 %slice.39 = f32[8,128,512]{2,1,0:T(8,128)} slice(f32[8,128,768]{2,1,0:T(8,128)} %all-gather.5.cloned.1.call-done), slice={[0:8], [0:128], [256:768]} | slice | bytes 4194304 | tf_op jit(solution)/shard_map/slice | solution.py:267
  231.0 4.3 %all-to-all-start.3 = ((f32[8,128,512]{2,1,0:T(8,128)}), f32[8,128,512]{2,1,0:T(8,128)}, u32[]{:S(2)}, u32[]{:S(2)}) async-start(f32[8,128,512]{2,1,0:T(8,128)} %slice.39), calls=%async_computation.3 | async-start | bytes 4194304 | tf_op jit(solution)/shard_map/all_to_all | solution.py:268
  235.3 19.1 %shard_map.62.refs_0_ = f32[4096,2048]{1,0:T(8,128)} custom-call(f32[4096,2048]{1,0:T(8,128)} %trailing.7, bf16[4096,1024]{1,0:T(8,128)(2,1)} %get-tuple-element.67.hi, bf16[4096,1024]{1,0:T(8,128)(2,1)} %get-tuple-element.68.lo, f32[1024,512]{1,0:T(8,128)S(1)} %bitcast.26, f32[4096,2048]{1,0:T(8,128)} %shard_map.61.refs_0_), custom_call_target="tpu_custom_call", output_to_operand_aliasing={{}: (4, {})} | custom-call | flops 1 | bytes 1 | tf_op jit(solution)/shard_map/pallas_call | solution.py:156
  254.4 2.3 slice.38
  256.7 5.3 %all-to-all-done.3 = f32[8,128,512]{2,1,0:T(8,128)} async-done(((f32[8,128,512]{2,1,0:T(8,128)}), f32[8,128,512]{2,1,0:T(8,128)}, u32[]{:S(2)}, u32[]{:S(2)}) %all-to-all-start.3) | async-done | bytes 2097184 | tf_op jit(solution)/shard_map/all_to_all | solution.py:268
  262.0 4.2 %all-to-all-start.2 = ((f32[8,128,256]{2,1,0:T(8,128)}), f32[8,128,256]{2,1,0:T(8,128)}, u32[]{:S(2)}, u32[]{:S(2)}) async-start(f32[8,128,256]{2,1,0:T(8,128)} %slice.38), calls=%async_computation.2 | async-start | bytes 2097152 | tf_op jit(solution)/shard_map/all_to_all | solution.py:268
  266.2 20.1 %shard_map.63.refs_0_ = f32[4096,2048]{1,0:T(8,128)} custom-call(f32[4096,2048]{1,0:T(8,128)} %trailing.7, bf16[4096,1024]{1,0:T(8,128)(2,1)} %get-tuple-element.67.hi, bf16[4096,1024]{1,0:T(8,128)(2,1)} %get-tuple-element.68.lo, f32[1024,512]{1,0:T(8,128)} %bitcast.15.right, f32[4096,2048]{1,0:T(8,128)} %shard_map.62.refs_0_), custom_call_target="tpu_custom_call", output_to_operand_aliasing={{}: (4, {})} | custom-call | flops 1 | bytes 1 | tf_op jit(solution)/shard_map/pallas_call | solution.py:156
  286.4 14.5 %shard_map.64 = f32[4096,2048]{1,0:T(8,128)} custom-call(f32[4096,2048]{1,0:T(8,128)} %trailing.7, bf16[4096,1024]{1,0:T(8,128)(2,1)} %get-tuple-element.67.hi, bf16[4096,1024]{1,0:T(8,128)(2,1)} %get-tuple-element.68.lo, f32[1024,256]{1,0:T(8,128)} %bitcast.14.right, f32[4096,2048]{1,0:T(8,128)} %shard_map.63.refs_0_), custom_call_target="tpu_custom_call", output_to_operand_aliasing={{}: (4, {})} | custom-call | flops 1 | bytes 1 | tf_op jit(solution)/shard_map/pallas_call | solution.py:156
  (68 shorter events, 5.4 us)
Async XLA Ops:
  6.5 3.6 %copy-start = (f32[2,128,512]{2,1,0:T(8,128)S(1)}, f32[2,128,512]{2,1,0:T(8,128)}, u32[]{:S(2)}) copy-start(f32[2,128,512]{2,1,0:T(8,128)} %param.8) | copy-start | bytes 1572868
  6.5 15.2 %copy-start.2 = (f32[128,4096]{1,0:T(8,128)S(1)}, f32[128,4096]{1,0:T(8,128)}, u32[]{:S(2)}) copy-start(f32[128,4096]{1,0:T(8,128)} %refs_1_) | copy-start | bytes 6291460
  6.5 3.6 %copy-start.17 = (f32[2,64,512]{2,1,0:T(8,128)S(1)}, f32[2,64,512]{2,1,0:T(8,128)}, u32[]{:S(2)}) copy-start(f32[2,64,512]{2,1,0:T(8,128)} %param.7) | copy-start | bytes 786436
  6.5 128.7 %all-gather.3.cloned.1.call-start = ((), (), s32[]{:S(2)}) async-start(), calls=%async_computation.4 | async-start | bytes 3932160 | tf_op jit(solution)/shard_map/all_gather | solution.py:197
  10.1 217.8 %all-gather.5.cloned.1.call-start = ((), (), s32[]{:S(2)}) async-start(), calls=%async_computation.5 | async-start | bytes 3932160 | tf_op jit(solution)/shard_map/all_gather | solution.py:197
  11.0 5.3 %collective-permute-start = (f32[2,64,64]{2,1,0:T(8,128)S(1)}, f32[2,64,64]{2,1,0:T(8,128)S(1)}, u32[]{:S(2)}, u32[]{:S(2)}) collective-permute-start(f32[2,64,64]{2,1,0:T(8,128)S(1)} %fusion.1), channel_id=1, source_target_pairs={{0,8},{8,0},{16,24},{24,16},{1,9},{9,1},{17,25},{25,17},{2,10},{10... | collective-permute-start | bytes 98312 | tf_op jit(solution)/shard_map/ppermute | solution.py:183
  16.4 5.3 %collective-permute-start.1 = (f32[2,64,64]{2,1,0:T(8,128)S(1)}, f32[2,64,64]{2,1,0:T(8,128)S(1)}, u32[]{:S(2)}, u32[]{:S(2)}) collective-permute-start(f32[2,64,64]{2,1,0:T(8,128)S(1)} %add.7), channel_id=1, source_target_pairs={{0,16},{8,24},{16,0},{24,8},{1,17},{9,25},{17,1},{25,9},{2,18},{10... | collective-permute-start | bytes 98312 | tf_op jit(solution)/shard_map/ppermute | solution.py:183
  21.8 79.2 %collective-permute-start.10 = (f32[128,4096]{1,0:T(8,128)S(1)}, f32[128,4096]{1,0:T(8,128)S(1)}, u32[]{:S(2)}, u32[]{:S(2)}) collective-permute-start(f32[128,4096]{1,0:T(8,128)S(1)} %copy-done.2), channel_id=1, source_target_pairs={{0,1},{1,0},{2,3},{3,2},{4,5},{5,4},{6,7},{7,6},{8,9},{9,8},{10,11... | collective-permute-start | bytes 6291464 | tf_op jit(solution)/shard_map/ppermute | solution.py:180
  21.8 80.4 %collective-permute-start.3 = (f32[128,4096]{1,0:T(8,128)S(1)}, f32[128,4096]{1,0:T(8,128)}, u32[]{:S(2)}, u32[]{:S(2)}) collective-permute-start(f32[128,4096]{1,0:T(8,128)S(1)} %copy-done.2), channel_id=1, source_target_pairs={{0,4},{1,5},{2,6},{3,7},{4,0},{5,1},{6,2},{7,3},{8,12},{9,13},{10,... | collective-permute-start | bytes 6291464 | tf_op jit(solution)/shard_map/ppermute | solution.py:180
  23.8 78.5 %collective-permute-start.2 = (f32[128,4096]{1,0:T(8,128)S(1)}, f32[128,4096]{1,0:T(8,128)}, u32[]{:S(2)}, u32[]{:S(2)}) collective-permute-start(f32[128,4096]{1,0:T(8,128)S(1)} %copy-done.2), channel_id=1, source_target_pairs={{0,2},{1,3},{2,0},{3,1},{4,6},{5,7},{6,4},{7,5},{8,10},{9,11},{10,... | collective-permute-start | bytes 6291464 | tf_op jit(solution)/shard_map/ppermute | solution.py:180
  25.2 47.4 %collective-permute-start.6 = (f32[2,64,64]{2,1,0:T(8,128)S(1)}, f32[2,64,64]{2,1,0:T(8,128)S(1)}, u32[]{:S(2)}, u32[]{:S(2)}) collective-permute-start(f32[2,64,64]{2,1,0:T(8,128)S(1)} %add.8.refs_0_), channel_id=1, source_target_pairs={{0,6},{1,7},{2,4},{3,5},{4,2},{5,3},{6,0},{7,1},{8,14},{9,15},{10,... | collective-permute-start | bytes 98312 | tf_op jit(solution)/shard_map/ppermute | solution.py:180
  25.4 96.0 %copy-start.15 = (f32[1,128,768]{2,1,0:T(8,128)S(1)}, f32[1,128,768]{2,1,0:T(8,128)}, u32[]{:S(2)}) copy-start(f32[1,128,768]{2,1,0:T(8,128)} %get-tuple-element.75) | copy-start | bytes 1179652
  25.4 96.0 %copy-start.16 = (f32[1,128,768]{2,1,0:T(8,128)S(1)}, f32[1,128,768]{2,1,0:T(8,128)}, u32[]{:S(2)}) copy-start(f32[1,128,768]{2,1,0:T(8,128)} %get-tuple-element.78) | copy-start | bytes 1179652
  25.5 49.0 %collective-permute-start.5 = (f32[2,64,64]{2,1,0:T(8,128)S(1)}, f32[2,64,64]{2,1,0:T(8,128)S(1)}, u32[]{:S(2)}, u32[]{:S(2)}) collective-permute-start(f32[2,64,64]{2,1,0:T(8,128)S(1)} %add.8.refs_0_), channel_id=1, source_target_pairs={{0,4},{1,5},{2,6},{3,7},{4,0},{5,1},{6,2},{7,3},{8,12},{9,13},{10,... | collective-permute-start | bytes 98312 | tf_op jit(solution)/shard_map/ppermute | solution.py:180
  72.7 4.3 %collective-permute-start.4 = (f32[2,64,64]{2,1,0:T(8,128)S(1)}, f32[2,64,64]{2,1,0:T(8,128)S(1)}, u32[]{:S(2)}, u32[]{:S(2)}) collective-permute-start(f32[2,64,64]{2,1,0:T(8,128)S(1)} %add.8.refs_0_), channel_id=1, source_target_pairs={{0,2},{1,3},{2,0},{3,1},{4,6},{5,7},{6,4},{7,5},{8,10},{9,11},{10,... | collective-permute-start | bytes 98312 | tf_op jit(solution)/shard_map/ppermute | solution.py:180
  77.0 0.6 copy-start.10
  77.6 0.6 copy-start.12
  78.2 6.7 %collective-permute-start.9 = (f32[8,64,64]{2,1,0:T(8,128)S(1)}, f32[8,64,64]{2,1,0:T(8,128)S(1)}, u32[]{:S(2)}, u32[]{:S(2)}) collective-permute-start(f32[8,64,64]{2,1,0:T(8,128)S(1)} %pad_maximum_fusion.3), channel_id=1, source_target_pairs={{0,1},{1,0},{2,3},{3,2},{4,5},{5,4},{6,7},{7,6},{8,9},{9,8},{10,11... | collective-permute-start | bytes 393224 | tf_op jit(solution)/shard_map/ppermute | solution.py:180
  78.2 18.5 %collective-permute-start.8 = (f32[2,128,512]{2,1,0:T(8,128)S(1)}, f32[2,128,512]{2,1,0:T(8,128)S(1)}, u32[]{:S(2)}, u32[]{:S(2)}) collective-permute-start(f32[2,128,512]{2,1,0:T(8,128)S(1)} %pad_maximum_fusion.2.refs_3_), channel_id=1, source_target_pairs={{0,8},{8,16},{16,24},{1,9},{9,17},{17,25},{2,10},{10,18},{18,26},{... | collective-permute-start | bytes 1572872 | tf_op jit(solution)/shard_map/ppermute | solution.py:183
  85.0 15.9 %collective-permute-start.7 = (f32[2,128,512]{2,1,0:T(8,128)S(1)}, f32[2,128,512]{2,1,0:T(8,128)S(1)}, u32[]{:S(2)}, u32[]{:S(2)}) collective-permute-start(f32[2,128,512]{2,1,0:T(8,128)S(1)} %pad_maximum_fusion.2.refs_3_), channel_id=1, source_target_pairs={{8,0},{16,8},{24,16},{9,1},{17,9},{25,17},{10,2},{18,10},{26,18},{... | collective-permute-start | bytes 1572872 | tf_op jit(solution)/shard_map/ppermute | solution.py:183
  100.9 1.3 copy-start.3
  102.2 33.0 %collective-permute-start.15 = (f32[128,4096]{1,0:T(8,128)}, f32[128,4096]{1,0:T(8,128)}, u32[]{:S(2)}, u32[]{:S(2)}) collective-permute-start(f32[128,4096]{1,0:T(8,128)} %collective-permute-done.2.refs_0_.refs_1_), channel_id=1, source_target_pairs={{0,1},{1,0},{2,3},{3,2},{4,5},{5,4},{6,7},{7,6},{8,9},{9,8},{10,11... | collective-permute-start | bytes 6291464 | tf_op jit(solution)/shard_map/ppermute | solution.py:180
  102.3 33.0 %collective-permute-start.16 = (f32[128,4096]{1,0:T(8,128)}, f32[128,4096]{1,0:T(8,128)}, u32[]{:S(2)}, u32[]{:S(2)}) collective-permute-start(f32[128,4096]{1,0:T(8,128)} %collective-permute-done.3.refs_0_.refs_1_), channel_id=1, source_target_pairs={{0,1},{1,0},{2,3},{3,2},{4,5},{5,4},{6,7},{7,6},{8,9},{9,8},{10,11... | collective-permute-start | bytes 6291464 | tf_op jit(solution)/shard_map/ppermute | solution.py:180
  102.8 16.4 %collective-permute-start.13 = (f32[2,128,512]{2,1,0:T(8,128)S(1)}, f32[2,128,512]{2,1,0:T(8,128)}, u32[]{:S(2)}, u32[]{:S(2)}) collective-permute-start(f32[2,128,512]{2,1,0:T(8,128)S(1)} %collective-permute-done.7.refs_4_), channel_id=1, source_target_pairs={{8,0},{16,8},{9,1},{17,9},{10,2},{18,10},{11,3},{19,11},{12,4},{20... | collective-permute-start | bytes 1572872 | tf_op jit(solution)/shard_map/ppermute | solution.py:183
  104.0 0.8 copy-start.8
  109.5 25.5 %collective-permute-start.12 = (f32[64,4096]{1,0:T(8,128)}, f32[64,4096]{1,0:T(8,128)}, u32[]{:S(2)}, u32[]{:S(2)}) collective-permute-start(f32[64,4096]{1,0:T(8,128)} %slice.33), channel_id=1, source_target_pairs={{0,2},{1,3},{2,0},{3,1},{4,6},{5,7},{6,4},{7,5},{8,10},{9,11},{10,... | collective-permute-start | bytes 3145736 | tf_op jit(solution)/shard_map/ppermute | solution.py:180
  110.0 25.2 %collective-permute-start.11 = (f32[64,4096]{1,0:T(8,128)}, f32[64,4096]{1,0:T(8,128)}, u32[]{:S(2)}, u32[]{:S(2)}) collective-permute-start(f32[64,4096]{1,0:T(8,128)} %slice.32), channel_id=1, source_target_pairs={{0,4},{1,5},{2,6},{3,7},{4,0},{5,1},{6,2},{7,3},{8,12},{9,13},{10,... | collective-permute-start | bytes 3145736 | tf_op jit(solution)/shard_map/ppermute | solution.py:180
  119.2 3.3 %collective-permute-start.14 = (f32[2,128,512]{2,1,0:T(8,128)S(1)}, f32[2,128,512]{2,1,0:T(8,128)}, u32[]{:S(2)}, u32[]{:S(2)}) collective-permute-start(f32[2,128,512]{2,1,0:T(8,128)S(1)} %collective-permute-done.8.refs_2_), channel_id=1, source_target_pairs={{8,16},{16,24},{9,17},{17,25},{10,18},{18,26},{11,19},{19,27},{12,... | collective-permute-start | bytes 1572872 | tf_op jit(solution)/shard_map/ppermute | solution.py:183
  120.6 0.8 copy-start.6
  122.4 20.6 %copy-start.14 = (s32[16]{0:T(128)S(1)}, s32[16]{0:T(128)}, u32[]{:S(2)}) copy-start(s32[16]{0:T(128)} %slots.1) | copy-start | bytes 196
  122.4 20.6 %copy-start.11 = (f32[2,64,64]{2,1,0:T(8,128)S(1)}, f32[2,64,64]{2,1,0:T(8,128)}, u32[]{:S(2)}) copy-start(f32[2,64,64]{2,1,0:T(8,128)} %copy-done.10) | copy-start | bytes 98308
  122.4 20.6 %copy-start.13 = (f32[2,64,64]{2,1,0:T(8,128)S(1)}, f32[2,64,64]{2,1,0:T(8,128)}, u32[]{:S(2)}) copy-start(f32[2,64,64]{2,1,0:T(8,128)} %copy-done.12) | copy-start | bytes 98308
  135.2 62.5 %all-to-all-start = ((f32[8,128,768]{2,1,0:T(8,128)}), f32[8,128,768]{2,1,0:T(8,128)}, u32[]{:S(2)}, u32[]{:S(2)}) async-start(f32[8,128,768]{2,1,0:T(8,128)} %all-gather.3.cloned.1.call-done), calls=%async_computation | async-start | bytes 6291456 | tf_op jit(solution)/shard_map/all_to_all | solution.py:268
  139.7 51.8 %collective-permute-start.19 = (f32[64,4096]{1,0:T(8,128)}, f32[64,4096]{1,0:T(8,128)}, u32[]{:S(2)}, u32[]{:S(2)}) collective-permute-start(f32[64,4096]{1,0:T(8,128)} %collective-permute-done.11.refs_0_), channel_id=1, source_target_pairs={{0,1},{1,0},{2,3},{3,2},{4,5},{5,4},{6,7},{7,6},{8,9},{9,8},{10,11... | collective-permute-start | bytes 3145736 | tf_op jit(solution)/shard_map/ppermute | solution.py:180
  140.1 51.4 %collective-permute-start.20 = (f32[64,4096]{1,0:T(8,128)}, f32[64,4096]{1,0:T(8,128)}, u32[]{:S(2)}, u32[]{:S(2)}) collective-permute-start(f32[64,4096]{1,0:T(8,128)} %collective-permute-done.12.refs_1_), channel_id=1, source_target_pairs={{0,1},{1,0},{2,3},{3,2},{4,5},{5,4},{6,7},{7,6},{8,9},{9,8},{10,11... | collective-permute-start | bytes 3145736 | tf_op jit(solution)/shard_map/ppermute | solution.py:180
  140.3 22.6 %collective-permute-start.17 = (f32[2,128,512]{2,1,0:T(8,128)}, f32[2,128,512]{2,1,0:T(8,128)}, u32[]{:S(2)}, u32[]{:S(2)}) collective-permute-start(f32[2,128,512]{2,1,0:T(8,128)} %collective-permute-done.14.refs_1_), channel_id=1, source_target_pairs={{16,24},{17,25},{18,26},{19,27},{20,28},{21,29},{22,30},{23,31}} | collective-permute-start | bytes 1572872 | tf_op jit(solution)/shard_map/ppermute | solution.py:183
  141.7 47.1 %collective-permute-start.18 = (f32[2,128,512]{2,1,0:T(8,128)}, f32[2,128,512]{2,1,0:T(8,128)}, u32[]{:S(2)}, u32[]{:S(2)}) collective-permute-start(f32[2,128,512]{2,1,0:T(8,128)} %collective-permute-done.13.refs_5_), channel_id=1, source_target_pairs={{8,0},{9,1},{10,2},{11,3},{12,4},{13,5},{14,6},{15,7}} | collective-permute-start | bytes 1572872 | tf_op jit(solution)/shard_map/ppermute | solution.py:183
  143.9 1.6 copy-start.4
  156.5 32.4 %copy-start.7 = (f32[2,128,512]{2,1,0:T(8,128)S(1)}, f32[2,128,512]{2,1,0:T(8,128)}, u32[]{:S(2)}) copy-start(f32[2,128,512]{2,1,0:T(8,128)} %copy-done.6) | copy-start | bytes 1572868
  156.5 32.4 %copy-start.9 = (f32[2,128,512]{2,1,0:T(8,128)S(1)}, f32[2,128,512]{2,1,0:T(8,128)}, u32[]{:S(2)}) copy-start(f32[2,128,512]{2,1,0:T(8,128)} %copy-done.8) | copy-start | bytes 1572868
  190.2 1.3 copy-start.5
  197.8 33.2 %all-to-all-start.1 = ((f32[8,128,512]{2,1,0:T(8,128)}), f32[8,128,512]{2,1,0:T(8,128)S(1)}, u32[]{:S(2)}, u32[]{:S(2)}) async-start(f32[8,128,512]{2,1,0:T(8,128)} %copy-done.5), calls=%async_computation.1 | async-start | bytes 4194304 | tf_op jit(solution)/shard_map/all_to_all | solution.py:268
  231.0 31.0 %all-to-all-start.3 = ((f32[8,128,512]{2,1,0:T(8,128)}), f32[8,128,512]{2,1,0:T(8,128)}, u32[]{:S(2)}, u32[]{:S(2)}) async-start(f32[8,128,512]{2,1,0:T(8,128)} %slice.39), calls=%async_computation.3 | async-start | bytes 4194304 | tf_op jit(solution)/shard_map/all_to_all | solution.py:268
  262.0 24.4 %all-to-all-start.2 = ((f32[8,128,256]{2,1,0:T(8,128)}), f32[8,128,256]{2,1,0:T(8,128)}, u32[]{:S(2)}, u32[]{:S(2)}) async-start(f32[8,128,256]{2,1,0:T(8,128)} %slice.38), calls=%async_computation.2 | async-start | bytes 2097152 | tf_op jit(solution)/shard_map/all_to_all | solution.py:268
  286.4 14.5 %copy-start.1 = (f32[2,128,512]{2,1,0:T(8,128)S(1)}, f32[2,128,512]{2,1,0:T(8,128)}, u32[]{:S(2)}) copy-start(f32[2,128,512]{2,1,0:T(8,128)} %param.8) | copy-start | bytes 1572868
Sparse Core Ops, SparseCore 0:
  10.2 66.1 all-gather.2
  122.5 72.4 all-gather.4
where the time goes:
time: 309 us; the launch traced here: 308 us
  waiting for transfers between devices  118 us (38%)
  Pallas kernels  106 us (34%)
  starting transfers between devices  47.3 us (15%)
  local copies, waits for them, and re-layouts  19.7 us (6%)
  between operations  13.7 us (4%)
    pallas_call x4, Pallas kernels, update_chunk(): pl.pallas_call(update_kernel, grid=(height // tile,), in_specs=[here, sid...  79.9 us
    ppermute x13, waiting for transfers between devices, across(): return lax.ppermute(x, 'col', [(i, i ^ bits) for i in range(columns)])  60.6 us
    ppermute x8, waiting for transfers between devices, along(): return lax.ppermute(x, 'row', moves)  52.6 us
    pallas_call x4, Pallas kernels, scale_into(): pl.pallas_call(scale_kernel, grid_spec=pltpu.PrefetchScalarGridSpec(num_s...  23.7 us
    ppermute x8, starting transfers between devices, along(): return lax.ppermute(x, 'row', moves)  19.7 us
    all_to_all x4, starting transfers between devices, exchange(): chunk = lax.all_to_all(sent, 'col', split_axis=0, concat_axis=0, tiled=True)  17 us
    ppermute x13, starting transfers between devices, across(): return lax.ppermute(x, 'col', [(i, i ^ bits) for i in range(columns)])  10.5 us
    unnamed x36, local copies, waits for them, and re-layouts  7.08 us
  transfers between devices with their start and end apart: 27, of which 11 were waited for; matrix products, arithmetic and copies ran while one was open for 4% of the time, Pallas kernels for 30%

commit v1 on v0

--- a/solution.py
+++ b/solution.py
@@ -7,9 +7,7 @@
 from jax.experimental.pallas import tpu as pltpu
 from jax.sharding import PartitionSpec as P
 
-HOPPED = (6, 2)
-GATHERED = ((0, 3), (3, 3))
-ORDER = ((1, 0, 3), (0, 6, 2), (2, 4, 2), (2, 3, 1))
+CHUNKS = ((0, 4), (4, 2), (6, 2))
 HIGHEST = lax.Precision.HIGHEST
 SCALE_VMEM = 48 * 1024 * 1024
 UPDATE_VMEM = 48 * 1024 * 1024
@@ -99,43 +97,6 @@
     )(col, slots, *near, far)
 
 
-def lay_kernel(planes, plane, *refs):
-    sources, out, sems = refs[: 2 * planes - 1], refs[-2], refs[-1]
-    blocks = out.shape[0] // planes
-    for z in range(planes):
-
-        @pl.when(plane[0] == z)
-        def _():
-            copies = [
-                pltpu.make_async_copy(
-                    sources[planes - 1 + q - z], out.at[pl.ds(q * blocks, blocks)], sems.at[q]
-                )
-                for q in range(planes)
-            ]
-            for copy in copies:
-                copy.start()
-            for copy in copies:
-                copy.wait()
-
-
-def lay(plane, sources):
-    planes = (len(sources) + 1) // 2
-    shape = sources[0].shape
-    return pl.pallas_call(
-        functools.partial(lay_kernel, planes),
-        grid_spec=pltpu.PrefetchScalarGridSpec(
-            num_scalar_prefetch=1,
-            grid=(1,),
-            in_specs=[pl.BlockSpec(memory_space=pl.ANY)] * len(sources),
-            out_specs=pl.BlockSpec((planes * shape[0], *shape[1:]), lambda i, plane: (0, 0, 0)),
-            scratch_shapes=[pltpu.SemaphoreType.DMA((planes,))],
-        ),
-        out_shape=jax.ShapeDtypeStruct((planes * shape[0], *shape[1:]), jnp.float32),
-        compiler_params=pltpu.CompilerParams(vmem_limit_bytes=SCALE_VMEM),
-        cost_estimate=EARLY,
-    )(plane, *sources)
-
-
 def update_kernel(trailing, hi, lo, right, *refs):
     out, right_hi, right_lo = refs[-3:]
 
@@ -193,9 +154,7 @@
 
     after = lax.optimization_barrier
 
-    everywhere = [None] + [
-        lax.all_gather(column_chunk(*columns_of), "row", axis=0, tiled=True) for columns_of in GATHERED
-    ]
+    everywhere = [lax.all_gather(column_chunk(*c), "row", axis=0, tiled=True) for c in CHUNKS]
     solved = lax.dot_general(
         vectors_t, inverse_lower_factors, (((2,), (2,)), ((0,), (0,))), precision=HIGHEST
     )
@@ -213,21 +172,10 @@
     for s in single:
         gathered[s][0] = [across(bulk, 2 * s)]
 
-    mine, near = after((column_chunk(*HOPPED), near))
-    from_above, from_below = [mine], [mine]
-
-    def hop(d):
-        from_above.append(along(from_above[-1], [(p, p - 1) for p in range(1, planes - d + 1)]))
-        from_below.append(along(from_below[-1], [(p, p + 1) for p in range(d - 1, planes - 1)]))
-
-    hop(1)
     far = across(jnp.concatenate(near), 1)
     gathered[0][1] = [across(bulk, 1)]
 
-    arrived, hopped, far, gathered[0][1] = after(
-        ([gathered[s][0] for s in single], (from_above[-1], from_below[-1]), far, gathered[0][1])
-    )
-    from_above[-1], from_below[-1] = hopped
+    arrived, far, gathered[0][1] = after(([gathered[s][0] for s in single], far, gathered[0][1]))
     for s, x in zip(single, arrived):
         gathered[s][0] = x
     several = sorted((s for s in range(1, lines) if s not in single), key=lambda s: bin(s).count("1"))
@@ -238,34 +186,20 @@
             across(upper[0][:cut], 2 * high),
             across(lower[-1][-cut:], 2 * low),
         ]
-    hop(2)
     for s in single:
         gathered[s][1] = [across(x, 1) for x in gathered[s][0]]
 
-    arrived, hopped, swapped, everywhere[1] = after(
-        (
-            [gathered[s][0] for s in several],
-            (from_above[-1], from_below[-1]),
-            [gathered[s][1] for s in single],
-            everywhere[1],
-        )
+    arrived, swapped, everywhere[0] = after(
+        ([gathered[s][0] for s in several], [gathered[s][1] for s in single], everywhere[0])
     )
-    from_above[-1], from_below[-1] = hopped
     for s, x in zip(several, arrived):
         gathered[s][0] = x
         gathered[s][1] = [across(part, 1) for part in x]
     for s, x in zip(single, swapped):
         gathered[s][1] = x
-    for d in range(3, planes):
-        hop(d)
 
     def exchange(number):
-        source, first, count = ORDER[number]
-        sent = everywhere[source]
-        if source and GATHERED[source - 1][1] != count:
-            at = (first - GATHERED[source - 1][0]) * eighth
-            sent = sent[:, :, at : at + count * eighth]
-        chunk = lax.all_to_all(sent, "col", split_axis=0, concat_axis=0, tiled=True)
+        chunk = lax.all_to_all(everywhere[number], "col", split_axis=0, concat_axis=0, tiled=True)
         return chunk.reshape(depth, -1)
 
     chunks = [exchange(0)]
@@ -279,17 +213,15 @@
             parts += [(group[0], 0), (group[0], 1)] if len(group) == 1 else [(x, 0) for x in group]
         left = scale_into(place, parts, blocks, s, left, depth)
 
-    plane = lax.axis_index("row").astype(jnp.int32).reshape(1)
-    everywhere[0] = lay(plane, from_below[:0:-1] + [mine] + from_above[1:])
-    everywhere[0], left = after((everywhere[0], left))
-    chunks.append(exchange(1))
     updated = None
-    for number, (_, first, _) in enumerate(ORDER):
+    for number, (first, _) in enumerate(CHUNKS):
+        if number + 1 < len(CHUNKS):
+            if updated is None:
+                everywhere[number + 1], left = after((everywhere[number + 1], left))
+            else:
+                everywhere[number + 1], updated = after((everywhere[number + 1], updated))
+            chunks.append(exchange(number + 1))
         updated = update_chunk(first * eighth, trailing, left, chunks[number], updated)
-        if number + 2 < len(ORDER):
-            source = ORDER[number + 2][0]
-            everywhere[source], updated = after((everywhere[source], updated))
-            chunks.append(exchange(number + 2))
     return updated
 
 

time: 309 us -> 261 us (0.84)
  starting transfers between devices: 47.3 us -> 30.4 us
  waiting for transfers between devices: 118 us -> 106 us
  local copies, waits for them, and re-layouts: 19.7 us -> 9.09 us
  Pallas kernels: 106 us -> 97 us
    ppermute x8 -> x2, waiting for transfers between devices: 52.6 us -> 4.49 us  [along(): return lax.ppermute(x, 'row', moves)]
    all_to_all x4 -> x3, waiting for transfers between devices: 5.28 us -> 29.2 us  [exchange(): lax.all_to_all(everywhere[number], 'col', split_axis=0, concat_axis=0, ti...]
    ppermute x8 -> x2, starting transfers between devices: 19.7 us -> 6.18 us  [along(): return lax.ppermute(x, 'row', moves)]
    ppermute x13, waiting for transfers between devices: 60.6 us -> 72.3 us  [across(): return lax.ppermute(x, 'col', [(i, i ^ bits) for i in range(columns)])]
    pallas_call x4 -> x3, Pallas kernels: 79.9 us -> 72.6 us  [update_chunk(): pl.pallas_call(update_kernel, grid=(height // tile,), in_specs=[here, sid...]
    slice x2 -> x0, local copies, waits for them, and re-layouts: 5.4 us -> none  [exchange(): sent = sent[:, :, at:at + count * eighth]]
    all_to_all x4 -> x3, starting transfers between devices: 17 us -> 12.5 us  [exchange(): lax.all_to_all(everywhere[number], 'col', split_axis=0, concat_axis=0, ti...]
    unnamed x36 -> x14, local copies, waits for them, and re-layouts: 7.08 us -> 2.93 us
  transfers between devices with their start and end apart: 27 -> 21, of which waited for: 11 -> 9; matrix products, arithmetic and copies ran while one was open for 4% -> 3% of each run, Pallas kernels for 30% -> 30%
where the time goes in v1:
time: 261 us; the launch traced here: 259 us
  waiting for transfers between devices  106 us (41%)
  Pallas kernels  97 us (37%)
  starting transfers between devices  30.4 us (12%)
  between operations  13.3 us (5%)
  local copies, waits for them, and re-layouts  9.09 us (3%)
  other arithmetic  2.82 us (1%)
    pallas_call x3, Pallas kernels, update_chunk(): pl.pallas_call(update_kernel, grid=(height // tile,), in_specs=[here, sid...  72.6 us
    ppermute x13, waiting for transfers between devices, across(): return lax.ppermute(x, 'col', [(i, i ^ bits) for i in range(columns)])  72.3 us
    all_to_all x3, waiting for transfers between devices, exchange(): lax.all_to_all(everywhere[number], 'col', split_axis=0, concat_axis=0, ti...  29.2 us
    pallas_call x4, Pallas kernels, scale_into(): pl.pallas_call(scale_kernel, grid_spec=pltpu.PrefetchScalarGridSpec(num_s...  23.5 us
    all_to_all x3, starting transfers between devices, exchange(): lax.all_to_all(everywhere[number], 'col', split_axis=0, concat_axis=0, ti...  12.5 us
    ppermute x13, starting transfers between devices, across(): return lax.ppermute(x, 'col', [(i, i ^ bits) for i in range(columns)])  11.6 us
    ppermute x2, starting transfers between devices, along(): return lax.ppermute(x, 'row', moves)  6.18 us
  transfers between devices with their start and end apart: 21, of which 9 were waited for; matrix products, arithmetic and copies ran while one was open for 3% of the time, Pallas kernels for 30%

profile of v1, /device:TPU:0, one launch (start us, length us, event | category | flops | bytes accessed | tf_op | source)
XLA Modules:
  0.0 259.5 jit_solution(2767969817724015270)
XLA Ops:
  6.5 1.5 slice_bitcast_fusion.1
  8.0 1.1 pad_maximum_fusion
  9.1 0.0 all-gather.4.cloned.1.call-start
  9.2 0.7 fusion
  9.9 0.2 fusion.1
  10.1 3.1 %collective-permute-start = (f32[2,64,64]{2,1,0:T(8,128)S(1)}, f32[2,64,64]{2,1,0:T(8,128)S(1)}, u32[]{:S(2)}, u32[]{:S(2)}) collective-permute-start(f32[2,64,64]{2,1,0:T(8,128)S(1)} %fusion.1), channel_id=1, source_target_pairs={{0,8},{8,0},{16,24},{24,16},{1,9},{9,1},{17,25},{25,17},{2,10},{10... | collective-permute-start | bytes 98312 | tf_op jit(solution)/shard_map/ppermute | solution.py:144
  13.2 2.2 collective-permute-done
  15.4 3.1 %collective-permute-start.1 = (f32[2,64,64]{2,1,0:T(8,128)S(1)}, f32[2,64,64]{2,1,0:T(8,128)S(1)}, u32[]{:S(2)}, u32[]{:S(2)}) collective-permute-start(f32[2,64,64]{2,1,0:T(8,128)S(1)} %add.7), channel_id=1, source_target_pairs={{0,16},{8,24},{16,0},{24,8},{1,17},{9,25},{17,1},{25,9},{2,18},{10... | collective-permute-start | bytes 98312 | tf_op jit(solution)/shard_map/ppermute | solution.py:144
  18.5 2.2 collective-permute-done.1
  20.8 0.1 collective-permute-start.8
  20.9 1.9 collective-permute-start.3
  22.8 1.5 collective-permute-start.2
  24.3 0.1 collective-permute-start.6
  24.4 1.9 collective-permute-start.5
  26.3 45.4 %collective-permute-done.6.refs_3_ = f32[2,64,64]{2,1,0:T(8,128)S(1)} collective-permute-done((f32[2,64,64]{2,1,0:T(8,128)S(1)}, f32[2,64,64]{2,1,0:T(8,128)S(1)}, u32[]{:S(2)}, u32[]{:S(2)}) %collective-permute-start.6) | collective-permute-done | bytes 32800 | tf_op jit(solution)/shard_map/ppermute | solution.py:141
  71.7 1.7 collective-permute-start.4
  73.4 2.5 collective-permute-done.4.refs_1_
  76.0 0.1 collective-permute-start.7
  76.1 1.5 collective-permute-done.7.refs_4_
  77.6 1.3 copy-done.3
  78.9 0.1 collective-permute-start.11
  79.1 0.4 collective-permute-start.12
  79.4 2.3 slice.26
  81.8 2.3 slice.27
  84.1 1.7 collective-permute-start.10
  85.8 1.5 collective-permute-start.9
  87.3 0.1 slice_bitcast_fusion.3
  87.4 0.8 pad_maximum_fusion.1
  88.3 21.3 %collective-permute-done.10.refs_1_ = f32[64,4096]{1,0:T(8,128)} collective-permute-done((f32[64,4096]{1,0:T(8,128)}, f32[64,4096]{1,0:T(8,128)}, u32[]{:S(2)}, u32[]{:S(2)}) %collective-permute-start.10) | collective-permute-done | bytes 1048608 | tf_op jit(solution)/shard_map/ppermute | solution.py:141
  109.6 1.4 collective-permute-done.9.refs_0_
  111.1 4.6 %all-to-all-start = ((f32[8,128,1024]{2,1,0:T(8,128)}), f32[8,128,1024]{2,1,0:T(8,128)}, u32[]{:S(2)}, u32[]{:S(2)}) async-start(f32[8,128,1024]{2,1,0:T(8,128)} %all-gather.6.cloned.1.call-done), calls=%async_computation | async-start | bytes 8388608 | tf_op jit(solution)/shard_map/all_to_all | solution.py:202
  115.6 0.0 all-gather.8.cloned.1.call-start
  115.7 0.8 pad_maximum_fusion.2
  116.6 0.4 collective-permute-start.13
  117.0 0.2 collective-permute-start.14
  117.1 0.8 shard_map.55.refs_4_
  117.9 1.6 copy-done.4
  119.5 4.7 %shard_map.56 = (bf16[4096,1024]{1,0:T(8,128)(2,1)}, bf16[4096,1024]{1,0:T(8,128)(2,1)}) custom-call(s32[1]{0:T(128)} %bitcast.8.place, f32[128,4096]{1,0:T(8,128)S(1)} %copy-done.2, f32[128,4096]{1,0:T(8,128)S(1)} %copy-done.2, f32[128,4096]{1,0:T(8,128)S(1)} %copy-done.4, f32[128,4096]{1,0:T(8,128)S(1)} %copy-done.4, f32[4,256,256]{2,1,0:T(8,128)S(1)} %shard_map.55.refs_4_), custom_call_target="tpu_custom_call" | custom-call | flops 1 | bytes 1 | tf_op jit(solution)/shard_map/pallas_call | solution.py:42
  124.2 6.2 %shard_map.57 = (bf16[4096,1024]{1,0:T(8,128)(2,1)}, bf16[4096,1024]{1,0:T(8,128)(2,1)}) custom-call(s32[1]{0:T(128)} %bitcast.7.place, f32[128,4096]{1,0:T(8,128)} %collective-permute-done.2.refs_0_.refs_1_, f32[128,4096]{1,0:T(8,128)} %collective-permute-done.2.refs_0_.refs_1_, ...), custom_call_target="tpu_custom_call", output_to_operand_aliasing={{0}: (6, {}), {1}: (7, {})} | custom-call | flops 1 | bytes 1 | tf_op jit(solution)/shard_map/pallas_call | solution.py:42
  130.5 6.3 %shard_map.58 = (bf16[4096,1024]{1,0:T(8,128)(2,1)}, bf16[4096,1024]{1,0:T(8,128)(2,1)}) custom-call(s32[1]{0:T(128)} %bitcast.6.place, f32[128,4096]{1,0:T(8,128)} %collective-permute-done.3.refs_0_.refs_1_, f32[128,4096]{1,0:T(8,128)} %collective-permute-done.3.refs_0_.refs_1_, ...), custom_call_target="tpu_custom_call", output_to_operand_aliasing={{0}: (6, {}), {1}: (7, {})} | custom-call | flops 1 | bytes 1 | tf_op jit(solution)/shard_map/pallas_call | solution.py:42
  136.8 6.3 %shard_map.59 = (bf16[4096,1024]{1,0:T(8,128)(2,1)}, bf16[4096,1024]{1,0:T(8,128)(2,1)}) custom-call(s32[1]{0:T(128)} %bitcast.2.place, f32[64,4096]{1,0:T(8,128)} %collective-permute-done.9.refs_0_, f32[64,4096]{1,0:T(8,128)} %collective-permute-done.10.refs_1_, ...), custom_call_target="tpu_custom_call", output_to_operand_aliasing={{0}: (6, {}), {1}: (7, {})} | custom-call | flops 1 | bytes 1 | tf_op jit(solution)/shard_map/pallas_call | solution.py:42
  143.1 21.7 %all-to-all-done = f32[8,128,1024]{2,1,0:T(8,128)} async-done(((f32[8,128,1024]{2,1,0:T(8,128)}), f32[8,128,1024]{2,1,0:T(8,128)}, u32[]{:S(2)}, u32[]{:S(2)}) %all-to-all-start) | async-done | bytes 4194336 | tf_op jit(solution)/shard_map/all_to_all | solution.py:202
  164.8 3.6 %all-to-all-start.2 = ((f32[8,128,512]{2,1,0:T(8,128)}), f32[8,128,512]{2,1,0:T(8,128)S(1)}, u32[]{:S(2)}, u32[]{:S(2)}) async-start(f32[8,128,512]{2,1,0:T(8,128)} %all-gather.4.cloned.1.call-done), calls=%async_computation.2 | async-start | bytes 4194304 | tf_op jit(solution)/shard_map/all_to_all | solution.py:202
  168.4 33.4 %shard_map.60.refs_0_ = f32[4096,2048]{1,0:T(8,128)} custom-call(f32[4096,2048]{1,0:T(8,128)} %trailing.5, bf16[4096,1024]{1,0:T(8,128)(2,1)} %get-tuple-element.47.hi, bf16[4096,1024]{1,0:T(8,128)(2,1)} %get-tuple-element.48.lo, f32[1024,1024]{1,0:T(8,128)} %bitcast.11.right), custom_call_target="tpu_custom_call" | custom-call | flops 1 | bytes 1 | tf_op jit(solution)/shard_map/pallas_call | solution.py:117
  201.7 4.4 %all-to-all-start.1 = ((f32[8,128,512]{2,1,0:T(8,128)}), f32[8,128,512]{2,1,0:T(8,128)}, u32[]{:S(2)}, u32[]{:S(2)}) async-start(f32[8,128,512]{2,1,0:T(8,128)} %all-gather.8.cloned.1.call-done), calls=%async_computation.1 | async-start | bytes 4194304 | tf_op jit(solution)/shard_map/all_to_all | solution.py:202
  206.1 19.1 %shard_map.61.refs_0_ = f32[4096,2048]{1,0:T(8,128)} custom-call(f32[4096,2048]{1,0:T(8,128)} %trailing.5, bf16[4096,1024]{1,0:T(8,128)(2,1)} %get-tuple-element.47.hi, bf16[4096,1024]{1,0:T(8,128)(2,1)} %get-tuple-element.48.lo, f32[1024,512]{1,0:T(8,128)S(1)} %bitcast.24, f32[4096,2048]{1,0:T(8,128)} %shard_map.60.refs_0_), custom_call_target="tpu_custom_call", output_to_operand_aliasing={{}: (4, {})} | custom-call | flops 1 | bytes 1 | tf_op jit(solution)/shard_map/pallas_call | solution.py:117
  225.2 7.5 %all-to-all-done.1 = f32[8,128,512]{2,1,0:T(8,128)} async-done(((f32[8,128,512]{2,1,0:T(8,128)}), f32[8,128,512]{2,1,0:T(8,128)}, u32[]{:S(2)}, u32[]{:S(2)}) %all-to-all-start.1) | async-done | bytes 2097184 | tf_op jit(solution)/shard_map/all_to_all | solution.py:202
  232.8 20.2 %shard_map.62 = f32[4096,2048]{1,0:T(8,128)} custom-call(f32[4096,2048]{1,0:T(8,128)} %trailing.5, bf16[4096,1024]{1,0:T(8,128)(2,1)} %get-tuple-element.47.hi, bf16[4096,1024]{1,0:T(8,128)(2,1)} %get-tuple-element.48.lo, f32[1024,512]{1,0:T(8,128)} %bitcast.12.right, f32[4096,2048]{1,0:T(8,128)} %shard_map.61.refs_0_), custom_call_target="tpu_custom_call", output_to_operand_aliasing={{}: (4, {})} | custom-call | flops 1 | bytes 1 | tf_op jit(solution)/shard_map/pallas_call | solution.py:117
  (31 shorter events, 0.2 us)
Async XLA Ops:
  6.5 2.6 %copy-start = (f32[2,128,512]{2,1,0:T(8,128)S(1)}, f32[2,128,512]{2,1,0:T(8,128)}, u32[]{:S(2)}) copy-start(f32[2,128,512]{2,1,0:T(8,128)} %param.8) | copy-start | bytes 1572868
  6.5 14.3 %copy-start.2 = (f32[128,4096]{1,0:T(8,128)S(1)}, f32[128,4096]{1,0:T(8,128)}, u32[]{:S(2)}) copy-start(f32[128,4096]{1,0:T(8,128)} %refs_1_) | copy-start | bytes 6291460
  6.5 2.6 %copy-start.6 = (f32[2,64,512]{2,1,0:T(8,128)S(1)}, f32[2,64,512]{2,1,0:T(8,128)}, u32[]{:S(2)}) copy-start(f32[2,64,512]{2,1,0:T(8,128)} %param.7) | copy-start | bytes 786436
  6.5 104.5 %all-gather.6.cloned.1.call-start = ((), (), s32[]{:S(2)}) async-start(), calls=%async_computation.4 | async-start | bytes 5242880 | tf_op jit(solution)/shard_map/all_gather | solution.py:157
  9.1 134.0 %all-gather.4.cloned.1.call-start = ((), (), s32[]{:S(2)}) async-start(), calls=%async_computation.3 | async-start | bytes 2621440 | tf_op jit(solution)/shard_map/all_gather | solution.py:157
  10.1 5.3 %collective-permute-start = (f32[2,64,64]{2,1,0:T(8,128)S(1)}, f32[2,64,64]{2,1,0:T(8,128)S(1)}, u32[]{:S(2)}, u32[]{:S(2)}) collective-permute-start(f32[2,64,64]{2,1,0:T(8,128)S(1)} %fusion.1), channel_id=1, source_target_pairs={{0,8},{8,0},{16,24},{24,16},{1,9},{9,1},{17,25},{25,17},{2,10},{10... | collective-permute-start | bytes 98312 | tf_op jit(solution)/shard_map/ppermute | solution.py:144
  15.4 5.3 %collective-permute-start.1 = (f32[2,64,64]{2,1,0:T(8,128)S(1)}, f32[2,64,64]{2,1,0:T(8,128)S(1)}, u32[]{:S(2)}, u32[]{:S(2)}) collective-permute-start(f32[2,64,64]{2,1,0:T(8,128)S(1)} %add.7), channel_id=1, source_target_pairs={{0,16},{8,24},{16,0},{24,8},{1,17},{9,25},{17,1},{25,9},{2,18},{10... | collective-permute-start | bytes 98312 | tf_op jit(solution)/shard_map/ppermute | solution.py:144
  20.8 56.8 %collective-permute-start.8 = (f32[128,4096]{1,0:T(8,128)S(1)}, f32[128,4096]{1,0:T(8,128)S(1)}, u32[]{:S(2)}, u32[]{:S(2)}) collective-permute-start(f32[128,4096]{1,0:T(8,128)S(1)} %copy-done.2), channel_id=1, source_target_pairs={{0,1},{1,0},{2,3},{3,2},{4,5},{5,4},{6,7},{7,6},{8,9},{9,8},{10,11... | collective-permute-start | bytes 6291464 | tf_op jit(solution)/shard_map/ppermute | solution.py:141
  20.9 58.1 %collective-permute-start.3 = (f32[128,4096]{1,0:T(8,128)S(1)}, f32[128,4096]{1,0:T(8,128)}, u32[]{:S(2)}, u32[]{:S(2)}) collective-permute-start(f32[128,4096]{1,0:T(8,128)S(1)} %copy-done.2), channel_id=1, source_target_pairs={{0,4},{1,5},{2,6},{3,7},{4,0},{5,1},{6,2},{7,3},{8,12},{9,13},{10,... | collective-permute-start | bytes 6291464 | tf_op jit(solution)/shard_map/ppermute | solution.py:141
  22.8 56.1 %collective-permute-start.2 = (f32[128,4096]{1,0:T(8,128)S(1)}, f32[128,4096]{1,0:T(8,128)}, u32[]{:S(2)}, u32[]{:S(2)}) collective-permute-start(f32[128,4096]{1,0:T(8,128)S(1)} %copy-done.2), channel_id=1, source_target_pairs={{0,2},{1,3},{2,0},{3,1},{4,6},{5,7},{6,4},{7,5},{8,10},{9,11},{10,... | collective-permute-start | bytes 6291464 | tf_op jit(solution)/shard_map/ppermute | solution.py:141
  24.3 47.4 %collective-permute-start.6 = (f32[2,64,64]{2,1,0:T(8,128)S(1)}, f32[2,64,64]{2,1,0:T(8,128)S(1)}, u32[]{:S(2)}, u32[]{:S(2)}) collective-permute-start(f32[2,64,64]{2,1,0:T(8,128)S(1)} %add.8.refs_0_), channel_id=1, source_target_pairs={{0,6},{1,7},{2,4},{3,5},{4,2},{5,3},{6,0},{7,1},{8,14},{9,15},{10,... | collective-permute-start | bytes 98312 | tf_op jit(solution)/shard_map/ppermute | solution.py:141
  24.4 49.0 %collective-permute-start.5 = (f32[2,64,64]{2,1,0:T(8,128)S(1)}, f32[2,64,64]{2,1,0:T(8,128)S(1)}, u32[]{:S(2)}, u32[]{:S(2)}) collective-permute-start(f32[2,64,64]{2,1,0:T(8,128)S(1)} %add.8.refs_0_), channel_id=1, source_target_pairs={{0,4},{1,5},{2,6},{3,7},{4,0},{5,1},{6,2},{7,3},{8,12},{9,13},{10,... | collective-permute-start | bytes 98312 | tf_op jit(solution)/shard_map/ppermute | solution.py:141
  71.7 4.3 %collective-permute-start.4 = (f32[2,64,64]{2,1,0:T(8,128)S(1)}, f32[2,64,64]{2,1,0:T(8,128)S(1)}, u32[]{:S(2)}, u32[]{:S(2)}) collective-permute-start(f32[2,64,64]{2,1,0:T(8,128)S(1)} %add.8.refs_0_), channel_id=1, source_target_pairs={{0,2},{1,3},{2,0},{3,1},{4,6},{5,7},{6,4},{7,5},{8,10},{9,11},{10,... | collective-permute-start | bytes 98312 | tf_op jit(solution)/shard_map/ppermute | solution.py:141
  76.0 1.6 collective-permute-start.7
  77.6 1.3 copy-start.3
  78.9 32.1 %collective-permute-start.11 = (f32[128,4096]{1,0:T(8,128)}, f32[128,4096]{1,0:T(8,128)}, u32[]{:S(2)}, u32[]{:S(2)}) collective-permute-start(f32[128,4096]{1,0:T(8,128)} %collective-permute-done.2.refs_0_.refs_1_), channel_id=1, source_target_pairs={{0,1},{1,0},{2,3},{3,2},{4,5},{5,4},{6,7},{7,6},{8,9},{9,8},{10,11... | collective-permute-start | bytes 6291464 | tf_op jit(solution)/shard_map/ppermute | solution.py:141
  79.1 32.0 %collective-permute-start.12 = (f32[128,4096]{1,0:T(8,128)}, f32[128,4096]{1,0:T(8,128)}, u32[]{:S(2)}, u32[]{:S(2)}) collective-permute-start(f32[128,4096]{1,0:T(8,128)} %collective-permute-done.3.refs_0_.refs_1_), channel_id=1, source_target_pairs={{0,1},{1,0},{2,3},{3,2},{4,5},{5,4},{6,7},{7,6},{8,9},{9,8},{10,11... | collective-permute-start | bytes 6291464 | tf_op jit(solution)/shard_map/ppermute | solution.py:141
  84.1 25.5 %collective-permute-start.10 = (f32[64,4096]{1,0:T(8,128)}, f32[64,4096]{1,0:T(8,128)}, u32[]{:S(2)}, u32[]{:S(2)}) collective-permute-start(f32[64,4096]{1,0:T(8,128)} %slice.27), channel_id=1, source_target_pairs={{0,2},{1,3},{2,0},{3,1},{4,6},{5,7},{6,4},{7,5},{8,10},{9,11},{10,... | collective-permute-start | bytes 3145736 | tf_op jit(solution)/shard_map/ppermute | solution.py:141
  85.8 25.2 %collective-permute-start.9 = (f32[64,4096]{1,0:T(8,128)}, f32[64,4096]{1,0:T(8,128)}, u32[]{:S(2)}, u32[]{:S(2)}) collective-permute-start(f32[64,4096]{1,0:T(8,128)} %slice.26), channel_id=1, source_target_pairs={{0,4},{1,5},{2,6},{3,7},{4,0},{5,1},{6,2},{7,3},{8,12},{9,13},{10,... | collective-permute-start | bytes 3145736 | tf_op jit(solution)/shard_map/ppermute | solution.py:141
  88.3 28.9 %copy-start.5 = (s32[16]{0:T(128)S(1)}, s32[16]{0:T(128)}, u32[]{:S(2)}) copy-start(s32[16]{0:T(128)} %slots.1) | copy-start | bytes 196
  111.1 53.7 %all-to-all-start = ((f32[8,128,1024]{2,1,0:T(8,128)}), f32[8,128,1024]{2,1,0:T(8,128)}, u32[]{:S(2)}, u32[]{:S(2)}) async-start(f32[8,128,1024]{2,1,0:T(8,128)} %all-gather.6.cloned.1.call-done), calls=%async_computation | async-start | bytes 8388608 | tf_op jit(solution)/shard_map/all_to_all | solution.py:202
  115.6 86.1 %all-gather.8.cloned.1.call-start = ((), (), s32[]{:S(2)}) async-start(), calls=%async_computation.5 | async-start | bytes 2621440 | tf_op jit(solution)/shard_map/all_gather | solution.py:157
  116.6 20.2 %collective-permute-start.13 = (f32[64,4096]{1,0:T(8,128)}, f32[64,4096]{1,0:T(8,128)}, u32[]{:S(2)}, u32[]{:S(2)}) collective-permute-start(f32[64,4096]{1,0:T(8,128)} %collective-permute-done.9.refs_0_), channel_id=1, source_target_pairs={{0,1},{1,0},{2,3},{3,2},{4,5},{5,4},{6,7},{7,6},{8,9},{9,8},{10,11... | collective-permute-start | bytes 3145736 | tf_op jit(solution)/shard_map/ppermute | solution.py:141
  117.0 19.8 %collective-permute-start.14 = (f32[64,4096]{1,0:T(8,128)}, f32[64,4096]{1,0:T(8,128)}, u32[]{:S(2)}, u32[]{:S(2)}) collective-permute-start(f32[64,4096]{1,0:T(8,128)} %collective-permute-done.10.refs_1_), channel_id=1, source_target_pairs={{0,1},{1,0},{2,3},{3,2},{4,5},{5,4},{6,7},{7,6},{8,9},{9,8},{10,11... | collective-permute-start | bytes 3145736 | tf_op jit(solution)/shard_map/ppermute | solution.py:141
  117.9 1.6 copy-start.4
  164.8 37.0 %all-to-all-start.2 = ((f32[8,128,512]{2,1,0:T(8,128)}), f32[8,128,512]{2,1,0:T(8,128)S(1)}, u32[]{:S(2)}, u32[]{:S(2)}) async-start(f32[8,128,512]{2,1,0:T(8,128)} %all-gather.4.cloned.1.call-done), calls=%async_computation.2 | async-start | bytes 4194304 | tf_op jit(solution)/shard_map/all_to_all | solution.py:202
  201.7 31.0 %all-to-all-start.1 = ((f32[8,128,512]{2,1,0:T(8,128)}), f32[8,128,512]{2,1,0:T(8,128)}, u32[]{:S(2)}, u32[]{:S(2)}) async-start(f32[8,128,512]{2,1,0:T(8,128)} %all-gather.8.cloned.1.call-done), calls=%async_computation.1 | async-start | bytes 4194304 | tf_op jit(solution)/shard_map/all_to_all | solution.py:202
  232.8 20.2 %copy-start.1 = (f32[2,128,512]{2,1,0:T(8,128)S(1)}, f32[2,128,512]{2,1,0:T(8,128)}, u32[]{:S(2)}) copy-start(f32[2,128,512]{2,1,0:T(8,128)} %param.8) | copy-start | bytes 1572868
Sparse Core Ops, SparseCore 0:
  9.2 83.4 all-gather.5
  94.3 44.4 all-gather.3
  140.4 44.6 all-gather.7

commit v2 on v1

--- a/solution.py
+++ b/solution.py
@@ -7,7 +7,8 @@
 from jax.experimental.pallas import tpu as pltpu
 from jax.sharding import PartitionSpec as P
 
-CHUNKS = ((0, 4), (4, 2), (6, 2))
+GATHERS = ((0, 4), (4, 2), (6, 2))
+CHUNKS = ((0, 0, 2), (0, 2, 2), (1, 4, 2), (2, 6, 2))
 HIGHEST = lax.Precision.HIGHEST
 SCALE_VMEM = 48 * 1024 * 1024
 UPDATE_VMEM = 48 * 1024 * 1024
@@ -110,7 +111,7 @@
 def update_chunk(start, trailing, left, right, previous):
     height = trailing.shape[0]
     depth, wide = right.shape
-    tile = min(height, 512)
+    tile = min(height, 1024)
     here = pl.BlockSpec((tile, wide), lambda i: (i, start // wide))
     side = pl.BlockSpec((tile, depth), lambda i: (i, 0))
     held = [] if previous is None else [previous]
@@ -154,7 +155,13 @@
 
     after = lax.optimization_barrier
 
-    everywhere = [lax.all_gather(column_chunk(*c), "row", axis=0, tiled=True) for c in CHUNKS]
+    everywhere = [lax.all_gather(column_chunk(*g), "row", axis=0, tiled=True) for g in GATHERS]
+    cut = rows // 2
+    own = [panel_factors[:cut], panel_factors[cut:]]
+    gathered = [[own, None]] + [[None, None] for _ in range(lines - 1)]
+    single = [1 << i for i in range(lines.bit_length() - 1)]
+    for s in single:
+        gathered[s][0] = [across(x, 2 * s) for x in own]
     solved = lax.dot_general(
         vectors_t, inverse_lower_factors, (((2,), (2,)), ((0,), (0,))), precision=HIGHEST
     )
@@ -163,43 +170,34 @@
     while bit < planes:
         cores = cores + along(cores, [(i, i ^ bit) for i in range(planes)])
         bit *= 2
-    bulk, cores = after((panel_factors, cores))
-    near = [cores] + [across(cores, 2 * s) for s in range(1, lines)]
-
-    cut = rows // 2
-    gathered = [[[bulk], None]] + [[None, None] for _ in range(lines - 1)]
-    single = [1 << i for i in range(lines.bit_length() - 1)]
-    for s in single:
-        gathered[s][0] = [across(bulk, 2 * s)]
-
-    far = across(jnp.concatenate(near), 1)
-    gathered[0][1] = [across(bulk, 1)]
-
-    arrived, far, gathered[0][1] = after(([gathered[s][0] for s in single], far, gathered[0][1]))
+
+    arrived, cores = after(([gathered[s][0] for s in single], cores))
     for s, x in zip(single, arrived):
         gathered[s][0] = x
+    near = [cores] + [across(cores, 2 * s) for s in range(1, lines)]
     several = sorted((s for s in range(1, lines) if s not in single), key=lambda s: bin(s).count("1"))
     for s in several:
         low, high = s & -s, 1 << (s.bit_length() - 1)
-        upper, lower = gathered[s ^ high][0], gathered[s ^ low][0]
         gathered[s][0] = [
-            across(upper[0][:cut], 2 * high),
-            across(lower[-1][-cut:], 2 * low),
+            across(gathered[s ^ high][0][0], 2 * high),
+            across(gathered[s ^ low][0][1], 2 * low),
         ]
-    for s in single:
-        gathered[s][1] = [across(x, 1) for x in gathered[s][0]]
-
-    arrived, swapped, everywhere[0] = after(
-        ([gathered[s][0] for s in several], [gathered[s][1] for s in single], everywhere[0])
-    )
+
+    arrived, near, everywhere[0] = after(([gathered[s][0] for s in several], near, everywhere[0]))
     for s, x in zip(several, arrived):
         gathered[s][0] = x
-        gathered[s][1] = [across(part, 1) for part in x]
-    for s, x in zip(single, swapped):
-        gathered[s][1] = x
+    far = across(jnp.concatenate(near), 1)
+    gathered[0] = [[panel_factors], [across(panel_factors, 1)]]
+    for s in range(1, lines):
+        gathered[s][1] = [across(x, 1) for x in gathered[s][0]]
 
     def exchange(number):
-        chunk = lax.all_to_all(everywhere[number], "col", split_axis=0, concat_axis=0, tiled=True)
+        source, first, count = CHUNKS[number]
+        sent = everywhere[source]
+        if GATHERS[source][1] != count:
+            at = (first - GATHERS[source][0]) * eighth
+            sent = sent[:, :, at : at + count * eighth]
+        chunk = lax.all_to_all(sent, "col", split_axis=0, concat_axis=0, tiled=True)
         return chunk.reshape(depth, -1)
 
     chunks = [exchange(0)]
@@ -214,12 +212,13 @@
         left = scale_into(place, parts, blocks, s, left, depth)
 
     updated = None
-    for number, (first, _) in enumerate(CHUNKS):
+    for number, (_, first, _) in enumerate(CHUNKS):
         if number + 1 < len(CHUNKS):
+            source = CHUNKS[number + 1][0]
             if updated is None:
-                everywhere[number + 1], left = after((everywhere[number + 1], left))
+                everywhere[source], left = after((everywhere[source], left))
             else:
-                everywhere[number + 1], updated = after((everywhere[number + 1], updated))
+                everywhere[source], updated = after((everywhere[source], updated))
             chunks.append(exchange(number + 1))
         updated = update_chunk(first * eighth, trailing, left, chunks[number], updated)
     return updated

time: 261 us -> 249 us (0.954)
  waiting for transfers between devices: 106 us -> 87.4 us
  Pallas kernels: 97 us -> 103 us
  starting transfers between devices: 30.4 us -> 35 us
  local copies, waits for them, and re-layouts: 9.09 us -> 6.38 us
    ppermute x13 -> x17, waiting for transfers between devices: 72.3 us -> 57.9 us  [across(): return lax.ppermute(x, 'col', [(i, i ^ bits) for i in range(columns)])]
    all_to_all x3 -> x4, waiting for transfers between devices: 29.2 us -> 17.7 us  [exchange(): chunk = lax.all_to_all(sent, 'col', split_axis=0, concat_axis=0, tiled=True)]
    ppermute x2, waiting for transfers between devices: 4.49 us -> 9.15 us  [along(): return lax.ppermute(x, 'row', moves)]
    pallas_call x3 -> x4, Pallas kernels: 72.6 us -> 76.8 us  [update_chunk(): pl.pallas_call(update_kernel, grid=(height // tile,), in_specs=[here, sid...]
    all_to_all x3 -> x4, starting transfers between devices: 12.5 us -> 16.5 us  [exchange(): chunk = lax.all_to_all(sent, 'col', split_axis=0, concat_axis=0, tiled=True)]
    unnamed x14 -> x12, local copies, waits for them, and re-layouts: 2.93 us -> 0.03 us
    all_gather x3, waiting for transfers between devices: 0.02 us -> 2.67 us  [body(): lax.all_gather(column_chunk(*g), 'row', axis=0, tiled=True)]
    ppermute x13 -> x17, starting transfers between devices: 11.6 us -> 13.2 us  [across(): return lax.ppermute(x, 'col', [(i, i ^ bits) for i in range(columns)])]
  transfers between devices with their start and end apart: 21 -> 26, of which waited for: 9 -> 13; matrix products, arithmetic and copies ran while one was open for 3% -> 3% of each run, Pallas kernels for 30% -> 34%
where the time goes in v2:
time: 249 us; the launch traced here: 248 us
  Pallas kernels  103 us (41%)
  waiting for transfers between devices  87.4 us (35%)
  starting transfers between devices  35 us (14%)
  between operations  13.3 us (5%)
  local copies, waits for them, and re-layouts  6.38 us (3%)
  other arithmetic  2.82 us (1%)
    pallas_call x4, Pallas kernels, update_chunk(): pl.pallas_call(update_kernel, grid=(height // tile,), in_specs=[here, sid...  76.8 us
    ppermute x17, waiting for transfers between devices, across(): return lax.ppermute(x, 'col', [(i, i ^ bits) for i in range(columns)])  57.9 us
    pallas_call x4, Pallas kernels, scale_into(): pl.pallas_call(scale_kernel, grid_spec=pltpu.PrefetchScalarGridSpec(num_s...  25 us
    all_to_all x4, waiting for transfers between devices, exchange(): chunk = lax.all_to_all(sent, 'col', split_axis=0, concat_axis=0, tiled=True)  17.7 us
    all_to_all x4, starting transfers between devices, exchange(): chunk = lax.all_to_all(sent, 'col', split_axis=0, concat_axis=0, tiled=True)  16.5 us
    ppermute x17, starting transfers between devices, across(): return lax.ppermute(x, 'col', [(i, i ^ bits) for i in range(columns)])  13.2 us
    ppermute x2, waiting for transfers between devices, along(): return lax.ppermute(x, 'row', moves)  9.15 us
    ppermute x2, starting transfers between devices, along(): return lax.ppermute(x, 'row', moves)  5.19 us
  transfers between devices with their start and end apart: 26, of which 13 were waited for; matrix products, arithmetic and copies ran while one was open for 3% of the time, Pallas kernels for 34%

profile of v2, /device:TPU:0, one launch (start us, length us, event | category | flops | bytes accessed | tf_op | source)
XLA Modules:
  0.0 248.4 jit_solution(8708033504236184258)
XLA Ops:
  6.5 1.4 slice_bitcast_fusion.1
  8.0 1.1 pad_maximum_fusion
  9.2 0.1 fusion
  9.3 3.0 %collective-permute-start = (f32[64,4096]{1,0:T(8,128)S(1)}, f32[64,4096]{1,0:T(8,128)}, u32[]{:S(2)}, u32[]{:S(2)}) collective-permute-start(f32[64,4096]{1,0:T(8,128)S(1)} %get-tuple-element.66), channel_id=1, source_target_pairs={{0,2},{1,3},{2,0},{3,1},{4,6},{5,7},{6,4},{7,5},{8,10},{9,11},{10,... | collective-permute-start | bytes 3145736 | tf_op jit(solution)/shard_map/ppermute | solution.py:142
  12.4 2.0 collective-permute-start.2
  14.4 0.7 fusion.1
  15.1 0.2 fusion.2
  15.3 2.1 collective-permute-start.4
  17.4 2.2 collective-permute-done.4
  19.7 3.1 %collective-permute-start.5 = (f32[2,64,64]{2,1,0:T(8,128)S(1)}, f32[2,64,64]{2,1,0:T(8,128)S(1)}, u32[]{:S(2)}, u32[]{:S(2)}) collective-permute-start(f32[2,64,64]{2,1,0:T(8,128)S(1)} %add.7), channel_id=1, source_target_pairs={{0,16},{8,24},{16,0},{24,8},{1,17},{9,25},{17,1},{25,9},{2,18},{10... | collective-permute-start | bytes 98312 | tf_op jit(solution)/shard_map/ppermute | solution.py:145
  22.8 6.9 %collective-permute-done.5 = f32[2,64,64]{2,1,0:T(8,128)S(1)} collective-permute-done((f32[2,64,64]{2,1,0:T(8,128)S(1)}, f32[2,64,64]{2,1,0:T(8,128)S(1)}, u32[]{:S(2)}, u32[]{:S(2)}) %collective-permute-start.5) | collective-permute-done | bytes 32800 | tf_op jit(solution)/shard_map/ppermute | solution.py:145
  29.7 6.7 %collective-permute-done.refs_0_ = f32[64,4096]{1,0:T(8,128)} collective-permute-done((f32[64,4096]{1,0:T(8,128)S(1)}, f32[64,4096]{1,0:T(8,128)}, u32[]{:S(2)}, u32[]{:S(2)}) %collective-permute-start) | collective-permute-done | bytes 1048608 | tf_op jit(solution)/shard_map/ppermute | solution.py:142
  36.4 21.6 %collective-permute-done.1.refs_1_ = f32[64,4096]{1,0:T(8,128)} collective-permute-done((f32[64,4096]{1,0:T(8,128)S(1)}, f32[64,4096]{1,0:T(8,128)}, u32[]{:S(2)}, u32[]{:S(2)}) %collective-permute-start.1) | collective-permute-done | bytes 1048608 | tf_op jit(solution)/shard_map/ppermute | solution.py:142
  58.1 1.5 collective-permute-done.3.refs_1_
  59.6 1.7 collective-permute-start.6
  61.3 1.5 collective-permute-start.7
  62.9 0.8 pad_maximum_fusion.2
  63.8 0.4 collective-permute-start.10
  64.2 21.9 %collective-permute-done.10.refs_3_ = f32[2,64,64]{2,1,0:T(8,128)S(1)} collective-permute-done((f32[2,64,64]{2,1,0:T(8,128)S(1)}, f32[2,64,64]{2,1,0:T(8,128)S(1)}, u32[]{:S(2)}, u32[]{:S(2)}) %collective-permute-start.10) | collective-permute-done | bytes 32800 | tf_op jit(solution)/shard_map/ppermute | solution.py:142
  86.1 1.4 collective-permute-start.8
  87.5 2.9 %collective-permute-done.8.refs_1_ = f32[2,64,64]{2,1,0:T(8,128)S(1)} collective-permute-done((f32[2,64,64]{2,1,0:T(8,128)S(1)}, f32[2,64,64]{2,1,0:T(8,128)S(1)}, u32[]{:S(2)}, u32[]{:S(2)}) %collective-permute-start.8) | collective-permute-done | bytes 32800 | tf_op jit(solution)/shard_map/ppermute | solution.py:142
  90.4 1.4 collective-permute-start.9
  91.8 2.9 %collective-permute-done.9.refs_2_ = f32[2,64,64]{2,1,0:T(8,128)S(1)} collective-permute-done((f32[2,64,64]{2,1,0:T(8,128)S(1)}, f32[2,64,64]{2,1,0:T(8,128)S(1)}, u32[]{:S(2)}, u32[]{:S(2)}) %collective-permute-start.9) | collective-permute-done | bytes 32800 | tf_op jit(solution)/shard_map/ppermute | solution.py:142
  94.7 3.1 %slice.39 = f32[8,128,512]{2,1,0:T(8,128)} slice(f32[8,128,1024]{2,1,0:T(8,128)} %all-gather.4.cloned.1.call-done), slice={[0:8], [0:128], [0:512]} | slice | bytes 4194304 | tf_op jit(solution)/shard_map/slice | solution.py:199
  97.8 4.4 %all-to-all-start.1 = ((f32[8,128,512]{2,1,0:T(8,128)}), f32[8,128,512]{2,1,0:T(8,128)}, u32[]{:S(2)}, u32[]{:S(2)}) async-start(f32[8,128,512]{2,1,0:T(8,128)} %slice.39), calls=%async_computation.1 | async-start | bytes 4194304 | tf_op jit(solution)/shard_map/all_to_all | solution.py:200
  102.2 0.4 collective-permute-start.13
  102.7 0.4 collective-permute-start.15
  103.3 0.4 collective-permute-start.11
  103.6 0.3 collective-permute-done.13.refs_4_
  103.9 0.2 collective-permute-start.12
  104.1 0.8 shard_map.55.refs_4_
  104.9 6.0 %shard_map.56 = (bf16[4096,1024]{1,0:T(8,128)(2,1)}, bf16[4096,1024]{1,0:T(8,128)(2,1)}) custom-call(s32[1]{0:T(128)} %bitcast.6.place, f32[128,4096]{1,0:T(8,128)S(1)} %copy-done.2, f32[128,4096]{1,0:T(8,128)S(1)} %copy-done.2, f32[128,4096]{1,0:T(8,128)} %collective-permute-done.18.refs_2_.refs_3_, f32[128,4096]{1,0:T(8,128)} %collective-permute-done.18.refs_2_.refs_3_, ...), custom_call_target="tpu_custom_call" | custom-call | flops 1 | bytes 1 | tf_op jit(solution)/shard_map/pallas_call | solution.py:43
  111.0 6.3 %shard_map.57 = (bf16[4096,1024]{1,0:T(8,128)(2,1)}, bf16[4096,1024]{1,0:T(8,128)(2,1)}) custom-call(s32[1]{0:T(128)} %bitcast.5.place, f32[64,4096]{1,0:T(8,128)} %collective-permute-done.refs_0_, f32[64,4096]{1,0:T(8,128)} %collective-permute-done.1.refs_1_, ...), custom_call_target="tpu_custom_call", output_to_operand_aliasing={{0}: (6, {}), {1}: (7, {})} | custom-call | flops 1 | bytes 1 | tf_op jit(solution)/shard_map/pallas_call | solution.py:43
  117.2 6.3 %shard_map.58 = (bf16[4096,1024]{1,0:T(8,128)(2,1)}, bf16[4096,1024]{1,0:T(8,128)(2,1)}) custom-call(s32[1]{0:T(128)} %bitcast.4.place, f32[64,4096]{1,0:T(8,128)} %collective-permute-done.2.refs_0_, f32[64,4096]{1,0:T(8,128)} %collective-permute-done.3.refs_1_, ...), custom_call_target="tpu_custom_call", output_to_operand_aliasing={{0}: (6, {}), {1}: (7, {})} | custom-call | flops 1 | bytes 1 | tf_op jit(solution)/shard_map/pallas_call | solution.py:43
  123.5 6.4 %shard_map.59 = (bf16[4096,1024]{1,0:T(8,128)(2,1)}, bf16[4096,1024]{1,0:T(8,128)(2,1)}) custom-call(s32[1]{0:T(128)} %bitcast.2.place, f32[64,4096]{1,0:T(8,128)} %collective-permute-done.6.refs_0_, f32[64,4096]{1,0:T(8,128)} %collective-permute-done.7.refs_1_, ...), custom_call_target="tpu_custom_call", output_to_operand_aliasing={{0}: (6, {}), {1}: (7, {})} | custom-call | flops 1 | bytes 1 | tf_op jit(solution)/shard_map/pallas_call | solution.py:43
  130.0 1.6 slice.36
  131.6 4.0 %all-to-all-start = ((f32[8,128,512]{2,1,0:T(8,128)}), f32[8,128,512]{2,1,0:T(8,128)S(1)}, u32[]{:S(2)}, u32[]{:S(2)}) async-start(f32[8,128,512]{2,1,0:T(8,128)} %slice.36), calls=%async_computation | async-start | bytes 4194304 | tf_op jit(solution)/shard_map/all_to_all | solution.py:200
  135.6 0.9 pad_maximum_fusion.1
  136.5 20.4 %shard_map.60.refs_0_ = f32[4096,2048]{1,0:T(8,128)} custom-call(f32[4096,2048]{1,0:T(8,128)} %trailing.7, bf16[4096,1024]{1,0:T(8,128)(2,1)} %get-tuple-element.52.hi, bf16[4096,1024]{1,0:T(8,128)(2,1)} %get-tuple-element.53.lo, f32[1024,512]{1,0:T(8,128)} %bitcast.12.right), custom_call_target="tpu_custom_call" | custom-call | flops 1 | bytes 1 | tf_op jit(solution)/shard_map/pallas_call | solution.py:118
  156.9 5.3 %all-to-all-done = f32[8,128,512]{2,1,0:T(8,128)S(1)} async-done(((f32[8,128,512]{2,1,0:T(8,128)}), f32[8,128,512]{2,1,0:T(8,128)S(1)}, u32[]{:S(2)}, u32[]{:S(2)}) %all-to-all-start) | async-done | bytes 2097184 | tf_op jit(solution)/shard_map/all_to_all | solution.py:200
  162.2 4.4 %all-to-all-start.3 = ((f32[8,128,512]{2,1,0:T(8,128)}), f32[8,128,512]{2,1,0:T(8,128)}, u32[]{:S(2)}, u32[]{:S(2)}) async-start(f32[8,128,512]{2,1,0:T(8,128)} %all-gather.8.cloned.1.call-done), calls=%async_computation.3 | async-start | bytes 4194304 | tf_op jit(solution)/shard_map/all_to_all | solution.py:200
  166.6 18.4 %shard_map.61.refs_0_ = f32[4096,2048]{1,0:T(8,128)} custom-call(f32[4096,2048]{1,0:T(8,128)} %trailing.7, bf16[4096,1024]{1,0:T(8,128)(2,1)} %get-tuple-element.52.hi, bf16[4096,1024]{1,0:T(8,128)(2,1)} %get-tuple-element.53.lo, f32[1024,512]{1,0:T(8,128)S(1)} %bitcast.25, f32[4096,2048]{1,0:T(8,128)} %shard_map.60.refs_0_), custom_call_target="tpu_custom_call", output_to_operand_aliasing={{}: (4, {})} | custom-call | flops 1 | bytes 1 | tf_op jit(solution)/shard_map/pallas_call | solution.py:118
  185.0 2.7 %all-gather.6.cloned.1.call-done = f32[8,128,512]{2,1,0:T(8,128)} async-done(((f32[2,128,512]{2,1,0:T(8,128)}), f32[8,128,512]{2,1,0:T(8,128)}) %all-gather.6.cloned.1.call-update) | async-done | bytes 2097168 | tf_op jit(solution)/shard_map/all_gather | solution.py:158
  187.6 5.6 %all-to-all-done.3 = f32[8,128,512]{2,1,0:T(8,128)} async-done(((f32[8,128,512]{2,1,0:T(8,128)}), f32[8,128,512]{2,1,0:T(8,128)}, u32[]{:S(2)}, u32[]{:S(2)}) %all-to-all-start.3) | async-done | bytes 2097184 | tf_op jit(solution)/shard_map/all_to_all | solution.py:200
  193.2 3.8 %all-to-all-start.2 = ((f32[8,128,512]{2,1,0:T(8,128)}), f32[8,128,512]{2,1,0:T(8,128)S(1)}, u32[]{:S(2)}, u32[]{:S(2)}) async-start(f32[8,128,512]{2,1,0:T(8,128)} %all-gather.6.cloned.1.call-done), calls=%async_computation.2 | async-start | bytes 4194304 | tf_op jit(solution)/shard_map/all_to_all | solution.py:200
  197.0 19.6 %shard_map.62.refs_0_ = f32[4096,2048]{1,0:T(8,128)} custom-call(f32[4096,2048]{1,0:T(8,128)} %trailing.7, bf16[4096,1024]{1,0:T(8,128)(2,1)} %get-tuple-element.52.hi, bf16[4096,1024]{1,0:T(8,128)(2,1)} %get-tuple-element.53.lo, f32[1024,512]{1,0:T(8,128)} %bitcast.14.right, f32[4096,2048]{1,0:T(8,128)} %shard_map.61.refs_0_), custom_call_target="tpu_custom_call", output_to_operand_aliasing={{}: (4, {})} | custom-call | flops 1 | bytes 1 | tf_op jit(solution)/shard_map/pallas_call | solution.py:118
  216.6 6.8 %all-to-all-done.2 = f32[8,128,512]{2,1,0:T(8,128)S(1)} async-done(((f32[8,128,512]{2,1,0:T(8,128)}), f32[8,128,512]{2,1,0:T(8,128)S(1)}, u32[]{:S(2)}, u32[]{:S(2)}) %all-to-all-start.2) | async-done | bytes 2097184 | tf_op jit(solution)/shard_map/all_to_all | solution.py:200
  223.4 18.4 %shard_map.63 = f32[4096,2048]{1,0:T(8,128)} custom-call(f32[4096,2048]{1,0:T(8,128)} %trailing.7, bf16[4096,1024]{1,0:T(8,128)(2,1)} %get-tuple-element.52.hi, bf16[4096,1024]{1,0:T(8,128)(2,1)} %get-tuple-element.53.lo, f32[1024,512]{1,0:T(8,128)S(1)} %bitcast.26, f32[4096,2048]{1,0:T(8,128)} %shard_map.62.refs_0_), custom_call_target="tpu_custom_call", output_to_operand_aliasing={{}: (4, {})} | custom-call | flops 1 | bytes 1 | tf_op jit(solution)/shard_map/pallas_call | solution.py:118
  (41 shorter events, 0.8 us)
Async XLA Ops:
  6.5 7.9 %copy-start = (f32[2,128,512]{2,1,0:T(8,128)S(1)}, f32[2,128,512]{2,1,0:T(8,128)}, u32[]{:S(2)}) copy-start(f32[2,128,512]{2,1,0:T(8,128)} %param.8) | copy-start | bytes 1572868
  6.5 2.6 %copy-start.2 = (f32[128,4096]{1,0:T(8,128)S(1)}, f32[128,4096]{1,0:T(8,128)}, u32[]{:S(2)}) copy-start(f32[128,4096]{1,0:T(8,128)} %refs_1_.1) | copy-start | bytes 6291460
  6.5 88.1 %all-gather.4.cloned.1.call-start = ((), (), s32[]{:S(2)}) async-start(), calls=%async_computation.4 | async-start | bytes 5242880 | tf_op jit(solution)/shard_map/all_gather | solution.py:158
  8.0 6.4 %copy-start.5 = (f32[2,64,512]{2,1,0:T(8,128)S(1)}, f32[2,64,512]{2,1,0:T(8,128)}, u32[]{:S(2)}) copy-start(f32[2,64,512]{2,1,0:T(8,128)} %param.7) | copy-start | bytes 786436
  9.1 147.8 %all-gather.8.cloned.1.call-start = ((), (), s32[]{:S(2)}) async-start(), calls=%async_computation.6 | async-start | bytes 2621440 | tf_op jit(solution)/shard_map/all_gather | solution.py:158
  9.3 27.1 %collective-permute-start = (f32[64,4096]{1,0:T(8,128)S(1)}, f32[64,4096]{1,0:T(8,128)}, u32[]{:S(2)}, u32[]{:S(2)}) collective-permute-start(f32[64,4096]{1,0:T(8,128)S(1)} %get-tuple-element.66), channel_id=1, source_target_pairs={{0,2},{1,3},{2,0},{3,1},{4,6},{5,7},{6,4},{7,5},{8,10},{9,11},{10,... | collective-permute-start | bytes 3145736 | tf_op jit(solution)/shard_map/ppermute | solution.py:142
  12.3 45.7 %collective-permute-start.1 = (f32[64,4096]{1,0:T(8,128)S(1)}, f32[64,4096]{1,0:T(8,128)}, u32[]{:S(2)}, u32[]{:S(2)}) collective-permute-start(f32[64,4096]{1,0:T(8,128)S(1)} %get-tuple-element.65), channel_id=1, source_target_pairs={{0,2},{1,3},{2,0},{3,1},{4,6},{5,7},{6,4},{7,5},{8,10},{9,11},{10,... | collective-permute-start | bytes 3145736 | tf_op jit(solution)/shard_map/ppermute | solution.py:142
  12.4 45.7 %collective-permute-start.2 = (f32[64,4096]{1,0:T(8,128)S(1)}, f32[64,4096]{1,0:T(8,128)}, u32[]{:S(2)}, u32[]{:S(2)}) collective-permute-start(f32[64,4096]{1,0:T(8,128)S(1)} %get-tuple-element.66), channel_id=1, source_target_pairs={{0,4},{1,5},{2,6},{3,7},{4,0},{5,1},{6,2},{7,3},{8,12},{9,13},{10,... | collective-permute-start | bytes 3145736 | tf_op jit(solution)/shard_map/ppermute | solution.py:142
  14.4 45.2 %collective-permute-start.3 = (f32[64,4096]{1,0:T(8,128)S(1)}, f32[64,4096]{1,0:T(8,128)}, u32[]{:S(2)}, u32[]{:S(2)}) collective-permute-start(f32[64,4096]{1,0:T(8,128)S(1)} %get-tuple-element.65), channel_id=1, source_target_pairs={{0,4},{1,5},{2,6},{3,7},{4,0},{5,1},{6,2},{7,3},{8,12},{9,13},{10,... | collective-permute-start | bytes 3145736 | tf_op jit(solution)/shard_map/ppermute | solution.py:142
  15.3 4.3 %collective-permute-start.4 = (f32[2,64,64]{2,1,0:T(8,128)S(1)}, f32[2,64,64]{2,1,0:T(8,128)S(1)}, u32[]{:S(2)}, u32[]{:S(2)}) collective-permute-start(f32[2,64,64]{2,1,0:T(8,128)S(1)} %fusion.2), channel_id=1, source_target_pairs={{0,8},{8,0},{16,24},{24,16},{1,9},{9,1},{17,25},{25,17},{2,10},{10... | collective-permute-start | bytes 98312 | tf_op jit(solution)/shard_map/ppermute | solution.py:145
  19.7 10.0 %collective-permute-start.5 = (f32[2,64,64]{2,1,0:T(8,128)S(1)}, f32[2,64,64]{2,1,0:T(8,128)S(1)}, u32[]{:S(2)}, u32[]{:S(2)}) collective-permute-start(f32[2,64,64]{2,1,0:T(8,128)S(1)} %add.7), channel_id=1, source_target_pairs={{0,16},{8,24},{16,0},{24,8},{1,17},{9,25},{17,1},{25,9},{2,18},{10... | collective-permute-start | bytes 98312 | tf_op jit(solution)/shard_map/ppermute | solution.py:145
  29.7 73.4 %collective-permute-start.18 = (f32[128,4096]{1,0:T(8,128)S(1)}, f32[128,4096]{1,0:T(8,128)}, u32[]{:S(2)}, u32[]{:S(2)}) collective-permute-start(f32[128,4096]{1,0:T(8,128)S(1)} %copy-done.2), channel_id=1, source_target_pairs={{0,1},{1,0},{2,3},{3,2},{4,5},{5,4},{6,7},{7,6},{8,9},{9,8},{10,11... | collective-permute-start | bytes 6291464 | tf_op jit(solution)/shard_map/ppermute | solution.py:142
  59.6 35.0 %collective-permute-start.6 = (f32[64,4096]{1,0:T(8,128)}, f32[64,4096]{1,0:T(8,128)}, u32[]{:S(2)}, u32[]{:S(2)}) collective-permute-start(f32[64,4096]{1,0:T(8,128)} %collective-permute-done.refs_0_), channel_id=1, source_target_pairs={{0,4},{1,5},{2,6},{3,7},{4,0},{5,1},{6,2},{7,3},{8,12},{9,13},{10,... | collective-permute-start | bytes 3145736 | tf_op jit(solution)/shard_map/ppermute | solution.py:142
  61.3 33.4 %collective-permute-start.7 = (f32[64,4096]{1,0:T(8,128)}, f32[64,4096]{1,0:T(8,128)}, u32[]{:S(2)}, u32[]{:S(2)}) collective-permute-start(f32[64,4096]{1,0:T(8,128)} %collective-permute-done.3.refs_1_), channel_id=1, source_target_pairs={{0,2},{1,3},{2,0},{3,1},{4,6},{5,7},{6,4},{7,5},{8,10},{9,11},{10,... | collective-permute-start | bytes 3145736 | tf_op jit(solution)/shard_map/ppermute | solution.py:142
  63.8 40.4 %copy-start.3 = (s32[16]{0:T(128)S(1)}, s32[16]{0:T(128)}, u32[]{:S(2)}) copy-start(s32[16]{0:T(128)} %slots.1) | copy-start | bytes 196
  63.8 39.5 %collective-permute-start.16 = (f32[64,4096]{1,0:T(8,128)}, f32[64,4096]{1,0:T(8,128)}, u32[]{:S(2)}, u32[]{:S(2)}) collective-permute-start(f32[64,4096]{1,0:T(8,128)} %collective-permute-done.refs_0_), channel_id=1, source_target_pairs={{0,1},{1,0},{2,3},{3,2},{4,5},{5,4},{6,7},{7,6},{8,9},{9,8},{10,11... | collective-permute-start | bytes 3145736 | tf_op jit(solution)/shard_map/ppermute | solution.py:142
  63.8 22.3 %collective-permute-start.10 = (f32[2,64,64]{2,1,0:T(8,128)S(1)}, f32[2,64,64]{2,1,0:T(8,128)S(1)}, u32[]{:S(2)}, u32[]{:S(2)}) collective-permute-start(f32[2,64,64]{2,1,0:T(8,128)S(1)} %add.8.refs_0_), channel_id=1, source_target_pairs={{0,6},{1,7},{2,4},{3,5},{4,2},{5,3},{6,0},{7,1},{8,14},{9,15},{10,... | collective-permute-start | bytes 98312 | tf_op jit(solution)/shard_map/ppermute | solution.py:142
  86.1 4.3 %collective-permute-start.8 = (f32[2,64,64]{2,1,0:T(8,128)S(1)}, f32[2,64,64]{2,1,0:T(8,128)S(1)}, u32[]{:S(2)}, u32[]{:S(2)}) collective-permute-start(f32[2,64,64]{2,1,0:T(8,128)S(1)} %add.8.refs_0_), channel_id=1, source_target_pairs={{0,2},{1,3},{2,0},{3,1},{4,6},{5,7},{6,4},{7,5},{8,10},{9,11},{10,... | collective-permute-start | bytes 98312 | tf_op jit(solution)/shard_map/ppermute | solution.py:142
  90.4 4.3 %collective-permute-start.9 = (f32[2,64,64]{2,1,0:T(8,128)S(1)}, f32[2,64,64]{2,1,0:T(8,128)S(1)}, u32[]{:S(2)}, u32[]{:S(2)}) collective-permute-start(f32[2,64,64]{2,1,0:T(8,128)S(1)} %add.8.refs_0_), channel_id=1, source_target_pairs={{0,4},{1,5},{2,6},{3,7},{4,0},{5,1},{6,2},{7,3},{8,12},{9,13},{10,... | collective-permute-start | bytes 98312 | tf_op jit(solution)/shard_map/ppermute | solution.py:142
  97.8 33.8 %all-to-all-start.1 = ((f32[8,128,512]{2,1,0:T(8,128)}), f32[8,128,512]{2,1,0:T(8,128)}, u32[]{:S(2)}, u32[]{:S(2)}) async-start(f32[8,128,512]{2,1,0:T(8,128)} %slice.39), calls=%async_computation.1 | async-start | bytes 4194304 | tf_op jit(solution)/shard_map/all_to_all | solution.py:200
  102.2 1.7 collective-permute-start.13
  102.6 8.4 %collective-permute-start.17 = (f32[64,4096]{1,0:T(8,128)}, f32[64,4096]{1,0:T(8,128)}, u32[]{:S(2)}, u32[]{:S(2)}) collective-permute-start(f32[64,4096]{1,0:T(8,128)} %collective-permute-done.1.refs_1_), channel_id=1, source_target_pairs={{0,1},{1,0},{2,3},{3,2},{4,5},{5,4},{6,7},{7,6},{8,9},{9,8},{10,11... | collective-permute-start | bytes 3145736 | tf_op jit(solution)/shard_map/ppermute | solution.py:142
  102.7 14.5 %collective-permute-start.15 = (f32[64,4096]{1,0:T(8,128)}, f32[64,4096]{1,0:T(8,128)}, u32[]{:S(2)}, u32[]{:S(2)}) collective-permute-start(f32[64,4096]{1,0:T(8,128)} %collective-permute-done.3.refs_1_), channel_id=1, source_target_pairs={{0,1},{1,0},{2,3},{3,2},{4,5},{5,4},{6,7},{7,6},{8,9},{9,8},{10,11... | collective-permute-start | bytes 3145736 | tf_op jit(solution)/shard_map/ppermute | solution.py:142
  103.1 14.1 %collective-permute-start.14 = (f32[64,4096]{1,0:T(8,128)}, f32[64,4096]{1,0:T(8,128)}, u32[]{:S(2)}, u32[]{:S(2)}) collective-permute-start(f32[64,4096]{1,0:T(8,128)} %collective-permute-done.2.refs_0_), channel_id=1, source_target_pairs={{0,1},{1,0},{2,3},{3,2},{4,5},{5,4},{6,7},{7,6},{8,9},{9,8},{10,11... | collective-permute-start | bytes 3145736 | tf_op jit(solution)/shard_map/ppermute | solution.py:142
  103.3 20.3 %collective-permute-start.11 = (f32[64,4096]{1,0:T(8,128)}, f32[64,4096]{1,0:T(8,128)}, u32[]{:S(2)}, u32[]{:S(2)}) collective-permute-start(f32[64,4096]{1,0:T(8,128)} %collective-permute-done.6.refs_0_), channel_id=1, source_target_pairs={{0,1},{1,0},{2,3},{3,2},{4,5},{5,4},{6,7},{7,6},{8,9},{9,8},{10,11... | collective-permute-start | bytes 3145736 | tf_op jit(solution)/shard_map/ppermute | solution.py:142
  103.9 19.6 %collective-permute-start.12 = (f32[64,4096]{1,0:T(8,128)}, f32[64,4096]{1,0:T(8,128)}, u32[]{:S(2)}, u32[]{:S(2)}) collective-permute-start(f32[64,4096]{1,0:T(8,128)} %collective-permute-done.7.refs_1_), channel_id=1, source_target_pairs={{0,1},{1,0},{2,3},{3,2},{4,5},{5,4},{6,7},{7,6},{8,9},{9,8},{10,11... | collective-permute-start | bytes 3145736 | tf_op jit(solution)/shard_map/ppermute | solution.py:142
  123.5 6.5 %copy-start.4 = (f32[8,128,1024]{2,1,0:T(8,128)S(1)}, f32[8,128,1024]{2,1,0:T(8,128)}, u32[]{:S(2)}) copy-start(f32[8,128,1024]{2,1,0:T(8,128)} %all-gather.4.cloned.1.call-done) | copy-start | bytes 12582916
  131.6 30.6 %all-to-all-start = ((f32[8,128,512]{2,1,0:T(8,128)}), f32[8,128,512]{2,1,0:T(8,128)S(1)}, u32[]{:S(2)}, u32[]{:S(2)}) async-start(f32[8,128,512]{2,1,0:T(8,128)} %slice.36), calls=%async_computation | async-start | bytes 4194304 | tf_op jit(solution)/shard_map/all_to_all | solution.py:200
  135.5 52.1 %all-gather.6.cloned.1.call-start = ((), (), s32[]{:S(2)}) async-start(), calls=%async_computation.5 | async-start | bytes 2621440 | tf_op jit(solution)/shard_map/all_gather | solution.py:158
  162.2 31.0 %all-to-all-start.3 = ((f32[8,128,512]{2,1,0:T(8,128)}), f32[8,128,512]{2,1,0:T(8,128)}, u32[]{:S(2)}, u32[]{:S(2)}) async-start(f32[8,128,512]{2,1,0:T(8,128)} %all-gather.8.cloned.1.call-done), calls=%async_computation.3 | async-start | bytes 4194304 | tf_op jit(solution)/shard_map/all_to_all | solution.py:200
  193.2 30.2 %all-to-all-start.2 = ((f32[8,128,512]{2,1,0:T(8,128)}), f32[8,128,512]{2,1,0:T(8,128)S(1)}, u32[]{:S(2)}, u32[]{:S(2)}) async-start(f32[8,128,512]{2,1,0:T(8,128)} %all-gather.6.cloned.1.call-done), calls=%async_computation.2 | async-start | bytes 4194304 | tf_op jit(solution)/shard_map/all_to_all | solution.py:200
  223.4 18.4 %copy-start.1 = (f32[2,128,512]{2,1,0:T(8,128)S(1)}, f32[2,128,512]{2,1,0:T(8,128)}, u32[]{:S(2)}) copy-start(f32[2,128,512]{2,1,0:T(8,128)} %param.8) | copy-start | bytes 1572868
Sparse Core Ops, SparseCore 0:
  9.2 84.7 all-gather.3
  95.6 45.7 all-gather.7
  142.9 44.6 all-gather.5

commit v3 on v2

--- a/solution.py
+++ b/solution.py
@@ -7,8 +7,8 @@
 from jax.experimental.pallas import tpu as pltpu
 from jax.sharding import PartitionSpec as P
 
-GATHERS = ((0, 4), (4, 2), (6, 2))
-CHUNKS = ((0, 0, 2), (0, 2, 2), (1, 4, 2), (2, 6, 2))
+GATHERS = ((0, 3), (3, 3), (6, 2))
+CHUNKS = ((0, 0, 3), (1, 3, 3), (2, 6, 2))
 HIGHEST = lax.Precision.HIGHEST
 SCALE_VMEM = 48 * 1024 * 1024
 UPDATE_VMEM = 48 * 1024 * 1024
@@ -171,10 +171,11 @@
         cores = cores + along(cores, [(i, i ^ bit) for i in range(planes)])
         bit *= 2
 
-    arrived, cores = after(([gathered[s][0] for s in single], cores))
+    near = [cores] + [across(cores, 2 * s) for s in range(1, lines)]
+
+    arrived, near = after(([gathered[s][0] for s in single], near))
     for s, x in zip(single, arrived):
         gathered[s][0] = x
-    near = [cores] + [across(cores, 2 * s) for s in range(1, lines)]
     several = sorted((s for s in range(1, lines) if s not in single), key=lambda s: bin(s).count("1"))
     for s in several:
         low, high = s & -s, 1 << (s.bit_length() - 1)
@@ -182,14 +183,21 @@
             across(gathered[s ^ high][0][0], 2 * high),
             across(gathered[s ^ low][0][1], 2 * low),
         ]
-
-    arrived, near, everywhere[0] = after(([gathered[s][0] for s in several], near, everywhere[0]))
-    for s, x in zip(several, arrived):
-        gathered[s][0] = x
     far = across(jnp.concatenate(near), 1)
-    gathered[0] = [[panel_factors], [across(panel_factors, 1)]]
-    for s in range(1, lines):
-        gathered[s][1] = [across(x, 1) for x in gathered[s][0]]
+    blocks = diagonal_blocks(col.astype(jnp.int32).reshape(1), slot_of_panel, near, far)
+
+    def scale(s, left):
+        place = (line ^ s).astype(jnp.int32).reshape(1)
+        groups = gathered[s][0], [across(x, 1) for x in gathered[s][0]]
+        parts = [(x, 0) for group in groups for x in group]
+        if s == 0:
+            whole = [panel_factors, across(panel_factors, 1)]
+            parts = [(x, half) for x in whole for half in range(2)]
+        return scale_into(place, parts, blocks, s, left, depth)
+
+    left = None
+    for s in [0] + single:
+        left = scale(s, left)
 
     def exchange(number):
         source, first, count = CHUNKS[number]
@@ -200,16 +208,12 @@
         chunk = lax.all_to_all(sent, "col", split_axis=0, concat_axis=0, tiled=True)
         return chunk.reshape(depth, -1)
 
+    arrived, left, everywhere[0] = after(([gathered[s][0] for s in several], left, everywhere[0]))
     chunks = [exchange(0)]
-    blocks = diagonal_blocks(col.astype(jnp.int32).reshape(1), slot_of_panel, near, far)
-
-    left = None
-    for s in range(lines):
-        place = (line ^ s).astype(jnp.int32).reshape(1)
-        parts = []
-        for group in gathered[s]:
-            parts += [(group[0], 0), (group[0], 1)] if len(group) == 1 else [(x, 0) for x in group]
-        left = scale_into(place, parts, blocks, s, left, depth)
+    for s, x in zip(several, arrived):
+        gathered[s][0] = x
+    for s in several:
+        left = scale(s, left)
 
     updated = None
     for number, (_, first, _) in enumerate(CHUNKS):

time: 249 us -> 246 us (0.988)
  waiting for transfers between devices: 87.4 us -> 92.7 us
  Pallas kernels: 103 us -> 98.3 us
  starting transfers between devices: 35 us -> 31.1 us
    all_gather x3, waiting for transfers between devices: 2.67 us -> 28.4 us  [body(): lax.all_gather(column_chunk(*g), 'row', axis=0, tiled=True)]
    all_to_all x4 -> x3, waiting for transfers between devices: 17.7 us -> 8.56 us  [exchange(): chunk = lax.all_to_all(sent, 'col', split_axis=0, concat_axis=0, tiled=True)]
    ppermute x17, waiting for transfers between devices: 57.9 us -> 50.2 us  [across(): return lax.ppermute(x, 'col', [(i, i ^ bits) for i in range(columns)])]
    slice x2 -> x0, local copies, waits for them, and re-layouts: 4.67 us -> none  [exchange(): sent = sent[:, :, at:at + count * eighth]]
    pallas_call x4 -> x3, Pallas kernels: 76.8 us -> 72.4 us  [update_chunk(): pl.pallas_call(update_kernel, grid=(height // tile,), in_specs=[here, sid...]
    all_to_all x4 -> x3, starting transfers between devices: 16.5 us -> 12.7 us  [exchange(): chunk = lax.all_to_all(sent, 'col', split_axis=0, concat_axis=0, tiled=True)]
    ppermute x2, waiting for transfers between devices: 9.15 us -> 5.42 us  [along(): return lax.ppermute(x, 'row', moves)]
  transfers between devices with their start and end apart: 26 -> 25, of which waited for: 13 -> 16; matrix products, arithmetic and copies ran while one was open for 3% -> 2% of each run, Pallas kernels for 34% -> 32%
where the time goes in v3:
time: 246 us; the launch traced here: 245 us
  Pallas kernels  98.3 us (40%)
  waiting for transfers between devices  92.7 us (38%)
  starting transfers between devices  31.1 us (13%)
  between operations  13.2 us (5%)
  local copies, waits for them, and re-layouts  5.38 us (2%)
  other arithmetic  2.77 us (1%)
    pallas_call x3, Pallas kernels, update_chunk(): pl.pallas_call(update_kernel, grid=(height // tile,), in_specs=[here, sid...  72.4 us
    ppermute x17, waiting for transfers between devices, across(): return lax.ppermute(x, 'col', [(i, i ^ bits) for i in range(columns)])  50.2 us
    all_gather x3, waiting for transfers between devices, body(): lax.all_gather(column_chunk(*g), 'row', axis=0, tiled=True)  28.4 us
    pallas_call x4, Pallas kernels, scale_into(): pl.pallas_call(scale_kernel, grid_spec=pltpu.PrefetchScalarGridSpec(num_s...  25.2 us
    all_to_all x3, starting transfers between devices, exchange(): chunk = lax.all_to_all(sent, 'col', split_axis=0, concat_axis=0, tiled=True)  12.7 us
    ppermute x17, starting transfers between devices, across(): return lax.ppermute(x, 'col', [(i, i ^ bits) for i in range(columns)])  12.1 us
    all_to_all x3, waiting for transfers between devices, exchange(): chunk = lax.all_to_all(sent, 'col', split_axis=0, concat_axis=0, tiled=True)  8.56 us
    ppermute x2, starting transfers between devices, along(): return lax.ppermute(x, 'row', moves)  6.19 us
  transfers between devices with their start and end apart: 25, of which 16 were waited for; matrix products, arithmetic and copies ran while one was open for 2% of the time, Pallas kernels for 32%

profile of v3, /device:TPU:0, one launch (start us, length us, event | category | flops | bytes accessed | tf_op | source)
XLA Modules:
  0.0 245.3 jit_solution(1651093183989212469)
XLA Ops:
  6.5 1.6 slice_bitcast_fusion.1
  8.2 1.0 pad_maximum_fusion.1
  9.2 1.6 fusion.1
  11.0 3.1 %collective-permute-start.4 = (f32[2,64,64]{2,1,0:T(8,128)S(1)}, f32[2,64,64]{2,1,0:T(8,128)S(1)}, u32[]{:S(2)}, u32[]{:S(2)}) collective-permute-start(f32[2,64,64]{2,1,0:T(8,128)S(1)} %fusion.2), channel_id=1, source_target_pairs={{0,8},{8,0},{16,24},{24,16},{1,9},{9,1},{17,25},{25,17},{2,10},{10... | collective-permute-start | bytes 98312 | tf_op jit(solution)/shard_map/ppermute | solution.py:145
  14.1 2.2 collective-permute-done.4
  16.4 3.1 %collective-permute-start.5 = (f32[2,64,64]{2,1,0:T(8,128)S(1)}, f32[2,64,64]{2,1,0:T(8,128)S(1)}, u32[]{:S(2)}, u32[]{:S(2)}) collective-permute-start(f32[2,64,64]{2,1,0:T(8,128)S(1)} %add.7), channel_id=1, source_target_pairs={{0,16},{8,24},{16,0},{24,8},{1,17},{9,25},{17,1},{25,9},{2,18},{10... | collective-permute-start | bytes 98312 | tf_op jit(solution)/shard_map/ppermute | solution.py:145
  19.5 3.2 %collective-permute-done.5 = f32[2,64,64]{2,1,0:T(8,128)S(1)} collective-permute-done((f32[2,64,64]{2,1,0:T(8,128)S(1)}, f32[2,64,64]{2,1,0:T(8,128)S(1)}, u32[]{:S(2)}, u32[]{:S(2)}) %collective-permute-start.5) | collective-permute-done | bytes 32800 | tf_op jit(solution)/shard_map/ppermute | solution.py:145
  22.7 2.3 collective-permute-start.8
  25.0 0.4 collective-permute-start.7
  25.4 0.8 collective-permute-start.6
  26.2 1.5 fusion
  27.8 1.3 collective-permute-start.3
  29.0 1.5 collective-permute-start.1
  30.6 0.4 collective-permute-start.2
  31.0 0.8 collective-permute-start
  31.8 0.9 pad_maximum_fusion
  32.8 21.4 %collective-permute-done.3.refs_1_ = f32[64,4096]{1,0:T(8,128)} collective-permute-done((f32[64,4096]{1,0:T(8,128)}, f32[64,4096]{1,0:T(8,128)}, u32[]{:S(2)}, u32[]{:S(2)}) %collective-permute-start.3) | collective-permute-done | bytes 1048608 | tf_op jit(solution)/shard_map/ppermute | solution.py:142
  54.2 1.3 collective-permute-done.1.refs_1_
  55.4 17.6 %collective-permute-done.2.refs_0_ = f32[64,4096]{1,0:T(8,128)} collective-permute-done((f32[64,4096]{1,0:T(8,128)}, f32[64,4096]{1,0:T(8,128)}, u32[]{:S(2)}, u32[]{:S(2)}) %collective-permute-start.2) | collective-permute-done | bytes 1048608 | tf_op jit(solution)/shard_map/ppermute | solution.py:142
  73.1 0.6 collective-permute-done.refs_0_
  73.7 0.6 collective-permute-start.13
  74.3 0.4 collective-permute-start.11
  74.8 1.9 collective-permute-done.13.refs_4_
  77.1 1.0 copy-done.5
  78.0 1.0 collective-permute-start.9
  79.0 1.5 collective-permute-start.10
  80.5 0.8 shard_map.55.refs_4_
  81.3 6.4 %shard_map.56 = (bf16[4096,1024]{1,0:T(8,128)(2,1)}, bf16[4096,1024]{1,0:T(8,128)(2,1)}) custom-call(s32[1]{0:T(128)} %bitcast.6.place, f32[128,4096]{1,0:T(8,128)S(1)} %copy-done.2, f32[128,4096]{1,0:T(8,128)S(1)} %copy-done.2, f32[128,4096]{1,0:T(8,128)} %collective-permute-done.16.refs_2_.refs_3_, f32[128,4096]{1,0:T(8,128)} %collective-permute-done.16.refs_2_.refs_3_, ...), custom_call_target="tpu_custom_call" | custom-call | flops 1 | bytes 1 | tf_op jit(solution)/shard_map/pallas_call | solution.py:43
  87.8 6.1 %shard_map.57 = (bf16[4096,1024]{1,0:T(8,128)(2,1)}, bf16[4096,1024]{1,0:T(8,128)(2,1)}) custom-call(s32[1]{0:T(128)} %bitcast.5.place, f32[64,4096]{1,0:T(8,128)} %collective-permute-done.refs_0_, f32[64,4096]{1,0:T(8,128)} %collective-permute-done.1.refs_1_, ...), custom_call_target="tpu_custom_call", output_to_operand_aliasing={{0}: (6, {}), {1}: (7, {})} | custom-call | flops 1 | bytes 1 | tf_op jit(solution)/shard_map/pallas_call | solution.py:43
  93.9 6.3 %shard_map.58 = (bf16[4096,1024]{1,0:T(8,128)(2,1)}, bf16[4096,1024]{1,0:T(8,128)(2,1)}) custom-call(s32[1]{0:T(128)} %bitcast.3.place, f32[64,4096]{1,0:T(8,128)} %collective-permute-done.2.refs_0_, f32[64,4096]{1,0:T(8,128)} %collective-permute-done.3.refs_1_, ...), custom_call_target="tpu_custom_call", output_to_operand_aliasing={{0}: (6, {}), {1}: (7, {})} | custom-call | flops 1 | bytes 1 | tf_op jit(solution)/shard_map/pallas_call | solution.py:43
  100.2 3.3 %collective-permute-done.9.refs_0_ = f32[64,4096]{1,0:T(8,128)} collective-permute-done((f32[64,4096]{1,0:T(8,128)}, f32[64,4096]{1,0:T(8,128)}, u32[]{:S(2)}, u32[]{:S(2)}) %collective-permute-start.9) | collective-permute-done | bytes 1048608 | tf_op jit(solution)/shard_map/ppermute | solution.py:142
  103.6 0.7 collective-permute-done.10.refs_1_
  104.3 4.5 %all-to-all-start = ((f32[8,128,768]{2,1,0:T(8,128)}), f32[8,128,768]{2,1,0:T(8,128)}, u32[]{:S(2)}, u32[]{:S(2)}) async-start(f32[8,128,768]{2,1,0:T(8,128)} %all-gather.6.cloned.1.call-done), calls=%async_computation | async-start | bytes 6291456 | tf_op jit(solution)/shard_map/all_to_all | solution.py:208
  109.4 0.8 pad_maximum_fusion.2
  110.3 1.9 collective-permute-done.17.refs_2_
  112.2 1.5 collective-permute-done.18.refs_3_
  113.7 1.2 copy-done.4
  114.9 6.3 %shard_map.59 = (bf16[4096,1024]{1,0:T(8,128)(2,1)}, bf16[4096,1024]{1,0:T(8,128)(2,1)}) custom-call(s32[1]{0:T(128)} %bitcast.2.place, f32[64,4096]{1,0:T(8,128)} %collective-permute-done.9.refs_0_, f32[64,4096]{1,0:T(8,128)} %collective-permute-done.10.refs_1_, ...), custom_call_target="tpu_custom_call", output_to_operand_aliasing={{0}: (6, {}), {1}: (7, {})} | custom-call | flops 1 | bytes 1 | tf_op jit(solution)/shard_map/pallas_call | solution.py:43
  121.2 19.3 %all-gather.4.cloned.1.call-done = f32[8,128,768]{2,1,0:T(8,128)} async-done(((f32[2,128,768]{2,1,0:T(8,128)}), f32[8,128,768]{2,1,0:T(8,128)}) %all-gather.4.cloned.1.call-update) | async-done | bytes 3145744 | tf_op jit(solution)/shard_map/all_gather | solution.py:158
  140.4 6.2 %all-to-all-done = f32[8,128,768]{2,1,0:T(8,128)} async-done(((f32[8,128,768]{2,1,0:T(8,128)}), f32[8,128,768]{2,1,0:T(8,128)}, u32[]{:S(2)}, u32[]{:S(2)}) %all-to-all-start) | async-done | bytes 3145760 | tf_op jit(solution)/shard_map/all_to_all | solution.py:208
  146.6 3.7 %all-to-all-start.2 = ((f32[8,128,768]{2,1,0:T(8,128)}), f32[8,128,768]{2,1,0:T(8,128)S(1)}, u32[]{:S(2)}, u32[]{:S(2)}) async-start(f32[8,128,768]{2,1,0:T(8,128)} %all-gather.4.cloned.1.call-done), calls=%async_computation.2 | async-start | bytes 6291456 | tf_op jit(solution)/shard_map/all_to_all | solution.py:208
  150.3 27.1 %shard_map.60.refs_0_ = f32[4096,2048]{1,0:T(8,128)} custom-call(f32[4096,2048]{1,0:T(8,128)} %trailing.5, bf16[4096,1024]{1,0:T(8,128)(2,1)} %get-tuple-element.51.hi, bf16[4096,1024]{1,0:T(8,128)(2,1)} %get-tuple-element.52.lo, f32[1024,768]{1,0:T(8,128)} %bitcast.11.right), custom_call_target="tpu_custom_call" | custom-call | flops 1 | bytes 1 | tf_op jit(solution)/shard_map/pallas_call | solution.py:118
  177.5 9.2 %all-gather.8.cloned.1.call-done = f32[8,128,512]{2,1,0:T(8,128)} async-done(((f32[2,128,512]{2,1,0:T(8,128)}), f32[8,128,512]{2,1,0:T(8,128)}) %all-gather.8.cloned.1.call-update) | async-done | bytes 2097168 | tf_op jit(solution)/shard_map/all_gather | solution.py:158
  186.6 1.5 all-to-all-done.2
  188.1 4.5 %all-to-all-start.1 = ((f32[8,128,512]{2,1,0:T(8,128)}), f32[8,128,512]{2,1,0:T(8,128)}, u32[]{:S(2)}, u32[]{:S(2)}) async-start(f32[8,128,512]{2,1,0:T(8,128)} %all-gather.8.cloned.1.call-done), calls=%async_computation.1 | async-start | bytes 4194304 | tf_op jit(solution)/shard_map/all_to_all | solution.py:208
  192.7 25.6 %shard_map.61.refs_0_ = f32[4096,2048]{1,0:T(8,128)} custom-call(f32[4096,2048]{1,0:T(8,128)} %trailing.5, bf16[4096,1024]{1,0:T(8,128)(2,1)} %get-tuple-element.51.hi, bf16[4096,1024]{1,0:T(8,128)(2,1)} %get-tuple-element.52.lo, f32[1024,768]{1,0:T(8,128)S(1)} %bitcast.24, f32[4096,2048]{1,0:T(8,128)} %shard_map.60.refs_0_), custom_call_target="tpu_custom_call", output_to_operand_aliasing={{}: (4, {})} | custom-call | flops 1 | bytes 1 | tf_op jit(solution)/shard_map/pallas_call | solution.py:118
  218.3 0.8 all-to-all-done.1
  219.1 19.6 %shard_map.62 = f32[4096,2048]{1,0:T(8,128)} custom-call(f32[4096,2048]{1,0:T(8,128)} %trailing.5, bf16[4096,1024]{1,0:T(8,128)(2,1)} %get-tuple-element.51.hi, bf16[4096,1024]{1,0:T(8,128)(2,1)} %get-tuple-element.52.lo, f32[1024,512]{1,0:T(8,128)} %bitcast.12.right, f32[4096,2048]{1,0:T(8,128)} %shard_map.61.refs_0_), custom_call_target="tpu_custom_call", output_to_operand_aliasing={{}: (4, {})} | custom-call | flops 1 | bytes 1 | tf_op jit(solution)/shard_map/pallas_call | solution.py:118
  (40 shorter events, 1.5 us)
Async XLA Ops:
  6.5 2.7 %copy-start = (f32[2,128,512]{2,1,0:T(8,128)S(1)}, f32[2,128,512]{2,1,0:T(8,128)}, u32[]{:S(2)}) copy-start(f32[2,128,512]{2,1,0:T(8,128)} %param.8) | copy-start | bytes 1572868
  6.5 19.7 %copy-start.2 = (f32[128,4096]{1,0:T(8,128)S(1)}, f32[128,4096]{1,0:T(8,128)}, u32[]{:S(2)}) copy-start(f32[128,4096]{1,0:T(8,128)} %refs_1_.1) | copy-start | bytes 6291460
  6.5 74.0 %copy-start.7 = (s32[16]{0:T(128)S(1)}, s32[16]{0:T(128)}, u32[]{:S(2)}) copy-start(s32[16]{0:T(128)} %slots.1) | copy-start | bytes 196
  6.5 97.7 %all-gather.6.cloned.1.call-start = ((), (), s32[]{:S(2)}) async-start(), calls=%async_computation.4 | async-start | bytes 3932160 | tf_op jit(solution)/shard_map/all_gather | solution.py:158
  9.1 131.3 %all-gather.4.cloned.1.call-start = ((), (), s32[]{:S(2)}) async-start(), calls=%async_computation.3 | async-start | bytes 3932160 | tf_op jit(solution)/shard_map/all_gather | solution.py:158
  11.0 5.3 %collective-permute-start.4 = (f32[2,64,64]{2,1,0:T(8,128)S(1)}, f32[2,64,64]{2,1,0:T(8,128)S(1)}, u32[]{:S(2)}, u32[]{:S(2)}) collective-permute-start(f32[2,64,64]{2,1,0:T(8,128)S(1)} %fusion.2), channel_id=1, source_target_pairs={{0,8},{8,0},{16,24},{24,16},{1,9},{9,1},{17,25},{25,17},{2,10},{10... | collective-permute-start | bytes 98312 | tf_op jit(solution)/shard_map/ppermute | solution.py:145
  16.4 6.3 %collective-permute-start.5 = (f32[2,64,64]{2,1,0:T(8,128)S(1)}, f32[2,64,64]{2,1,0:T(8,128)S(1)}, u32[]{:S(2)}, u32[]{:S(2)}) collective-permute-start(f32[2,64,64]{2,1,0:T(8,128)S(1)} %add.7), channel_id=1, source_target_pairs={{0,16},{8,24},{16,0},{24,8},{1,17},{9,25},{17,1},{25,9},{2,18},{10... | collective-permute-start | bytes 98312 | tf_op jit(solution)/shard_map/ppermute | solution.py:145
  22.7 7.9 %collective-permute-start.8 = (f32[2,64,64]{2,1,0:T(8,128)S(1)}, f32[2,64,64]{2,1,0:T(8,128)S(1)}, u32[]{:S(2)}, u32[]{:S(2)}) collective-permute-start(f32[2,64,64]{2,1,0:T(8,128)S(1)} %add.8.refs_0_), channel_id=1, source_target_pairs={{0,6},{1,7},{2,4},{3,5},{4,2},{5,3},{6,0},{7,1},{8,14},{9,15},{10,... | collective-permute-start | bytes 98312 | tf_op jit(solution)/shard_map/ppermute | solution.py:142
  25.0 6.0 %collective-permute-start.7 = (f32[2,64,64]{2,1,0:T(8,128)S(1)}, f32[2,64,64]{2,1,0:T(8,128)S(1)}, u32[]{:S(2)}, u32[]{:S(2)}) collective-permute-start(f32[2,64,64]{2,1,0:T(8,128)S(1)} %add.8.refs_0_), channel_id=1, source_target_pairs={{0,4},{1,5},{2,6},{3,7},{4,0},{5,1},{6,2},{7,3},{8,12},{9,13},{10,... | collective-permute-start | bytes 98312 | tf_op jit(solution)/shard_map/ppermute | solution.py:142
  25.4 6.4 %collective-permute-start.6 = (f32[2,64,64]{2,1,0:T(8,128)S(1)}, f32[2,64,64]{2,1,0:T(8,128)S(1)}, u32[]{:S(2)}, u32[]{:S(2)}) collective-permute-start(f32[2,64,64]{2,1,0:T(8,128)S(1)} %add.8.refs_0_), channel_id=1, source_target_pairs={{0,2},{1,3},{2,0},{3,1},{4,6},{5,7},{6,4},{7,5},{8,10},{9,11},{10,... | collective-permute-start | bytes 98312 | tf_op jit(solution)/shard_map/ppermute | solution.py:142
  27.8 26.4 %collective-permute-start.3 = (f32[64,4096]{1,0:T(8,128)}, f32[64,4096]{1,0:T(8,128)}, u32[]{:S(2)}, u32[]{:S(2)}) collective-permute-start(f32[64,4096]{1,0:T(8,128)} %get-tuple-element.63), channel_id=1, source_target_pairs={{0,4},{1,5},{2,6},{3,7},{4,0},{5,1},{6,2},{7,3},{8,12},{9,13},{10,... | collective-permute-start | bytes 3145736 | tf_op jit(solution)/shard_map/ppermute | solution.py:142
  29.0 26.4 %collective-permute-start.1 = (f32[64,4096]{1,0:T(8,128)}, f32[64,4096]{1,0:T(8,128)}, u32[]{:S(2)}, u32[]{:S(2)}) collective-permute-start(f32[64,4096]{1,0:T(8,128)} %get-tuple-element.63), channel_id=1, source_target_pairs={{0,2},{1,3},{2,0},{3,1},{4,6},{5,7},{6,4},{7,5},{8,10},{9,11},{10,... | collective-permute-start | bytes 3145736 | tf_op jit(solution)/shard_map/ppermute | solution.py:142
  30.6 42.5 %collective-permute-start.2 = (f32[64,4096]{1,0:T(8,128)}, f32[64,4096]{1,0:T(8,128)}, u32[]{:S(2)}, u32[]{:S(2)}) collective-permute-start(f32[64,4096]{1,0:T(8,128)} %get-tuple-element.64), channel_id=1, source_target_pairs={{0,4},{1,5},{2,6},{3,7},{4,0},{5,1},{6,2},{7,3},{8,12},{9,13},{10,... | collective-permute-start | bytes 3145736 | tf_op jit(solution)/shard_map/ppermute | solution.py:142
  31.0 42.7 %collective-permute-start = (f32[64,4096]{1,0:T(8,128)}, f32[64,4096]{1,0:T(8,128)}, u32[]{:S(2)}, u32[]{:S(2)}) collective-permute-start(f32[64,4096]{1,0:T(8,128)} %get-tuple-element.64), channel_id=1, source_target_pairs={{0,2},{1,3},{2,0},{3,1},{4,6},{5,7},{6,4},{7,5},{8,10},{9,11},{10,... | collective-permute-start | bytes 3145736 | tf_op jit(solution)/shard_map/ppermute | solution.py:142
  31.8 47.2 %collective-permute-start.16 = (f32[128,4096]{1,0:T(8,128)S(1)}, f32[128,4096]{1,0:T(8,128)}, u32[]{:S(2)}, u32[]{:S(2)}) collective-permute-start(f32[128,4096]{1,0:T(8,128)S(1)} %copy-done.2), channel_id=1, source_target_pairs={{0,1},{1,0},{2,3},{3,2},{4,5},{5,4},{6,7},{7,6},{8,9},{9,8},{10,11... | collective-permute-start | bytes 6291464 | tf_op jit(solution)/shard_map/ppermute | solution.py:142
  73.7 3.4 %collective-permute-start.15 = (f32[64,4096]{1,0:T(8,128)}, f32[64,4096]{1,0:T(8,128)S(1)}, u32[]{:S(2)}, u32[]{:S(2)}) collective-permute-start(f32[64,4096]{1,0:T(8,128)} %collective-permute-done.1.refs_1_), channel_id=1, source_target_pairs={{0,1},{1,0},{2,3},{3,2},{4,5},{5,4},{6,7},{7,6},{8,9},{9,8},{10,11... | collective-permute-start | bytes 3145736 | tf_op jit(solution)/shard_map/ppermute | solution.py:142
  73.7 3.0 %collective-permute-start.13 = (f32[8,64,64]{2,1,0:T(8,128)S(1)}, f32[8,64,64]{2,1,0:T(8,128)S(1)}, u32[]{:S(2)}, u32[]{:S(2)}) collective-permute-start(f32[8,64,64]{2,1,0:T(8,128)S(1)} %pad_maximum_fusion.3), channel_id=1, source_target_pairs={{0,1},{1,0},{2,3},{3,2},{4,5},{5,4},{6,7},{7,6},{8,9},{9,8},{10,11... | collective-permute-start | bytes 393224 | tf_op jit(solution)/shard_map/ppermute | solution.py:142
  74.3 13.5 %collective-permute-start.14 = (f32[64,4096]{1,0:T(8,128)}, f32[64,4096]{1,0:T(8,128)}, u32[]{:S(2)}, u32[]{:S(2)}) collective-permute-start(f32[64,4096]{1,0:T(8,128)} %collective-permute-done.refs_0_), channel_id=1, source_target_pairs={{0,1},{1,0},{2,3},{3,2},{4,5},{5,4},{6,7},{7,6},{8,9},{9,8},{10,11... | collective-permute-start | bytes 3145736 | tf_op jit(solution)/shard_map/ppermute | solution.py:142
  74.3 19.6 %collective-permute-start.11 = (f32[64,4096]{1,0:T(8,128)}, f32[64,4096]{1,0:T(8,128)}, u32[]{:S(2)}, u32[]{:S(2)}) collective-permute-start(f32[64,4096]{1,0:T(8,128)} %collective-permute-done.2.refs_0_), channel_id=1, source_target_pairs={{0,1},{1,0},{2,3},{3,2},{4,5},{5,4},{6,7},{7,6},{8,9},{9,8},{10,11... | collective-permute-start | bytes 3145736 | tf_op jit(solution)/shard_map/ppermute | solution.py:142
  76.7 17.2 %collective-permute-start.12 = (f32[64,4096]{1,0:T(8,128)}, f32[64,4096]{1,0:T(8,128)}, u32[]{:S(2)}, u32[]{:S(2)}) collective-permute-start(f32[64,4096]{1,0:T(8,128)} %collective-permute-done.3.refs_1_), channel_id=1, source_target_pairs={{0,1},{1,0},{2,3},{3,2},{4,5},{5,4},{6,7},{7,6},{8,9},{9,8},{10,11... | collective-permute-start | bytes 3145736 | tf_op jit(solution)/shard_map/ppermute | solution.py:142
  77.1 1.0 copy-start.5
  78.0 25.5 %collective-permute-start.9 = (f32[64,4096]{1,0:T(8,128)}, f32[64,4096]{1,0:T(8,128)}, u32[]{:S(2)}, u32[]{:S(2)}) collective-permute-start(f32[64,4096]{1,0:T(8,128)} %collective-permute-done.refs_0_), channel_id=1, source_target_pairs={{0,4},{1,5},{2,6},{3,7},{4,0},{5,1},{6,2},{7,3},{8,12},{9,13},{10,... | collective-permute-start | bytes 3145736 | tf_op jit(solution)/shard_map/ppermute | solution.py:142
  79.0 25.2 %collective-permute-start.10 = (f32[64,4096]{1,0:T(8,128)}, f32[64,4096]{1,0:T(8,128)}, u32[]{:S(2)}, u32[]{:S(2)}) collective-permute-start(f32[64,4096]{1,0:T(8,128)} %collective-permute-done.3.refs_1_), channel_id=1, source_target_pairs={{0,2},{1,3},{2,0},{3,1},{4,6},{5,7},{6,4},{7,5},{8,10},{9,11},{10,... | collective-permute-start | bytes 3145736 | tf_op jit(solution)/shard_map/ppermute | solution.py:142
  80.5 7.2 %copy-start.6 = (f32[64,4096]{1,0:T(8,128)S(1)}, f32[64,4096]{1,0:T(8,128)}, u32[]{:S(2)}) copy-start(f32[64,4096]{1,0:T(8,128)} %copy-done.5) | copy-start | bytes 3145732
  81.3 12.6 %copy-start.3 = (f32[4,256,256]{2,1,0:T(8,128)}, f32[4,256,256]{2,1,0:T(8,128)S(1)}, u32[]{:S(2)}) copy-start(f32[4,256,256]{2,1,0:T(8,128)S(1)} %shard_map.55.refs_4_) | copy-start | bytes 3145732
  104.3 42.4 %all-to-all-start = ((f32[8,128,768]{2,1,0:T(8,128)}), f32[8,128,768]{2,1,0:T(8,128)}, u32[]{:S(2)}, u32[]{:S(2)}) async-start(f32[8,128,768]{2,1,0:T(8,128)} %all-gather.6.cloned.1.call-done), calls=%async_computation | async-start | bytes 6291456 | tf_op jit(solution)/shard_map/all_to_all | solution.py:208
  108.7 77.9 %all-gather.8.cloned.1.call-start = ((), (), s32[]{:S(2)}) async-start(), calls=%async_computation.5 | async-start | bytes 2621440 | tf_op jit(solution)/shard_map/all_gather | solution.py:158
  108.8 3.4 %collective-permute-start.17 = (f32[64,4096]{1,0:T(8,128)}, f32[64,4096]{1,0:T(8,128)}, u32[]{:S(2)}, u32[]{:S(2)}) collective-permute-start(f32[64,4096]{1,0:T(8,128)} %collective-permute-done.9.refs_0_), channel_id=1, source_target_pairs={{0,1},{1,0},{2,3},{3,2},{4,5},{5,4},{6,7},{7,6},{8,9},{9,8},{10,11... | collective-permute-start | bytes 3145736 | tf_op jit(solution)/shard_map/ppermute | solution.py:142
  109.1 4.5 %collective-permute-start.18 = (f32[64,4096]{1,0:T(8,128)}, f32[64,4096]{1,0:T(8,128)}, u32[]{:S(2)}, u32[]{:S(2)}) collective-permute-start(f32[64,4096]{1,0:T(8,128)} %collective-permute-done.10.refs_1_), channel_id=1, source_target_pairs={{0,1},{1,0},{2,3},{3,2},{4,5},{5,4},{6,7},{7,6},{8,9},{9,8},{10,11... | collective-permute-start | bytes 3145736 | tf_op jit(solution)/shard_map/ppermute | solution.py:142
  113.7 1.2 copy-start.4
  146.6 41.5 %all-to-all-start.2 = ((f32[8,128,768]{2,1,0:T(8,128)}), f32[8,128,768]{2,1,0:T(8,128)S(1)}, u32[]{:S(2)}, u32[]{:S(2)}) async-start(f32[8,128,768]{2,1,0:T(8,128)} %all-gather.4.cloned.1.call-done), calls=%async_computation.2 | async-start | bytes 6291456 | tf_op jit(solution)/shard_map/all_to_all | solution.py:208
  188.1 31.0 %all-to-all-start.1 = ((f32[8,128,512]{2,1,0:T(8,128)}), f32[8,128,512]{2,1,0:T(8,128)}, u32[]{:S(2)}, u32[]{:S(2)}) async-start(f32[8,128,512]{2,1,0:T(8,128)} %all-gather.8.cloned.1.call-done), calls=%async_computation.1 | async-start | bytes 4194304 | tf_op jit(solution)/shard_map/all_to_all | solution.py:208
  219.1 19.6 %copy-start.1 = (f32[2,128,512]{2,1,0:T(8,128)S(1)}, f32[2,128,512]{2,1,0:T(8,128)}, u32[]{:S(2)}) copy-start(f32[2,128,512]{2,1,0:T(8,128)} %param.8) | copy-start | bytes 1572868
Sparse Core Ops, SparseCore 0:
  9.3 66.1 all-gather.5
  77.1 63.3 all-gather.3
  142.0 44.5 all-gather.7

commit v4 on v3

--- a/solution.py
+++ b/solution.py
@@ -7,8 +7,9 @@
 from jax.experimental.pallas import tpu as pltpu
 from jax.sharding import PartitionSpec as P
 
-GATHERS = ((0, 3), (3, 3), (6, 2))
-CHUNKS = ((0, 0, 3), (1, 3, 3), (2, 6, 2))
+GATHERS = ((0, 3), (4, 2), (6, 2))
+HOPPED = (3, 1)
+CHUNKS = ((0, 3), (3, 3), (6, 2))
 HIGHEST = lax.Precision.HIGHEST
 SCALE_VMEM = 48 * 1024 * 1024
 UPDATE_VMEM = 48 * 1024 * 1024
@@ -98,6 +99,51 @@
     )(col, slots, *near, far)
 
 
+def lay_kernel(planes, plane, *refs):
+    sources, rest, (out, sems) = refs[: 2 * planes - 1], refs[-3], refs[-2:]
+    blocks = out.shape[0] // planes
+    wide = sources[0].shape[2]
+    tail = pltpu.make_async_copy(rest, out.at[:, :, pl.ds(wide, rest.shape[2])], sems.at[planes])
+    tail.start()
+    for z in range(planes):
+
+        @pl.when(plane[0] == z)
+        def _():
+            copies = [
+                pltpu.make_async_copy(
+                    sources[planes - 1 + q - z],
+                    out.at[pl.ds(q * blocks, blocks), :, pl.ds(0, wide)],
+                    sems.at[q],
+                )
+                for q in range(planes)
+            ]
+            for copy in copies:
+                copy.start()
+            for copy in copies:
+                copy.wait()
+
+    tail.wait()
+
+
+def lay(plane, sources, rest):
+    planes = (len(sources) + 1) // 2
+    shape = sources[0].shape
+    result = (rest.shape[0], shape[1], shape[2] + rest.shape[2])
+    return pl.pallas_call(
+        functools.partial(lay_kernel, planes),
+        grid_spec=pltpu.PrefetchScalarGridSpec(
+            num_scalar_prefetch=1,
+            grid=(1,),
+            in_specs=[pl.BlockSpec(memory_space=pl.ANY)] * (len(sources) + 1),
+            out_specs=pl.BlockSpec(result, lambda i, plane: (0, 0, 0)),
+            scratch_shapes=[pltpu.SemaphoreType.DMA((planes + 1,))],
+        ),
+        out_shape=jax.ShapeDtypeStruct(result, jnp.float32),
+        compiler_params=pltpu.CompilerParams(vmem_limit_bytes=SCALE_VMEM),
+        cost_estimate=EARLY,
+    )(plane, *sources, rest)
+
+
 def update_kernel(trailing, hi, lo, right, *refs):
     out, right_hi, right_lo = refs[-3:]
 
@@ -158,10 +204,14 @@
     everywhere = [lax.all_gather(column_chunk(*g), "row", axis=0, tiled=True) for g in GATHERS]
     cut = rows // 2
     own = [panel_factors[:cut], panel_factors[cut:]]
-    gathered = [[own, None]] + [[None, None] for _ in range(lines - 1)]
+    gathered = [[own, None]] + [[[None, None], None] for _ in range(lines - 1)]
     single = [1 << i for i in range(lines.bit_length() - 1)]
+
+    def early(s):
+        return 0 if s == 1 else 1
+
     for s in single:
-        gathered[s][0] = [across(x, 2 * s) for x in own]
+        gathered[s][0][early(s)] = across(own[early(s)], 2 * s)
     solved = lax.dot_general(
         vectors_t, inverse_lower_factors, (((2,), (2,)), ((0,), (0,))), precision=HIGHEST
     )
@@ -171,9 +221,14 @@
         cores = cores + along(cores, [(i, i ^ bit) for i in range(planes)])
         bit *= 2
 
+    arrived, cores, bulk = after(([gathered[s][0][early(s)] for s in single], cores, own))
     near = [cores] + [across(cores, 2 * s) for s in range(1, lines)]
-
-    arrived, near = after(([gathered[s][0] for s in single], near))
+    for s, x in zip(single, arrived):
+        gathered[s][0][early(s)] = x
+        gathered[s][0][1 - early(s)] = across(bulk[1 - early(s)], 2 * s)
+
+    mine = column_chunk(*HOPPED)
+    arrived, near, mine = after(([gathered[s][0] for s in single], near, mine))
     for s, x in zip(single, arrived):
         gathered[s][0] = x
     several = sorted((s for s in range(1, lines) if s not in single), key=lambda s: bin(s).count("1"))
@@ -183,6 +238,14 @@
             across(gathered[s ^ high][0][0], 2 * high),
             across(gathered[s ^ low][0][1], 2 * low),
         ]
+
+    from_above, from_below = [mine], [mine]
+
+    def hop(d):
+        from_above.append(along(from_above[-1], [(p, p - 1) for p in range(1, planes - d + 1)]))
+        from_below.append(along(from_below[-1], [(p, p + 1) for p in range(d - 1, planes - 1)]))
+
+    hop(1)
     far = across(jnp.concatenate(near), 1)
     blocks = diagonal_blocks(col.astype(jnp.int32).reshape(1), slot_of_panel, near, far)
 
@@ -200,30 +263,32 @@
         left = scale(s, left)
 
     def exchange(number):
-        source, first, count = CHUNKS[number]
-        sent = everywhere[source]
-        if GATHERS[source][1] != count:
-            at = (first - GATHERS[source][0]) * eighth
-            sent = sent[:, :, at : at + count * eighth]
-        chunk = lax.all_to_all(sent, "col", split_axis=0, concat_axis=0, tiled=True)
+        chunk = lax.all_to_all(everywhere[number], "col", split_axis=0, concat_axis=0, tiled=True)
         return chunk.reshape(depth, -1)
 
-    arrived, left, everywhere[0] = after(([gathered[s][0] for s in several], left, everywhere[0]))
+    arrived, left, everywhere[0], hopped = after(
+        ([gathered[s][0] for s in several], left, everywhere[0], (from_above[-1], from_below[-1]))
+    )
+    from_above[-1], from_below[-1] = hopped
     chunks = [exchange(0)]
     for s, x in zip(several, arrived):
         gathered[s][0] = x
+    for d in range(2, planes):
+        hop(d)
     for s in several:
         left = scale(s, left)
+    plane = lax.axis_index("row").astype(jnp.int32).reshape(1)
+    everywhere[1] = lay(plane, from_below[:0:-1] + [mine] + from_above[1:], everywhere[1])
 
     updated = None
-    for number, (_, first, _) in enumerate(CHUNKS):
-        if number + 1 < len(CHUNKS):
-            source = CHUNKS[number + 1][0]
+    for number, (first, _) in enumerate(CHUNKS):
+        later = number + 1
+        if later < len(CHUNKS):
             if updated is None:
-                everywhere[source], left = after((everywhere[source], left))
+                everywhere[later], left = after((everywhere[later], left))
             else:
-                everywhere[source], updated = after((everywhere[source], updated))
-            chunks.append(exchange(number + 1))
+                everywhere[later], updated = after((everywhere[later], updated))
+            chunks.append(exchange(later))
         updated = update_chunk(first * eighth, trailing, left, chunks[number], updated)
     return updated
 

time: 246 us -> 254 us (1.033)
  starting transfers between devices: 31.1 us -> 41.5 us
  waiting for transfers between devices: 92.7 us -> 85.8 us
  local copies, waits for them, and re-layouts: 5.38 us -> 9.41 us
    ppermute x2 -> x8, waiting for transfers between devices: 5.42 us -> 40 us  [along(): return lax.ppermute(x, 'row', moves)]
    all_gather x3, waiting for transfers between devices: 28.4 us -> 0.04 us  [body(): lax.all_gather(column_chunk(*g), 'row', axis=0, tiled=True)]
    ppermute x17, waiting for transfers between devices: 50.2 us -> 33.5 us  [across(): return lax.ppermute(x, 'col', [(i, i ^ bits) for i in range(columns)])]
    ppermute x2 -> x8, starting transfers between devices: 6.19 us -> 15.1 us  [along(): return lax.ppermute(x, 'row', moves)]
    unnamed x16 -> x28, local copies, waits for them, and re-layouts: 2.21 us -> 7.04 us
    all_to_all x3, waiting for transfers between devices: 8.56 us -> 12.2 us  [exchange(): lax.all_to_all(everywhere[number], 'col', split_axis=0, concat_axis=0, ti...]
    pallas_call x0 -> x1, Pallas kernels: none -> 3.16 us  [lay(): pl.pallas_call(functools.partial(lay_kernel, planes), grid_spec=pltpu.Pre...]
  transfers between devices with their start and end apart: 25 -> 31, of which waited for: 16 -> 11; matrix products, arithmetic and copies ran while one was open for 2% -> 2% of each run, Pallas kernels for 32% -> 32%
where the time goes in v4:
time: 254 us
  Pallas kernels  98.9 us (39%)
  waiting for transfers between devices  85.8 us (34%)
  starting transfers between devices  41.5 us (16%)
  between operations  13.4 us (5%)
  local copies, waits for them, and re-layouts  9.41 us (4%)
  other arithmetic  3.71 us (1%)
    pallas_call x3, Pallas kernels, update_chunk(): pl.pallas_call(update_kernel, grid=(height // tile,), in_specs=[here, sid...  71.2 us
    ppermute x8, waiting for transfers between devices, along(): return lax.ppermute(x, 'row', moves)  40 us
    ppermute x17, waiting for transfers between devices, across(): return lax.ppermute(x, 'col', [(i, i ^ bits) for i in range(columns)])  33.5 us
    pallas_call x4, Pallas kernels, scale_into(): pl.pallas_call(scale_kernel, grid_spec=pltpu.PrefetchScalarGridSpec(num_s...  23.7 us
    ppermute x8, starting transfers between devices, along(): return lax.ppermute(x, 'row', moves)  15.1 us
    ppermute x17, starting transfers between devices, across(): return lax.ppermute(x, 'col', [(i, i ^ bits) for i in range(columns)])  14.4 us
    all_to_all x3, waiting for transfers between devices, exchange(): lax.all_to_all(everywhere[number], 'col', split_axis=0, concat_axis=0, ti...  12.2 us
    all_to_all x3, starting transfers between devices, exchange(): lax.all_to_all(everywhere[number], 'col', split_axis=0, concat_axis=0, ti...  11.9 us
  transfers between devices with their start and end apart: 31, of which 11 were waited for; matrix products, arithmetic and copies ran while one was open for 2% of the time, Pallas kernels for 32%

profile of v4, /device:TPU:0, one launch (start us, length us, event | category | flops | bytes accessed | tf_op | source)
XLA Modules:
  0.0 253.6 jit_solution(9096351751916689475)
XLA Ops:
  6.5 1.3 slice_bitcast_fusion.1
  7.9 1.0 pad_maximum_fusion
  9.1 3.0 %collective-permute-start.1 = (f32[64,4096]{1,0:T(8,128)S(1)}, f32[64,4096]{1,0:T(8,128)}, u32[]{:S(2)}, u32[]{:S(2)}) collective-permute-start(f32[64,4096]{1,0:T(8,128)S(1)} %get-tuple-element.40), channel_id=1, source_target_pairs={{0,4},{1,5},{2,6},{3,7},{4,0},{5,1},{6,2},{7,3},{8,12},{9,13},{10,... | collective-permute-start | bytes 3145736 | tf_op jit(solution)/shard_map/ppermute | solution.py:188
  12.1 1.5 collective-permute-start
  13.6 0.7 fusion.1
  14.5 1.6 collective-permute-start.2
  16.2 2.7 %collective-permute-done.2 = f32[2,64,64]{2,1,0:T(8,128)S(1)} collective-permute-done((f32[2,64,64]{2,1,0:T(8,128)S(1)}, f32[2,64,64]{2,1,0:T(8,128)S(1)}, u32[]{:S(2)}, u32[]{:S(2)}) %collective-permute-start.2) | collective-permute-done | bytes 32800 | tf_op jit(solution)/shard_map/ppermute | solution.py:191
  18.9 2.7 %collective-permute-start.3 = (f32[2,64,64]{2,1,0:T(8,128)S(1)}, f32[2,64,64]{2,1,0:T(8,128)S(1)}, u32[]{:S(2)}, u32[]{:S(2)}) collective-permute-start(f32[2,64,64]{2,1,0:T(8,128)S(1)} %add.7), channel_id=1, source_target_pairs={{0,16},{8,24},{16,0},{24,8},{1,17},{9,25},{17,1},{25,9},{2,18},{10... | collective-permute-start | bytes 98312 | tf_op jit(solution)/shard_map/ppermute | solution.py:191
  21.5 6.1 %collective-permute-done.3 = f32[2,64,64]{2,1,0:T(8,128)S(1)} collective-permute-done((f32[2,64,64]{2,1,0:T(8,128)S(1)}, f32[2,64,64]{2,1,0:T(8,128)S(1)}, u32[]{:S(2)}, u32[]{:S(2)}) %collective-permute-start.3) | collective-permute-done | bytes 32800 | tf_op jit(solution)/shard_map/ppermute | solution.py:191
  27.7 7.7 %collective-permute-done.1.refs_1_ = f32[64,4096]{1,0:T(8,128)} collective-permute-done((f32[64,4096]{1,0:T(8,128)S(1)}, f32[64,4096]{1,0:T(8,128)}, u32[]{:S(2)}, u32[]{:S(2)}) %collective-permute-start.1) | collective-permute-done | bytes 1048608 | tf_op jit(solution)/shard_map/ppermute | solution.py:188
  35.4 1.5 collective-permute-done.refs_0_
  36.8 1.5 collective-permute-start.4
  38.8 1.5 collective-permute-start.8
  40.8 21.4 %collective-permute-done.8.refs_3_ = f32[2,64,64]{2,1,0:T(8,128)S(1)} collective-permute-done((f32[2,64,64]{2,1,0:T(8,128)S(1)}, f32[2,64,64]{2,1,0:T(8,128)S(1)}, u32[]{:S(2)}, u32[]{:S(2)}) %collective-permute-start.8) | collective-permute-done | bytes 32800 | tf_op jit(solution)/shard_map/ppermute | solution.py:188
  62.2 1.4 collective-permute-start.6
  63.6 1.0 collective-permute-done.7.refs_2_
  64.6 1.9 collective-permute-done.6.refs_1_
  66.5 1.1 copy-done.8
  68.6 1.3 copy-done.5
  69.9 1.4 collective-permute-start.9
  71.5 1.0 copy-done.10
  72.5 1.4 collective-permute-start.10
  73.9 0.9 slice_bitcast_fusion.3
  74.8 0.8 pad_maximum_fusion.1
  75.7 4.2 %collective-permute-start.18 = (f32[2,128,256]{2,1,0:T(8,128)S(1)}, f32[2,128,256]{2,1,0:T(8,128)}, u32[]{:S(2)}, u32[]{:S(2)}) collective-permute-start(f32[2,128,256]{2,1,0:T(8,128)S(1)} %pad_maximum_fusion.3.refs_3_), channel_id=1, source_target_pairs={{0,8},{8,16},{16,24},{1,9},{9,17},{17,25},{2,10},{10,18},{18,26},{... | collective-permute-start | bytes 786440 | tf_op jit(solution)/shard_map/ppermute | solution.py:191
  79.9 1.3 collective-permute-start.17
  81.2 0.8 shard_map.55.refs_4_
  82.0 2.1 copy-done.6
  84.1 4.7 %shard_map.56 = (bf16[4096,1024]{1,0:T(8,128)(2,1)}, bf16[4096,1024]{1,0:T(8,128)(2,1)}) custom-call(s32[1]{0:T(128)} %bitcast.6.place, f32[128,4096]{1,0:T(8,128)S(1)} %copy-done.2, f32[128,4096]{1,0:T(8,128)S(1)} %copy-done.2, f32[128,4096]{1,0:T(8,128)S(1)} %copy-done.6, f32[128,4096]{1,0:T(8,128)S(1)} %copy-done.6, f32[4,256,256]{2,1,0:T(8,128)S(1)} %shard_map.55.refs_4_), custom_call_target="tpu_custom_call" | custom-call | flops 1 | bytes 1 | tf_op jit(solution)/shard_map/pallas_call | solution.py:44
  88.8 6.5 %shard_map.57 = (bf16[4096,1024]{1,0:T(8,128)(2,1)}, bf16[4096,1024]{1,0:T(8,128)(2,1)}) custom-call(s32[1]{0:T(128)} %bitcast.5.place, f32[64,4096]{1,0:T(8,128)} %collective-permute-done.refs_0_, f32[64,4096]{1,0:T(8,128)} %collective-permute-done.4.refs_1_, ...), custom_call_target="tpu_custom_call", output_to_operand_aliasing={{0}: (6, {}), {1}: (7, {})} | custom-call | flops 1 | bytes 1 | tf_op jit(solution)/shard_map/pallas_call | solution.py:44
  95.3 6.0 %shard_map.58 = (bf16[4096,1024]{1,0:T(8,128)(2,1)}, bf16[4096,1024]{1,0:T(8,128)(2,1)}) custom-call(s32[1]{0:T(128)} %bitcast.3.place, f32[64,4096]{1,0:T(8,128)S(1)} %copy-done.9, f32[64,4096]{1,0:T(8,128)} %collective-permute-done.1.refs_1_, f32[64,4096]{1,0:T(8,128)S(1)} %copy-done.11, ...), custom_call_target="tpu_custom_call", output_to_operand_aliasing={{0}: (6, {}), {1}: (7, {})} | custom-call | flops 1 | bytes 1 | tf_op jit(solution)/shard_map/pallas_call | solution.py:44
  101.4 3.7 %all-to-all-start = ((f32[8,128,768]{2,1,0:T(8,128)}), f32[8,128,768]{2,1,0:T(8,128)S(1)}, u32[]{:S(2)}, u32[]{:S(2)}) async-start(f32[8,128,768]{2,1,0:T(8,128)} %all-gather.4.cloned.1.call-done), calls=%async_computation | async-start | bytes 6291456 | tf_op jit(solution)/shard_map/all_to_all | solution.py:266
  105.7 1.4 collective-permute-start.19
  107.1 1.3 collective-permute-start.21
  108.4 1.9 pad_maximum_fusion.2
  110.3 1.4 collective-permute-start.20
  111.6 17.5 %collective-permute-done.21.refs_5_ = f32[2,128,256]{2,1,0:T(8,128)} collective-permute-done((f32[2,128,256]{2,1,0:T(8,128)}, f32[2,128,256]{2,1,0:T(8,128)}, u32[]{:S(2)}, u32[]{:S(2)}) %collective-permute-start.21) | collective-permute-done | bytes 262176 | tf_op jit(solution)/shard_map/ppermute | solution.py:191
  129.2 1.3 collective-permute-start.22
  130.5 13.6 %collective-permute-done.22.refs_6_ = f32[2,128,256]{2,1,0:T(8,128)} collective-permute-done((f32[2,128,256]{2,1,0:T(8,128)}, f32[2,128,256]{2,1,0:T(8,128)}, u32[]{:S(2)}, u32[]{:S(2)}) %collective-permute-start.22) | collective-permute-done | bytes 262176 | tf_op jit(solution)/shard_map/ppermute | solution.py:191
  144.2 1.6 copy-done.7
  145.8 3.2 %shard_map.59 = f32[8,128,768]{2,1,0:T(8,128)} custom-call(s32[1]{0:T(128)} %bitcast.plane, f32[2,128,256]{2,1,0:T(8,128)} %collective-permute-done.20.refs_0_, f32[2,128,256]{2,1,0:T(8,128)} %collective-permute-done.19.refs_1_, f32[2,128,256]{2,1,0:T(8,128)} %collective-permute-done.18.refs_2_, f32[2,128,256]{2,1,0:T(8,128)S(1)} %pad_maximum_fusion.3.refs_3_, ...), custom_call_target="tpu_custom_call" | custom-call | flops 1 | bytes 1 | tf_op jit(solution)/shard_map/pallas_call | solution.py:132
  149.0 6.4 %shard_map.60 = (bf16[4096,1024]{1,0:T(8,128)(2,1)}, bf16[4096,1024]{1,0:T(8,128)(2,1)}) custom-call(s32[1]{0:T(128)} %bitcast.11.place, f32[64,4096]{1,0:T(8,128)} %collective-permute-done.9.refs_0_, f32[64,4096]{1,0:T(8,128)} %collective-permute-done.10.refs_1_, ...), custom_call_target="tpu_custom_call", output_to_operand_aliasing={{0}: (6, {}), {1}: (7, {})} | custom-call | flops 1 | bytes 1 | tf_op jit(solution)/shard_map/pallas_call | solution.py:44
  155.4 4.5 %all-to-all-start.2 = ((f32[8,128,768]{2,1,0:T(8,128)}), f32[8,128,768]{2,1,0:T(8,128)}, u32[]{:S(2)}, u32[]{:S(2)}) async-start(f32[8,128,768]{2,1,0:T(8,128)} %shard_map.59), calls=%async_computation.2 | async-start | bytes 6291456 | tf_op jit(solution)/shard_map/all_to_all | solution.py:266
  159.8 25.7 %shard_map.61.refs_0_ = f32[4096,2048]{1,0:T(8,128)} custom-call(f32[4096,2048]{1,0:T(8,128)} %trailing.5, bf16[4096,1024]{1,0:T(8,128)(2,1)} %get-tuple-element.67.hi, bf16[4096,1024]{1,0:T(8,128)(2,1)} %get-tuple-element.68.lo, f32[1024,768]{1,0:T(8,128)S(1)} %bitcast.29), custom_call_target="tpu_custom_call" | custom-call | flops 1 | bytes 1 | tf_op jit(solution)/shard_map/pallas_call | solution.py:164
  185.5 12.2 %all-to-all-done.2 = f32[8,128,768]{2,1,0:T(8,128)} async-done(((f32[8,128,768]{2,1,0:T(8,128)}), f32[8,128,768]{2,1,0:T(8,128)}, u32[]{:S(2)}, u32[]{:S(2)}) %all-to-all-start.2) | async-done | bytes 3145760 | tf_op jit(solution)/shard_map/all_to_all | solution.py:266
  197.7 3.8 %all-to-all-start.1 = ((f32[8,128,512]{2,1,0:T(8,128)}), f32[8,128,512]{2,1,0:T(8,128)S(1)}, u32[]{:S(2)}, u32[]{:S(2)}) async-start(f32[8,128,512]{2,1,0:T(8,128)} %all-gather.8.cloned.1.call-done), calls=%async_computation.1 | async-start | bytes 4194304 | tf_op jit(solution)/shard_map/all_to_all | solution.py:266
  201.5 27.1 %shard_map.62.refs_0_ = f32[4096,2048]{1,0:T(8,128)} custom-call(f32[4096,2048]{1,0:T(8,128)} %trailing.5, bf16[4096,1024]{1,0:T(8,128)(2,1)} %get-tuple-element.67.hi, bf16[4096,1024]{1,0:T(8,128)(2,1)} %get-tuple-element.68.lo, f32[1024,768]{1,0:T(8,128)} %bitcast.16.right, f32[4096,2048]{1,0:T(8,128)} %shard_map.61.refs_0_), custom_call_target="tpu_custom_call", output_to_operand_aliasing={{}: (4, {})} | custom-call | flops 1 | bytes 1 | tf_op jit(solution)/shard_map/pallas_call | solution.py:164
  228.7 18.4 %shard_map.63 = f32[4096,2048]{1,0:T(8,128)} custom-call(f32[4096,2048]{1,0:T(8,128)} %trailing.5, bf16[4096,1024]{1,0:T(8,128)(2,1)} %get-tuple-element.67.hi, bf16[4096,1024]{1,0:T(8,128)(2,1)} %get-tuple-element.68.lo, f32[1024,512]{1,0:T(8,128)S(1)} %bitcast.30, f32[4096,2048]{1,0:T(8,128)} %shard_map.62.refs_0_), custom_call_target="tpu_custom_call", output_to_operand_aliasing={{}: (4, {})} | custom-call | flops 1 | bytes 1 | tf_op jit(solution)/shard_map/pallas_call | solution.py:164
  (67 shorter events, 3.5 us)
Async XLA Ops:
  6.5 7.1 %copy-start = (f32[2,128,512]{2,1,0:T(8,128)S(1)}, f32[2,128,512]{2,1,0:T(8,128)}, u32[]{:S(2)}) copy-start(f32[2,128,512]{2,1,0:T(8,128)} %param.8) | copy-start | bytes 1572868
  6.5 2.4 copy-start.2
  6.5 94.9 %all-gather.4.cloned.1.call-start = ((), (), s32[]{:S(2)}) async-start(), calls=%async_computation.3 | async-start | bytes 3932160 | tf_op jit(solution)/shard_map/all_gather | solution.py:204
  7.9 5.7 %copy-start.13 = (f32[2,64,512]{2,1,0:T(8,128)S(1)}, f32[2,64,512]{2,1,0:T(8,128)}, u32[]{:S(2)}) copy-start(f32[2,64,512]{2,1,0:T(8,128)} %param.7) | copy-start | bytes 786436
  8.9 121.6 %all-gather.6.cloned.1.call-start = ((), (), s32[]{:S(2)}) async-start(), calls=%async_computation.4 | async-start | bytes 2621440 | tf_op jit(solution)/shard_map/all_gather | solution.py:204
  9.1 26.3 %collective-permute-start.1 = (f32[64,4096]{1,0:T(8,128)S(1)}, f32[64,4096]{1,0:T(8,128)}, u32[]{:S(2)}, u32[]{:S(2)}) collective-permute-start(f32[64,4096]{1,0:T(8,128)S(1)} %get-tuple-element.40), channel_id=1, source_target_pairs={{0,4},{1,5},{2,6},{3,7},{4,0},{5,1},{6,2},{7,3},{8,12},{9,13},{10,... | collective-permute-start | bytes 3145736 | tf_op jit(solution)/shard_map/ppermute | solution.py:188
  12.1 24.7 %collective-permute-start = (f32[64,4096]{1,0:T(8,128)S(1)}, f32[64,4096]{1,0:T(8,128)}, u32[]{:S(2)}, u32[]{:S(2)}) collective-permute-start(f32[64,4096]{1,0:T(8,128)S(1)} %get-tuple-element.41), channel_id=1, source_target_pairs={{0,2},{1,3},{2,0},{3,1},{4,6},{5,7},{6,4},{7,5},{8,10},{9,11},{10,... | collective-permute-start | bytes 3145736 | tf_op jit(solution)/shard_map/ppermute | solution.py:188
  14.3 66.9 %copy-start.12 = (s32[16]{0:T(128)S(1)}, s32[16]{0:T(128)}, u32[]{:S(2)}) copy-start(s32[16]{0:T(128)} %slots.1) | copy-start | bytes 196
  14.5 4.3 %collective-permute-start.2 = (f32[2,64,64]{2,1,0:T(8,128)S(1)}, f32[2,64,64]{2,1,0:T(8,128)S(1)}, u32[]{:S(2)}, u32[]{:S(2)}) collective-permute-start(f32[2,64,64]{2,1,0:T(8,128)S(1)} %fusion.2), channel_id=1, source_target_pairs={{0,8},{8,0},{16,24},{24,16},{1,9},{9,1},{17,25},{25,17},{2,10},{10... | collective-permute-start | bytes 98312 | tf_op jit(solution)/shard_map/ppermute | solution.py:191
  18.9 8.8 %collective-permute-start.3 = (f32[2,64,64]{2,1,0:T(8,128)S(1)}, f32[2,64,64]{2,1,0:T(8,128)S(1)}, u32[]{:S(2)}, u32[]{:S(2)}) collective-permute-start(f32[2,64,64]{2,1,0:T(8,128)S(1)} %add.7), channel_id=1, source_target_pairs={{0,16},{8,24},{16,0},{24,8},{1,17},{9,25},{17,1},{25,9},{2,18},{10... | collective-permute-start | bytes 98312 | tf_op jit(solution)/shard_map/ppermute | solution.py:191
  36.8 29.6 %collective-permute-start.4 = (f32[64,4096]{1,0:T(8,128)S(1)}, f32[64,4096]{1,0:T(8,128)}, u32[]{:S(2)}, u32[]{:S(2)}) collective-permute-start(f32[64,4096]{1,0:T(8,128)S(1)} %get-tuple-element.40), channel_id=1, source_target_pairs={{0,2},{1,3},{2,0},{3,1},{4,6},{5,7},{6,4},{7,5},{8,10},{9,11},{10,... | collective-permute-start | bytes 3145736 | tf_op jit(solution)/shard_map/ppermute | solution.py:188
  38.3 28.1 %collective-permute-start.5 = (f32[64,4096]{1,0:T(8,128)S(1)}, f32[64,4096]{1,0:T(8,128)S(1)}, u32[]{:S(2)}, u32[]{:S(2)}) collective-permute-start(f32[64,4096]{1,0:T(8,128)S(1)} %get-tuple-element.41), channel_id=1, source_target_pairs={{0,4},{1,5},{2,6},{3,7},{4,0},{5,1},{6,2},{7,3},{8,12},{9,13},{10,... | collective-permute-start | bytes 3145736 | tf_op jit(solution)/shard_map/ppermute | solution.py:188
  38.8 29.8 %collective-permute-start.16 = (f32[128,4096]{1,0:T(8,128)S(1)}, f32[128,4096]{1,0:T(8,128)S(1)}, u32[]{:S(2)}, u32[]{:S(2)}) collective-permute-start(f32[128,4096]{1,0:T(8,128)S(1)} %copy-done.2), channel_id=1, source_target_pairs={{0,1},{1,0},{2,3},{3,2},{4,5},{5,4},{6,7},{7,6},{8,9},{9,8},{10,11... | collective-permute-start | bytes 6291464 | tf_op jit(solution)/shard_map/ppermute | solution.py:188
  38.8 23.3 %collective-permute-start.8 = (f32[2,64,64]{2,1,0:T(8,128)S(1)}, f32[2,64,64]{2,1,0:T(8,128)S(1)}, u32[]{:S(2)}, u32[]{:S(2)}) collective-permute-start(f32[2,64,64]{2,1,0:T(8,128)S(1)} %add.8.refs_0_), channel_id=1, source_target_pairs={{0,6},{1,7},{2,4},{3,5},{4,2},{5,3},{6,0},{7,1},{8,14},{9,15},{10,... | collective-permute-start | bytes 98312 | tf_op jit(solution)/shard_map/ppermute | solution.py:188
  40.4 24.2 %collective-permute-start.7 = (f32[2,64,64]{2,1,0:T(8,128)S(1)}, f32[2,64,64]{2,1,0:T(8,128)S(1)}, u32[]{:S(2)}, u32[]{:S(2)}) collective-permute-start(f32[2,64,64]{2,1,0:T(8,128)S(1)} %add.8.refs_0_), channel_id=1, source_target_pairs={{0,4},{1,5},{2,6},{3,7},{4,0},{5,1},{6,2},{7,3},{8,12},{9,13},{10,... | collective-permute-start | bytes 98312 | tf_op jit(solution)/shard_map/ppermute | solution.py:188
  62.2 4.3 %collective-permute-start.6 = (f32[2,64,64]{2,1,0:T(8,128)S(1)}, f32[2,64,64]{2,1,0:T(8,128)S(1)}, u32[]{:S(2)}, u32[]{:S(2)}) collective-permute-start(f32[2,64,64]{2,1,0:T(8,128)S(1)} %add.8.refs_0_), channel_id=1, source_target_pairs={{0,2},{1,3},{2,0},{3,1},{4,6},{5,7},{6,4},{7,5},{8,10},{9,11},{10,... | collective-permute-start | bytes 98312 | tf_op jit(solution)/shard_map/ppermute | solution.py:188
  66.4 5.0 %collective-permute-start.11 = (f32[64,4096]{1,0:T(8,128)S(1)}, f32[64,4096]{1,0:T(8,128)S(1)}, u32[]{:S(2)}, u32[]{:S(2)}) collective-permute-start(f32[64,4096]{1,0:T(8,128)S(1)} %collective-permute-done.5.refs_0_), channel_id=1, source_target_pairs={{0,1},{1,0},{2,3},{3,2},{4,5},{5,4},{6,7},{7,6},{8,9},{9,8},{10,11... | collective-permute-start | bytes 3145736 | tf_op jit(solution)/shard_map/ppermute | solution.py:188
  66.5 1.1 copy-start.8
  67.5 8.1 %collective-permute-start.15 = (f32[64,4096]{1,0:T(8,128)}, f32[64,4096]{1,0:T(8,128)}, u32[]{:S(2)}, u32[]{:S(2)}) collective-permute-start(f32[64,4096]{1,0:T(8,128)} %collective-permute-done.4.refs_1_), channel_id=1, source_target_pairs={{0,1},{1,0},{2,3},{3,2},{4,5},{5,4},{6,7},{7,6},{8,9},{9,8},{10,11... | collective-permute-start | bytes 3145736 | tf_op jit(solution)/shard_map/ppermute | solution.py:188
  68.0 11.9 %collective-permute-start.14 = (f32[64,4096]{1,0:T(8,128)}, f32[64,4096]{1,0:T(8,128)}, u32[]{:S(2)}, u32[]{:S(2)}) collective-permute-start(f32[64,4096]{1,0:T(8,128)} %collective-permute-done.refs_0_), channel_id=1, source_target_pairs={{0,1},{1,0},{2,3},{3,2},{4,5},{5,4},{6,7},{7,6},{8,9},{9,8},{10,11... | collective-permute-start | bytes 3145736 | tf_op jit(solution)/shard_map/ppermute | solution.py:188
  68.1 3.3 %collective-permute-start.13 = (f32[8,64,64]{2,1,0:T(8,128)S(1)}, f32[8,64,64]{2,1,0:T(8,128)S(1)}, u32[]{:S(2)}, u32[]{:S(2)}) collective-permute-start(f32[8,64,64]{2,1,0:T(8,128)S(1)} %pad_maximum_fusion.4), channel_id=1, source_target_pairs={{0,1},{1,0},{2,3},{3,2},{4,5},{5,4},{6,7},{7,6},{8,9},{9,8},{10,11... | collective-permute-start | bytes 393224 | tf_op jit(solution)/shard_map/ppermute | solution.py:188
  68.6 1.3 copy-start.5
  69.9 31.4 %collective-permute-start.9 = (f32[64,4096]{1,0:T(8,128)}, f32[64,4096]{1,0:T(8,128)}, u32[]{:S(2)}, u32[]{:S(2)}) collective-permute-start(f32[64,4096]{1,0:T(8,128)} %collective-permute-done.refs_0_), channel_id=1, source_target_pairs={{0,4},{1,5},{2,6},{3,7},{4,0},{5,1},{6,2},{7,3},{8,12},{9,13},{10,... | collective-permute-start | bytes 3145736 | tf_op jit(solution)/shard_map/ppermute | solution.py:188
  71.4 23.9 %collective-permute-start.12 = (f32[64,4096]{1,0:T(8,128)}, f32[64,4096]{1,0:T(8,128)}, u32[]{:S(2)}, u32[]{:S(2)}) collective-permute-start(f32[64,4096]{1,0:T(8,128)} %collective-permute-done.1.refs_1_), channel_id=1, source_target_pairs={{0,1},{1,0},{2,3},{3,2},{4,5},{5,4},{6,7},{7,6},{8,9},{9,8},{10,11... | collective-permute-start | bytes 3145736 | tf_op jit(solution)/shard_map/ppermute | solution.py:188
  71.5 1.0 copy-start.10
  72.5 28.9 %collective-permute-start.10 = (f32[64,4096]{1,0:T(8,128)}, f32[64,4096]{1,0:T(8,128)}, u32[]{:S(2)}, u32[]{:S(2)}) collective-permute-start(f32[64,4096]{1,0:T(8,128)} %collective-permute-done.1.refs_1_), channel_id=1, source_target_pairs={{0,2},{1,3},{2,0},{3,1},{4,6},{5,7},{6,4},{7,5},{8,10},{9,11},{10,... | collective-permute-start | bytes 3145736 | tf_op jit(solution)/shard_map/ppermute | solution.py:188
  75.7 25.7 %collective-permute-start.18 = (f32[2,128,256]{2,1,0:T(8,128)S(1)}, f32[2,128,256]{2,1,0:T(8,128)}, u32[]{:S(2)}, u32[]{:S(2)}) collective-permute-start(f32[2,128,256]{2,1,0:T(8,128)S(1)} %pad_maximum_fusion.3.refs_3_), channel_id=1, source_target_pairs={{0,8},{8,16},{16,24},{1,9},{9,17},{17,25},{2,10},{10,18},{18,26},{... | collective-permute-start | bytes 786440 | tf_op jit(solution)/shard_map/ppermute | solution.py:191
  79.9 21.5 %collective-permute-start.17 = (f32[2,128,256]{2,1,0:T(8,128)S(1)}, f32[2,128,256]{2,1,0:T(8,128)}, u32[]{:S(2)}, u32[]{:S(2)}) collective-permute-start(f32[2,128,256]{2,1,0:T(8,128)S(1)} %pad_maximum_fusion.3.refs_3_), channel_id=1, source_target_pairs={{8,0},{16,8},{24,16},{9,1},{17,9},{25,17},{10,2},{18,10},{26,18},{... | collective-permute-start | bytes 786440 | tf_op jit(solution)/shard_map/ppermute | solution.py:191
  82.0 13.3 %copy-start.3 = (f32[4,256,256]{2,1,0:T(8,128)}, f32[4,256,256]{2,1,0:T(8,128)S(1)}, u32[]{:S(2)}) copy-start(f32[4,256,256]{2,1,0:T(8,128)S(1)} %shard_map.55.refs_4_) | copy-start | bytes 3145732
  82.0 2.1 copy-start.6
  88.8 6.5 %copy-start.9 = (f32[64,4096]{1,0:T(8,128)S(1)}, f32[64,4096]{1,0:T(8,128)}, u32[]{:S(2)}) copy-start(f32[64,4096]{1,0:T(8,128)} %copy-done.8) | copy-start | bytes 3145732
  88.8 6.5 %copy-start.11 = (f32[64,4096]{1,0:T(8,128)S(1)}, f32[64,4096]{1,0:T(8,128)}, u32[]{:S(2)}) copy-start(f32[64,4096]{1,0:T(8,128)} %copy-done.10) | copy-start | bytes 3145732
  101.4 54.0 %all-to-all-start = ((f32[8,128,768]{2,1,0:T(8,128)}), f32[8,128,768]{2,1,0:T(8,128)S(1)}, u32[]{:S(2)}, u32[]{:S(2)}) async-start(f32[8,128,768]{2,1,0:T(8,128)} %all-gather.4.cloned.1.call-done), calls=%async_computation | async-start | bytes 6291456 | tf_op jit(solution)/shard_map/all_to_all | solution.py:266
  105.1 80.4 %all-gather.8.cloned.1.call-start = ((), (), s32[]{:S(2)}) async-start(), calls=%async_computation.5 | async-start | bytes 2621440 | tf_op jit(solution)/shard_map/all_gather | solution.py:204
  105.1 43.8 %collective-permute-start.23 = (f32[64,4096]{1,0:T(8,128)}, f32[64,4096]{1,0:T(8,128)}, u32[]{:S(2)}, u32[]{:S(2)}) collective-permute-start(f32[64,4096]{1,0:T(8,128)} %collective-permute-done.9.refs_0_), channel_id=1, source_target_pairs={{0,1},{1,0},{2,3},{3,2},{4,5},{5,4},{6,7},{7,6},{8,9},{9,8},{10,11... | collective-permute-start | bytes 3145736 | tf_op jit(solution)/shard_map/ppermute | solution.py:188
  105.5 43.4 %collective-permute-start.24 = (f32[64,4096]{1,0:T(8,128)}, f32[64,4096]{1,0:T(8,128)}, u32[]{:S(2)}, u32[]{:S(2)}) collective-permute-start(f32[64,4096]{1,0:T(8,128)} %collective-permute-done.10.refs_1_), channel_id=1, source_target_pairs={{0,1},{1,0},{2,3},{3,2},{4,5},{5,4},{6,7},{7,6},{8,9},{9,8},{10,11... | collective-permute-start | bytes 3145736 | tf_op jit(solution)/shard_map/ppermute | solution.py:188
  105.7 4.5 %collective-permute-start.19 = (f32[2,128,256]{2,1,0:T(8,128)}, f32[2,128,256]{2,1,0:T(8,128)}, u32[]{:S(2)}, u32[]{:S(2)}) collective-permute-start(f32[2,128,256]{2,1,0:T(8,128)} %collective-permute-done.18.refs_2_), channel_id=1, source_target_pairs={{8,16},{16,24},{9,17},{17,25},{10,18},{18,26},{11,19},{19,27},{12,... | collective-permute-start | bytes 786440 | tf_op jit(solution)/shard_map/ppermute | solution.py:191
  107.1 22.1 %collective-permute-start.21 = (f32[2,128,256]{2,1,0:T(8,128)}, f32[2,128,256]{2,1,0:T(8,128)}, u32[]{:S(2)}, u32[]{:S(2)}) collective-permute-start(f32[2,128,256]{2,1,0:T(8,128)} %collective-permute-done.17.refs_4_), channel_id=1, source_target_pairs={{8,0},{16,8},{9,1},{17,9},{10,2},{18,10},{11,3},{19,11},{12,4},{20... | collective-permute-start | bytes 786440 | tf_op jit(solution)/shard_map/ppermute | solution.py:191
  110.3 20.2 %collective-permute-start.20 = (f32[2,128,256]{2,1,0:T(8,128)}, f32[2,128,256]{2,1,0:T(8,128)}, u32[]{:S(2)}, u32[]{:S(2)}) collective-permute-start(f32[2,128,256]{2,1,0:T(8,128)} %collective-permute-done.19.refs_1_), channel_id=1, source_target_pairs={{16,24},{17,25},{18,26},{19,27},{20,28},{21,29},{22,30},{23,31}} | collective-permute-start | bytes 786440 | tf_op jit(solution)/shard_map/ppermute | solution.py:191
  129.2 15.0 %collective-permute-start.22 = (f32[2,128,256]{2,1,0:T(8,128)}, f32[2,128,256]{2,1,0:T(8,128)}, u32[]{:S(2)}, u32[]{:S(2)}) collective-permute-start(f32[2,128,256]{2,1,0:T(8,128)} %collective-permute-done.21.refs_5_), channel_id=1, source_target_pairs={{8,0},{9,1},{10,2},{11,3},{12,4},{13,5},{14,6},{15,7}} | collective-permute-start | bytes 786440 | tf_op jit(solution)/shard_map/ppermute | solution.py:191
  144.2 1.6 copy-start.7
  145.8 3.2 %copy-start.4 = (f32[4,256,256]{2,1,0:T(8,128)S(1)}, f32[4,256,256]{2,1,0:T(8,128)}, u32[]{:S(2)}) copy-start(f32[4,256,256]{2,1,0:T(8,128)} %copy-done.3) | copy-start | bytes 3145732
  155.4 42.4 %all-to-all-start.2 = ((f32[8,128,768]{2,1,0:T(8,128)}), f32[8,128,768]{2,1,0:T(8,128)}, u32[]{:S(2)}, u32[]{:S(2)}) async-start(f32[8,128,768]{2,1,0:T(8,128)} %shard_map.59), calls=%async_computation.2 | async-start | bytes 6291456 | tf_op jit(solution)/shard_map/all_to_all | solution.py:266
  197.7 30.9 %all-to-all-start.1 = ((f32[8,128,512]{2,1,0:T(8,128)}), f32[8,128,512]{2,1,0:T(8,128)S(1)}, u32[]{:S(2)}, u32[]{:S(2)}) async-start(f32[8,128,512]{2,1,0:T(8,128)} %all-gather.8.cloned.1.call-done), calls=%async_computation.1 | async-start | bytes 4194304 | tf_op jit(solution)/shard_map/all_to_all | solution.py:266
  228.7 18.4 %copy-start.1 = (f32[2,128,512]{2,1,0:T(8,128)S(1)}, f32[2,128,512]{2,1,0:T(8,128)}, u32[]{:S(2)}) copy-start(f32[2,128,512]{2,1,0:T(8,128)} %param.8) | copy-start | bytes 1572868
Sparse Core Ops, SparseCore 0:
  9.0 67.1 all-gather.3
  77.7 50.2 all-gather.5
  129.6 43.8 all-gather.7

commit v5 on v3

--- a/solution.py
+++ b/solution.py
@@ -7,8 +7,7 @@
 from jax.experimental.pallas import tpu as pltpu
 from jax.sharding import PartitionSpec as P
 
-GATHERS = ((0, 3), (3, 3), (6, 2))
-CHUNKS = ((0, 0, 3), (1, 3, 3), (2, 6, 2))
+CHUNKS = ((0, 3), (3, 3), (6, 2))
 HIGHEST = lax.Precision.HIGHEST
 SCALE_VMEM = 48 * 1024 * 1024
 UPDATE_VMEM = 48 * 1024 * 1024
@@ -26,10 +25,17 @@
 
 
 def scale_kernel(place, *refs):
-    parts, cores, (hi, lo) = refs[:4], refs[4], refs[-2:]
-    group = jnp.concatenate([part[...] for part in parts], axis=0)
-    scaled = dot3(*split(cores[0]), *split(group))
-    hi[...], lo[...] = split(scaled.T)
+    parts, cores, (out, low) = refs[:4], refs[4], refs[-2:]
+
+    @pl.when(pl.program_id(1) == 0)
+    def _():
+        group = jnp.concatenate([part[...] for part in parts], axis=0)
+        scaled = dot3(*split(cores[0]), *split(group))
+        out[...], low[...] = split(scaled.T)
+
+    @pl.when(pl.program_id(1) == 1)
+    def _():
+        out[...] = low[...]
 
 
 def scale_into(place, parts, cores, line, previous, depth):
@@ -37,24 +43,23 @@
     rows = cores.shape[1]
     half = rows // 4
     tile = min(width, 1024)
-    block = pl.BlockSpec((tile, rows), lambda i, place: (i, place[0]))
-    shape = jax.ShapeDtypeStruct((width, depth), jnp.bfloat16)
-    held = [] if previous is None else list(previous)
+    held = [] if previous is None else [previous]
     return pl.pallas_call(
         scale_kernel,
         grid_spec=pltpu.PrefetchScalarGridSpec(
             num_scalar_prefetch=1,
-            grid=(width // tile,),
+            grid=(width // tile, 2),
             in_specs=[
-                pl.BlockSpec((half, tile), functools.partial(lambda at, i, place: (at, i), at))
+                pl.BlockSpec((half, tile), functools.partial(lambda at, i, j, place: (at, i), at))
                 for _, at in parts
             ]
-            + [pl.BlockSpec((1, rows, rows), lambda i, place: (line, 0, 0))]
+            + [pl.BlockSpec((1, rows, rows), lambda i, j, place: (line, 0, 0))]
             + [pl.BlockSpec(memory_space=pl.ANY)] * len(held),
-            out_specs=[block, block],
+            out_specs=pl.BlockSpec((tile, rows), lambda i, j, place: (i, place[0] + j * (depth // rows))),
+            scratch_shapes=[pltpu.VMEM((tile, rows), jnp.bfloat16)],
         ),
-        out_shape=[shape, shape],
-        input_output_aliases={} if previous is None else {6: 0, 7: 1},
+        out_shape=jax.ShapeDtypeStruct((width, 2 * depth), jnp.bfloat16),
+        input_output_aliases={} if previous is None else {6: 0},
         compiler_params=pltpu.CompilerParams(vmem_limit_bytes=SCALE_VMEM),
         cost_estimate=EARLY,
     )(place, *(a for a, _ in parts), cores, *held)
@@ -98,14 +103,18 @@
     )(col, slots, *near, far)
 
 
-def update_kernel(trailing, hi, lo, right, *refs):
-    out, right_hi, right_lo = refs[-3:]
+def update_kernel(trailing, left, right, *refs):
+    out, twice, low = refs[-3:]
+    depth = right.shape[0]
 
     @pl.when(pl.program_id(0) == 0)
     def _():
-        right_hi[...], right_lo[...] = split(right[...])
-
-    out[...] = trailing[...] - dot3(hi[...], lo[...], right_hi[...], right_lo[...])
+        high, low[...] = split(right[...])
+        twice[:depth] = high
+        twice[depth:] = high
+
+    dot = functools.partial(jnp.dot, preferred_element_type=jnp.float32)
+    out[...] = trailing[...] - (dot(left[...], twice[...]) + dot(left[:, :depth], low[...]))
 
 
 def update_chunk(start, trailing, left, right, previous):
@@ -113,20 +122,26 @@
     depth, wide = right.shape
     tile = min(height, 1024)
     here = pl.BlockSpec((tile, wide), lambda i: (i, start // wide))
-    side = pl.BlockSpec((tile, depth), lambda i: (i, 0))
     held = [] if previous is None else [previous]
     return pl.pallas_call(
         update_kernel,
         grid=(height // tile,),
-        in_specs=[here, side, side, pl.BlockSpec((depth, wide), lambda i: (0, 0))]
+        in_specs=[
+            here,
+            pl.BlockSpec((tile, 2 * depth), lambda i: (i, 0)),
+            pl.BlockSpec((depth, wide), lambda i: (0, 0)),
+        ]
         + [pl.BlockSpec(memory_space=pl.ANY)] * len(held),
         out_specs=here,
         out_shape=jax.ShapeDtypeStruct(trailing.shape, jnp.float32),
-        scratch_shapes=[pltpu.VMEM((depth, wide), jnp.bfloat16)] * 2,
-        input_output_aliases={} if previous is None else {4: 0},
+        scratch_shapes=[
+            pltpu.VMEM((2 * depth, wide), jnp.bfloat16),
+            pltpu.VMEM((depth, wide), jnp.bfloat16),
+        ],
+        input_output_aliases={} if previous is None else {3: 0},
         compiler_params=pltpu.CompilerParams(vmem_limit_bytes=UPDATE_VMEM),
         cost_estimate=EARLY,
-    )(trailing, *left, right, *held)
+    )(trailing, left, right, *held)
 
 
 def body(planes, columns, trailing, panel_factors, vectors_t, inverse_lower_factors, slot_of_panel):
@@ -155,13 +170,17 @@
 
     after = lax.optimization_barrier
 
-    everywhere = [lax.all_gather(column_chunk(*g), "row", axis=0, tiled=True) for g in GATHERS]
+    everywhere = [lax.all_gather(column_chunk(*g), "row", axis=0, tiled=True) for g in CHUNKS]
     cut = rows // 2
     own = [panel_factors[:cut], panel_factors[cut:]]
-    gathered = [[own, None]] + [[None, None] for _ in range(lines - 1)]
+    gathered = [[own, None]] + [[[None, None], None] for _ in range(lines - 1)]
     single = [1 << i for i in range(lines.bit_length() - 1)]
+
+    def early(s):
+        return 0 if s == 1 else 1
+
     for s in single:
-        gathered[s][0] = [across(x, 2 * s) for x in own]
+        gathered[s][0][early(s)] = across(own[early(s)], 2 * s)
     solved = lax.dot_general(
         vectors_t, inverse_lower_factors, (((2,), (2,)), ((0,), (0,))), precision=HIGHEST
     )
@@ -173,9 +192,10 @@
 
     near = [cores] + [across(cores, 2 * s) for s in range(1, lines)]
 
-    arrived, near = after(([gathered[s][0] for s in single], near))
+    arrived, near, own = after(([gathered[s][0][early(s)] for s in single], near, own))
     for s, x in zip(single, arrived):
-        gathered[s][0] = x
+        gathered[s][0][early(s)] = x
+        gathered[s][0][1 - early(s)] = across(own[1 - early(s)], 2 * s)
     several = sorted((s for s in range(1, lines) if s not in single), key=lambda s: bin(s).count("1"))
     for s in several:
         low, high = s & -s, 1 << (s.bit_length() - 1)
@@ -183,6 +203,12 @@
             across(gathered[s ^ high][0][0], 2 * high),
             across(gathered[s ^ low][0][1], 2 * low),
         ]
+
+    arrived, near, everywhere[0] = after(
+        ([gathered[s][0] for s in range(1, lines)], near, everywhere[0])
+    )
+    for s, x in zip(range(1, lines), arrived):
+        gathered[s][0] = x
     far = across(jnp.concatenate(near), 1)
     blocks = diagonal_blocks(col.astype(jnp.int32).reshape(1), slot_of_panel, near, far)
 
@@ -195,35 +221,25 @@
             parts = [(x, half) for x in whole for half in range(2)]
         return scale_into(place, parts, blocks, s, left, depth)
 
+    def exchange(number):
+        chunk = lax.all_to_all(everywhere[number], "col", split_axis=0, concat_axis=0, tiled=True)
+        return chunk.reshape(depth, -1)
+
+    chunks = [exchange(0)]
+
     left = None
-    for s in [0] + single:
+    for s in range(lines):
         left = scale(s, left)
 
-    def exchange(number):
-        source, first, count = CHUNKS[number]
-        sent = everywhere[source]
-        if GATHERS[source][1] != count:
-            at = (first - GATHERS[source][0]) * eighth
-            sent = sent[:, :, at : at + count * eighth]
-        chunk = lax.all_to_all(sent, "col", split_axis=0, concat_axis=0, tiled=True)
-        return chunk.reshape(depth, -1)
-
-    arrived, left, everywhere[0] = after(([gathered[s][0] for s in several], left, everywhere[0]))
-    chunks = [exchange(0)]
-    for s, x in zip(several, arrived):
-        gathered[s][0] = x
-    for s in several:
-        left = scale(s, left)
-
     updated = None
-    for number, (_, first, _) in enumerate(CHUNKS):
-        if number + 1 < len(CHUNKS):
-            source = CHUNKS[number + 1][0]
+    for number, (first, _) in enumerate(CHUNKS):
+        later = number + 1
+        if later < len(CHUNKS):
             if updated is None:
-                everywhere[source], left = after((everywhere[source], left))
+                everywhere[later], left = after((everywhere[later], left))
             else:
-                everywhere[source], updated = after((everywhere[source], updated))
-            chunks.append(exchange(number + 1))
+                everywhere[later], updated = after((everywhere[later], updated))
+            chunks.append(exchange(later))
         updated = update_chunk(first * eighth, trailing, left, chunks[number], updated)
     return updated
 

time: 246 us -> 245 us (level)
  Pallas kernels: 98.3 us -> 114 us
  waiting for transfers between devices: 92.7 us -> 79.6 us
  local copies, waits for them, and re-layouts: 5.38 us -> 2.72 us
    pallas_call x4, Pallas kernels: 25.2 us -> 40.1 us  [scale_into(): pl.pallas_call(scale_kernel, grid_spec=pltpu.PrefetchScalarGridSpec(num_s...]
    all_gather x3, waiting for transfers between devices: 28.4 us -> 15.6 us  [body(): lax.all_gather(column_chunk(*g), 'row', axis=0, tiled=True)]
    all_to_all x3, waiting for transfers between devices: 8.56 us -> 0.91 us  [exchange(): lax.all_to_all(everywhere[number], 'col', split_axis=0, concat_axis=0, ti...]
    ppermute x2, waiting for transfers between devices: 5.42 us -> 9.24 us  [along(): return lax.ppermute(x, 'row', moves)]
    ppermute x17, waiting for transfers between devices: 50.2 us -> 53.8 us  [across(): return lax.ppermute(x, 'col', [(i, i ^ bits) for i in range(columns)])]
  transfers between devices with their start and end apart: 25 -> 25, of which waited for: 16 -> 11; matrix products, arithmetic and copies ran while one was open for 2% -> 1% of each run, Pallas kernels for 32% -> 39%
where the time goes in v5:
time: 245 us; the launch traced here: 244 us
  Pallas kernels  114 us (47%)
  waiting for transfers between devices  79.6 us (32%)
  starting transfers between devices  31.1 us (13%)
  between operations  13.3 us (5%)
  other arithmetic  2.76 us (1%)
  local copies, waits for them, and re-layouts  2.72 us (1%)
    pallas_call x3, Pallas kernels, update_chunk(): pl.pallas_call(update_kernel, grid=(height // tile,), in_specs=[here, pl....  72.9 us
    ppermute x17, waiting for transfers between devices, across(): return lax.ppermute(x, 'col', [(i, i ^ bits) for i in range(columns)])  53.8 us
    pallas_call x4, Pallas kernels, scale_into(): pl.pallas_call(scale_kernel, grid_spec=pltpu.PrefetchScalarGridSpec(num_s...  40.1 us
    all_gather x3, waiting for transfers between devices, body(): lax.all_gather(column_chunk(*g), 'row', axis=0, tiled=True)  15.6 us
    ppermute x17, starting transfers between devices, across(): return lax.ppermute(x, 'col', [(i, i ^ bits) for i in range(columns)])  14.1 us
    all_to_all x3, starting transfers between devices, exchange(): lax.all_to_all(everywhere[number], 'col', split_axis=0, concat_axis=0, ti...  12.7 us
    ppermute x2, waiting for transfers between devices, along(): return lax.ppermute(x, 'row', moves)  9.24 us
  transfers between devices with their start and end apart: 25, of which 11 were waited for; matrix products, arithmetic and copies ran while one was open for 1% of the time, Pallas kernels for 39%

profile of v5, /device:TPU:0, one launch (start us, length us, event | category | flops | bytes accessed | tf_op | source)
XLA Modules:
  0.0 244.1 jit_solution(2636266539590768510)
XLA Ops:
  6.5 1.5 slice_bitcast_fusion.1
  8.1 0.9 pad_maximum_fusion.1
  9.1 0.9 pad_maximum_fusion
  10.1 0.2 fusion
  10.2 3.0 %collective-permute-start.1 = (f32[64,4096]{1,0:T(8,128)S(1)}, f32[64,4096]{1,0:T(8,128)}, u32[]{:S(2)}, u32[]{:S(2)}) collective-permute-start(f32[64,4096]{1,0:T(8,128)S(1)} %get-tuple-element.29), channel_id=1, source_target_pairs={{0,4},{1,5},{2,6},{3,7},{4,0},{5,1},{6,2},{7,3},{8,12},{9,13},{10,... | collective-permute-start | bytes 3145736 | tf_op jit(solution)/shard_map/ppermute | solution.py:157
  13.3 1.5 collective-permute-start
  14.8 0.7 fusion.1
  15.4 0.2 fusion.2
  15.7 1.6 collective-permute-start.2
  17.3 2.7 %collective-permute-done.2 = f32[2,64,64]{2,1,0:T(8,128)S(1)} collective-permute-done((f32[2,64,64]{2,1,0:T(8,128)S(1)}, f32[2,64,64]{2,1,0:T(8,128)S(1)}, u32[]{:S(2)}, u32[]{:S(2)}) %collective-permute-start.2) | collective-permute-done | bytes 32800 | tf_op jit(solution)/shard_map/ppermute | solution.py:160
  20.0 2.7 %collective-permute-start.3 = (f32[2,64,64]{2,1,0:T(8,128)S(1)}, f32[2,64,64]{2,1,0:T(8,128)S(1)}, u32[]{:S(2)}, u32[]{:S(2)}) collective-permute-start(f32[2,64,64]{2,1,0:T(8,128)S(1)} %add.7), channel_id=1, source_target_pairs={{0,16},{8,24},{16,0},{24,8},{1,17},{9,25},{17,1},{25,9},{2,18},{10... | collective-permute-start | bytes 98312 | tf_op jit(solution)/shard_map/ppermute | solution.py:160
  22.7 6.6 %collective-permute-done.3 = f32[2,64,64]{2,1,0:T(8,128)S(1)} collective-permute-done((f32[2,64,64]{2,1,0:T(8,128)S(1)}, f32[2,64,64]{2,1,0:T(8,128)S(1)}, u32[]{:S(2)}, u32[]{:S(2)}) %collective-permute-start.3) | collective-permute-done | bytes 32800 | tf_op jit(solution)/shard_map/ppermute | solution.py:160
  29.2 0.1 collective-permute-start.6
  29.3 1.6 collective-permute-start.5
  30.9 1.9 collective-permute-start.4
  32.8 7.0 %collective-permute-done.6.refs_3_ = f32[2,64,64]{2,1,0:T(8,128)S(1)} collective-permute-done((f32[2,64,64]{2,1,0:T(8,128)S(1)}, f32[2,64,64]{2,1,0:T(8,128)S(1)}, u32[]{:S(2)}, u32[]{:S(2)}) %collective-permute-start.6) | collective-permute-done | bytes 32800 | tf_op jit(solution)/shard_map/ppermute | solution.py:157
  39.8 0.9 collective-permute-done.4.refs_1_
  40.7 1.5 collective-permute-start.7
  42.2 0.8 collective-permute-start.8
  43.0 1.2 collective-permute-start.9
  44.2 0.5 collective-permute-start.10
  44.8 22.1 %collective-permute-done.7.refs_1_ = f32[64,4096]{1,0:T(8,128)} collective-permute-done((f32[64,4096]{1,0:T(8,128)S(1)}, f32[64,4096]{1,0:T(8,128)}, u32[]{:S(2)}, u32[]{:S(2)}) %collective-permute-start.7) | collective-permute-done | bytes 1048608 | tf_op jit(solution)/shard_map/ppermute | solution.py:157
  66.9 1.5 collective-permute-done.8.refs_0_
  68.4 19.9 %collective-permute-done.9.refs_0_ = f32[64,4096]{1,0:T(8,128)} collective-permute-done((f32[64,4096]{1,0:T(8,128)}, f32[64,4096]{1,0:T(8,128)}, u32[]{:S(2)}, u32[]{:S(2)}) %collective-permute-start.9) | collective-permute-done | bytes 1048608 | tf_op jit(solution)/shard_map/ppermute | solution.py:157
  88.3 4.5 %all-to-all-start = ((f32[8,128,768]{2,1,0:T(8,128)}), f32[8,128,768]{2,1,0:T(8,128)}, u32[]{:S(2)}, u32[]{:S(2)}) async-start(f32[8,128,768]{2,1,0:T(8,128)} %all-gather.6.cloned.1.call-done), calls=%async_computation | async-start | bytes 6291456 | tf_op jit(solution)/shard_map/all_to_all | solution.py:225
  92.9 0.4 collective-permute-start.16
  93.3 0.3 collective-permute-start.13
  93.5 0.3 collective-permute-start.14
  93.8 0.2 collective-permute-start.17
  94.0 0.3 collective-permute-start.15
  94.4 2.3 collective-permute-done.13.refs_4_
  96.6 0.1 collective-permute-start.11
  96.8 1.0 copy-done.3
  97.8 0.4 collective-permute-start.12
  98.2 0.8 pad_maximum_fusion.2
  99.1 0.8 shard_map.55.refs_4_
  99.9 9.7 %shard_map.56.refs_5_ = bf16[4096,2048]{1,0:T(8,128)(2,1)} custom-call(s32[1]{0:T(128)} %bitcast.8.place, f32[128,4096]{1,0:T(8,128)S(1)} %copy-done.2, f32[128,4096]{1,0:T(8,128)S(1)} %copy-done.2, f32[128,4096]{1,0:T(8,128)} %collective-permute-done.18.refs_2_.refs_3_, f32[128,4096]{1,0:T(8,128)} %collective-permute-done.18.refs_2_.refs_3_, ...), custom_call_target="tpu_custom_call" | custom-call | flops 1 | bytes 1 | tf_op jit(solution)/shard_map/pallas_call | solution.py:47
  109.6 9.9 %shard_map.57.refs_5_ = bf16[4096,2048]{1,0:T(8,128)(2,1)} custom-call(s32[1]{0:T(128)} %bitcast.7.place, f32[64,4096]{1,0:T(8,128)} %collective-permute-done.refs_0_, f32[64,4096]{1,0:T(8,128)} %collective-permute-done.7.refs_1_, f32[64,4096]{1,0:T(8,128)S(1)} %copy-done.4, ...), custom_call_target="tpu_custom_call", output_to_operand_aliasing={{}: (6, {})} | custom-call | flops 1 | bytes 1 | tf_op jit(solution)/shard_map/pallas_call | solution.py:47
  119.5 10.2 %shard_map.58.refs_5_ = bf16[4096,2048]{1,0:T(8,128)(2,1)} custom-call(s32[1]{0:T(128)} %bitcast.6.place, f32[64,4096]{1,0:T(8,128)} %collective-permute-done.8.refs_0_, f32[64,4096]{1,0:T(8,128)} %collective-permute-done.1.refs_1_, f32[64,4096]{1,0:T(8,128)} %collective-permute-done.14.refs_2_, ...), custom_call_target="tpu_custom_call", output_to_operand_aliasing={{}: (6, {})} | custom-call | flops 1 | bytes 1 | tf_op jit(solution)/shard_map/pallas_call | solution.py:47
  129.7 10.2 %shard_map.59.left = bf16[4096,2048]{1,0:T(8,128)(2,1)} custom-call(s32[1]{0:T(128)} %bitcast.2.place, f32[64,4096]{1,0:T(8,128)} %collective-permute-done.9.refs_0_, f32[64,4096]{1,0:T(8,128)} %collective-permute-done.10.refs_1_, f32[64,4096]{1,0:T(8,128)} %collective-permute-done.11.refs_2_, ...), custom_call_target="tpu_custom_call", output_to_operand_aliasing={{}: (6, {})} | custom-call | flops 1 | bytes 1 | tf_op jit(solution)/shard_map/pallas_call | solution.py:47
  140.0 0.8 all-gather.4.cloned.1.call-done
  140.8 3.7 %all-to-all-start.2 = ((f32[8,128,768]{2,1,0:T(8,128)}), f32[8,128,768]{2,1,0:T(8,128)S(1)}, u32[]{:S(2)}, u32[]{:S(2)}) async-start(f32[8,128,768]{2,1,0:T(8,128)} %all-gather.4.cloned.1.call-done), calls=%async_computation.2 | async-start | bytes 6291456 | tf_op jit(solution)/shard_map/all_to_all | solution.py:225
  144.4 27.8 %shard_map.60.refs_0_ = f32[4096,2048]{1,0:T(8,128)} custom-call(f32[4096,2048]{1,0:T(8,128)} %trailing.5, bf16[4096,2048]{1,0:T(8,128)(2,1)} %shard_map.59.left, f32[1024,768]{1,0:T(8,128)} %bitcast.11.right), custom_call_target="tpu_custom_call" | custom-call | flops 1 | bytes 1 | tf_op jit(solution)/shard_map/pallas_call | solution.py:126
  172.2 14.8 %all-gather.8.cloned.1.call-done = f32[8,128,512]{2,1,0:T(8,128)} async-done(((f32[2,128,512]{2,1,0:T(8,128)}), f32[8,128,512]{2,1,0:T(8,128)}) %all-gather.8.cloned.1.call-update) | async-done | bytes 2097168 | tf_op jit(solution)/shard_map/all_gather | solution.py:173
  187.0 4.5 %all-to-all-start.1 = ((f32[8,128,512]{2,1,0:T(8,128)}), f32[8,128,512]{2,1,0:T(8,128)}, u32[]{:S(2)}, u32[]{:S(2)}) async-start(f32[8,128,512]{2,1,0:T(8,128)} %all-gather.8.cloned.1.call-done), calls=%async_computation.1 | async-start | bytes 4194304 | tf_op jit(solution)/shard_map/all_to_all | solution.py:225
  191.5 25.6 %shard_map.61.refs_0_ = f32[4096,2048]{1,0:T(8,128)} custom-call(f32[4096,2048]{1,0:T(8,128)} %trailing.5, bf16[4096,2048]{1,0:T(8,128)(2,1)} %shard_map.59.left, f32[1024,768]{1,0:T(8,128)S(1)} %bitcast.24, f32[4096,2048]{1,0:T(8,128)} %shard_map.60.refs_0_), custom_call_target="tpu_custom_call", output_to_operand_aliasing={{}: (3, {})} | custom-call | flops 1 | bytes 1 | tf_op jit(solution)/shard_map/pallas_call | solution.py:126
  217.1 0.9 all-to-all-done.1
  218.0 19.6 %shard_map.62 = f32[4096,2048]{1,0:T(8,128)} custom-call(f32[4096,2048]{1,0:T(8,128)} %trailing.5, bf16[4096,2048]{1,0:T(8,128)(2,1)} %shard_map.59.left, f32[1024,512]{1,0:T(8,128)} %bitcast.12.right, f32[4096,2048]{1,0:T(8,128)} %shard_map.61.refs_0_), custom_call_target="tpu_custom_call", output_to_operand_aliasing={{}: (3, {})} | custom-call | flops 1 | bytes 1 | tf_op jit(solution)/shard_map/pallas_call | solution.py:126
  (38 shorter events, 0.3 us)
Async XLA Ops:
  6.5 8.2 %copy-start = (f32[2,128,512]{2,1,0:T(8,128)S(1)}, f32[2,128,512]{2,1,0:T(8,128)}, u32[]{:S(2)}) copy-start(f32[2,128,512]{2,1,0:T(8,128)} %param.8) | copy-start | bytes 1572868
  6.5 81.8 %all-gather.6.cloned.1.call-start = ((), (), s32[]{:S(2)}) async-start(), calls=%async_computation.4 | async-start | bytes 3932160 | tf_op jit(solution)/shard_map/all_gather | solution.py:173
  8.1 2.0 copy-start.2
  9.0 131.7 %all-gather.4.cloned.1.call-start = ((), (), s32[]{:S(2)}) async-start(), calls=%async_computation.3 | async-start | bytes 3932160 | tf_op jit(solution)/shard_map/all_gather | solution.py:173
  10.0 4.7 %copy-start.6 = (f32[2,64,512]{2,1,0:T(8,128)S(1)}, f32[2,64,512]{2,1,0:T(8,128)}, u32[]{:S(2)}) copy-start(f32[2,64,512]{2,1,0:T(8,128)} %param.7) | copy-start | bytes 786436
  10.2 30.5 %collective-permute-start.1 = (f32[64,4096]{1,0:T(8,128)S(1)}, f32[64,4096]{1,0:T(8,128)}, u32[]{:S(2)}, u32[]{:S(2)}) collective-permute-start(f32[64,4096]{1,0:T(8,128)S(1)} %get-tuple-element.29), channel_id=1, source_target_pairs={{0,4},{1,5},{2,6},{3,7},{4,0},{5,1},{6,2},{7,3},{8,12},{9,13},{10,... | collective-permute-start | bytes 3145736 | tf_op jit(solution)/shard_map/ppermute | solution.py:157
  13.3 27.4 %collective-permute-start = (f32[64,4096]{1,0:T(8,128)S(1)}, f32[64,4096]{1,0:T(8,128)}, u32[]{:S(2)}, u32[]{:S(2)}) collective-permute-start(f32[64,4096]{1,0:T(8,128)S(1)} %get-tuple-element.30), channel_id=1, source_target_pairs={{0,2},{1,3},{2,0},{3,1},{4,6},{5,7},{6,4},{7,5},{8,10},{9,11},{10,... | collective-permute-start | bytes 3145736 | tf_op jit(solution)/shard_map/ppermute | solution.py:157
  15.7 4.3 %collective-permute-start.2 = (f32[2,64,64]{2,1,0:T(8,128)S(1)}, f32[2,64,64]{2,1,0:T(8,128)S(1)}, u32[]{:S(2)}, u32[]{:S(2)}) collective-permute-start(f32[2,64,64]{2,1,0:T(8,128)S(1)} %fusion.2), channel_id=1, source_target_pairs={{0,8},{8,0},{16,24},{24,16},{1,9},{9,1},{17,25},{25,17},{2,10},{10... | collective-permute-start | bytes 98312 | tf_op jit(solution)/shard_map/ppermute | solution.py:160
  20.0 9.2 %collective-permute-start.3 = (f32[2,64,64]{2,1,0:T(8,128)S(1)}, f32[2,64,64]{2,1,0:T(8,128)S(1)}, u32[]{:S(2)}, u32[]{:S(2)}) collective-permute-start(f32[2,64,64]{2,1,0:T(8,128)S(1)} %add.7), channel_id=1, source_target_pairs={{0,16},{8,24},{16,0},{24,8},{1,17},{9,25},{17,1},{25,9},{2,18},{10... | collective-permute-start | bytes 98312 | tf_op jit(solution)/shard_map/ppermute | solution.py:160
  29.2 10.6 %collective-permute-start.6 = (f32[2,64,64]{2,1,0:T(8,128)S(1)}, f32[2,64,64]{2,1,0:T(8,128)S(1)}, u32[]{:S(2)}, u32[]{:S(2)}) collective-permute-start(f32[2,64,64]{2,1,0:T(8,128)S(1)} %add.8.refs_0_), channel_id=1, source_target_pairs={{0,6},{1,7},{2,4},{3,5},{4,2},{5,3},{6,0},{7,1},{8,14},{9,15},{10,... | collective-permute-start | bytes 98312 | tf_op jit(solution)/shard_map/ppermute | solution.py:157
  29.3 10.5 %collective-permute-start.5 = (f32[2,64,64]{2,1,0:T(8,128)S(1)}, f32[2,64,64]{2,1,0:T(8,128)S(1)}, u32[]{:S(2)}, u32[]{:S(2)}) collective-permute-start(f32[2,64,64]{2,1,0:T(8,128)S(1)} %add.8.refs_0_), channel_id=1, source_target_pairs={{0,4},{1,5},{2,6},{3,7},{4,0},{5,1},{6,2},{7,3},{8,12},{9,13},{10,... | collective-permute-start | bytes 98312 | tf_op jit(solution)/shard_map/ppermute | solution.py:157
  30.9 9.8 %collective-permute-start.4 = (f32[2,64,64]{2,1,0:T(8,128)S(1)}, f32[2,64,64]{2,1,0:T(8,128)S(1)}, u32[]{:S(2)}, u32[]{:S(2)}) collective-permute-start(f32[2,64,64]{2,1,0:T(8,128)S(1)} %add.8.refs_0_), channel_id=1, source_target_pairs={{0,2},{1,3},{2,0},{3,1},{4,6},{5,7},{6,4},{7,5},{8,10},{9,11},{10,... | collective-permute-start | bytes 98312 | tf_op jit(solution)/shard_map/ppermute | solution.py:157
  40.7 26.2 %collective-permute-start.7 = (f32[64,4096]{1,0:T(8,128)S(1)}, f32[64,4096]{1,0:T(8,128)}, u32[]{:S(2)}, u32[]{:S(2)}) collective-permute-start(f32[64,4096]{1,0:T(8,128)S(1)} %get-tuple-element.29), channel_id=1, source_target_pairs={{0,2},{1,3},{2,0},{3,1},{4,6},{5,7},{6,4},{7,5},{8,10},{9,11},{10,... | collective-permute-start | bytes 3145736 | tf_op jit(solution)/shard_map/ppermute | solution.py:157
  42.2 26.2 %collective-permute-start.8 = (f32[64,4096]{1,0:T(8,128)S(1)}, f32[64,4096]{1,0:T(8,128)}, u32[]{:S(2)}, u32[]{:S(2)}) collective-permute-start(f32[64,4096]{1,0:T(8,128)S(1)} %get-tuple-element.30), channel_id=1, source_target_pairs={{0,4},{1,5},{2,6},{3,7},{4,0},{5,1},{6,2},{7,3},{8,12},{9,13},{10,... | collective-permute-start | bytes 3145736 | tf_op jit(solution)/shard_map/ppermute | solution.py:157
  43.0 45.3 %collective-permute-start.9 = (f32[64,4096]{1,0:T(8,128)}, f32[64,4096]{1,0:T(8,128)}, u32[]{:S(2)}, u32[]{:S(2)}) collective-permute-start(f32[64,4096]{1,0:T(8,128)} %collective-permute-done.refs_0_), channel_id=1, source_target_pairs={{0,4},{1,5},{2,6},{3,7},{4,0},{5,1},{6,2},{7,3},{8,12},{9,13},{10,... | collective-permute-start | bytes 3145736 | tf_op jit(solution)/shard_map/ppermute | solution.py:157
  44.2 44.1 %collective-permute-start.10 = (f32[64,4096]{1,0:T(8,128)}, f32[64,4096]{1,0:T(8,128)}, u32[]{:S(2)}, u32[]{:S(2)}) collective-permute-start(f32[64,4096]{1,0:T(8,128)} %collective-permute-done.1.refs_1_), channel_id=1, source_target_pairs={{0,2},{1,3},{2,0},{3,1},{4,6},{5,7},{6,4},{7,5},{8,10},{9,11},{10,... | collective-permute-start | bytes 3145736 | tf_op jit(solution)/shard_map/ppermute | solution.py:157
  44.8 49.3 %collective-permute-start.18 = (f32[128,4096]{1,0:T(8,128)S(1)}, f32[128,4096]{1,0:T(8,128)}, u32[]{:S(2)}, u32[]{:S(2)}) collective-permute-start(f32[128,4096]{1,0:T(8,128)S(1)} %copy-done.2), channel_id=1, source_target_pairs={{0,1},{1,0},{2,3},{3,2},{4,5},{5,4},{6,7},{7,6},{8,9},{9,8},{10,11... | collective-permute-start | bytes 6291464 | tf_op jit(solution)/shard_map/ppermute | solution.py:157
  88.3 52.5 %all-to-all-start = ((f32[8,128,768]{2,1,0:T(8,128)}), f32[8,128,768]{2,1,0:T(8,128)}, u32[]{:S(2)}, u32[]{:S(2)}) async-start(f32[8,128,768]{2,1,0:T(8,128)} %all-gather.6.cloned.1.call-done), calls=%async_computation | async-start | bytes 6291456 | tf_op jit(solution)/shard_map/all_to_all | solution.py:225
  92.8 6.3 %copy-start.5 = (s32[16]{0:T(128)S(1)}, s32[16]{0:T(128)}, u32[]{:S(2)}) copy-start(s32[16]{0:T(128)} %slots.1) | copy-start | bytes 196
  92.8 94.2 %all-gather.8.cloned.1.call-start = ((), (), s32[]{:S(2)}) async-start(), calls=%async_computation.5 | async-start | bytes 2621440 | tf_op jit(solution)/shard_map/all_gather | solution.py:173
  92.9 3.9 %collective-permute-start.16 = (f32[64,4096]{1,0:T(8,128)}, f32[64,4096]{1,0:T(8,128)S(1)}, u32[]{:S(2)}, u32[]{:S(2)}) collective-permute-start(f32[64,4096]{1,0:T(8,128)} %collective-permute-done.refs_0_), channel_id=1, source_target_pairs={{0,1},{1,0},{2,3},{3,2},{4,5},{5,4},{6,7},{7,6},{8,9},{9,8},{10,11... | collective-permute-start | bytes 3145736 | tf_op jit(solution)/shard_map/ppermute | solution.py:157
  93.3 3.4 %collective-permute-start.13 = (f32[8,64,64]{2,1,0:T(8,128)S(1)}, f32[8,64,64]{2,1,0:T(8,128)S(1)}, u32[]{:S(2)}, u32[]{:S(2)}) collective-permute-start(f32[8,64,64]{2,1,0:T(8,128)S(1)} %pad_maximum_fusion.3), channel_id=1, source_target_pairs={{0,1},{1,0},{2,3},{3,2},{4,5},{5,4},{6,7},{7,6},{8,9},{9,8},{10,11... | collective-permute-start | bytes 393224 | tf_op jit(solution)/shard_map/ppermute | solution.py:157
  93.5 26.0 %collective-permute-start.14 = (f32[64,4096]{1,0:T(8,128)}, f32[64,4096]{1,0:T(8,128)}, u32[]{:S(2)}, u32[]{:S(2)}) collective-permute-start(f32[64,4096]{1,0:T(8,128)} %collective-permute-done.8.refs_0_), channel_id=1, source_target_pairs={{0,1},{1,0},{2,3},{3,2},{4,5},{5,4},{6,7},{7,6},{8,9},{9,8},{10,11... | collective-permute-start | bytes 3145736 | tf_op jit(solution)/shard_map/ppermute | solution.py:157
  93.8 15.7 %collective-permute-start.17 = (f32[64,4096]{1,0:T(8,128)}, f32[64,4096]{1,0:T(8,128)}, u32[]{:S(2)}, u32[]{:S(2)}) collective-permute-start(f32[64,4096]{1,0:T(8,128)} %collective-permute-done.7.refs_1_), channel_id=1, source_target_pairs={{0,1},{1,0},{2,3},{3,2},{4,5},{5,4},{6,7},{7,6},{8,9},{9,8},{10,11... | collective-permute-start | bytes 3145736 | tf_op jit(solution)/shard_map/ppermute | solution.py:157
  94.0 25.5 %collective-permute-start.15 = (f32[64,4096]{1,0:T(8,128)}, f32[64,4096]{1,0:T(8,128)}, u32[]{:S(2)}, u32[]{:S(2)}) collective-permute-start(f32[64,4096]{1,0:T(8,128)} %collective-permute-done.1.refs_1_), channel_id=1, source_target_pairs={{0,1},{1,0},{2,3},{3,2},{4,5},{5,4},{6,7},{7,6},{8,9},{9,8},{10,11... | collective-permute-start | bytes 3145736 | tf_op jit(solution)/shard_map/ppermute | solution.py:157
  96.6 33.1 %collective-permute-start.11 = (f32[64,4096]{1,0:T(8,128)}, f32[64,4096]{1,0:T(8,128)}, u32[]{:S(2)}, u32[]{:S(2)}) collective-permute-start(f32[64,4096]{1,0:T(8,128)} %collective-permute-done.9.refs_0_), channel_id=1, source_target_pairs={{0,1},{1,0},{2,3},{3,2},{4,5},{5,4},{6,7},{7,6},{8,9},{9,8},{10,11... | collective-permute-start | bytes 3145736 | tf_op jit(solution)/shard_map/ppermute | solution.py:157
  96.8 1.0 copy-start.3
  97.8 32.0 %collective-permute-start.12 = (f32[64,4096]{1,0:T(8,128)}, f32[64,4096]{1,0:T(8,128)}, u32[]{:S(2)}, u32[]{:S(2)}) collective-permute-start(f32[64,4096]{1,0:T(8,128)} %collective-permute-done.10.refs_1_), channel_id=1, source_target_pairs={{0,1},{1,0},{2,3},{3,2},{4,5},{5,4},{6,7},{7,6},{8,9},{9,8},{10,11... | collective-permute-start | bytes 3145736 | tf_op jit(solution)/shard_map/ppermute | solution.py:157
  99.9 9.7 %copy-start.4 = (f32[64,4096]{1,0:T(8,128)S(1)}, f32[64,4096]{1,0:T(8,128)}, u32[]{:S(2)}) copy-start(f32[64,4096]{1,0:T(8,128)} %copy-done.3) | copy-start | bytes 3145732
  140.8 46.2 %all-to-all-start.2 = ((f32[8,128,768]{2,1,0:T(8,128)}), f32[8,128,768]{2,1,0:T(8,128)S(1)}, u32[]{:S(2)}, u32[]{:S(2)}) async-start(f32[8,128,768]{2,1,0:T(8,128)} %all-gather.4.cloned.1.call-done), calls=%async_computation.2 | async-start | bytes 6291456 | tf_op jit(solution)/shard_map/all_to_all | solution.py:225
  187.0 31.0 %all-to-all-start.1 = ((f32[8,128,512]{2,1,0:T(8,128)}), f32[8,128,512]{2,1,0:T(8,128)}, u32[]{:S(2)}, u32[]{:S(2)}) async-start(f32[8,128,512]{2,1,0:T(8,128)} %all-gather.8.cloned.1.call-done), calls=%async_computation.1 | async-start | bytes 4194304 | tf_op jit(solution)/shard_map/all_to_all | solution.py:225
  218.0 19.6 %copy-start.1 = (f32[2,128,512]{2,1,0:T(8,128)S(1)}, f32[2,128,512]{2,1,0:T(8,128)}, u32[]{:S(2)}) copy-start(f32[2,128,512]{2,1,0:T(8,128)} %param.8) | copy-start | bytes 1572868
Sparse Core Ops, SparseCore 0:
  9.2 67.5 all-gather.5
  78.3 62.4 all-gather.3
  142.4 44.5 all-gather.7

commit v6 on v3

--- a/solution.py
+++ b/solution.py
@@ -7,8 +7,7 @@
 from jax.experimental.pallas import tpu as pltpu
 from jax.sharding import PartitionSpec as P
 
-GATHERS = ((0, 3), (3, 3), (6, 2))
-CHUNKS = ((0, 0, 3), (1, 3, 3), (2, 6, 2))
+CHUNKS = ((0, 2), (3, 3), (6, 2), (2, 1))
 HIGHEST = lax.Precision.HIGHEST
 SCALE_VMEM = 48 * 1024 * 1024
 UPDATE_VMEM = 48 * 1024 * 1024
@@ -155,13 +154,17 @@
 
     after = lax.optimization_barrier
 
-    everywhere = [lax.all_gather(column_chunk(*g), "row", axis=0, tiled=True) for g in GATHERS]
+    everywhere = [lax.all_gather(column_chunk(*g), "row", axis=0, tiled=True) for g in CHUNKS]
     cut = rows // 2
     own = [panel_factors[:cut], panel_factors[cut:]]
-    gathered = [[own, None]] + [[None, None] for _ in range(lines - 1)]
+    gathered = [[own, None]] + [[[None, None], None] for _ in range(lines - 1)]
     single = [1 << i for i in range(lines.bit_length() - 1)]
+
+    def early(s):
+        return 0 if s == 1 else 1
+
     for s in single:
-        gathered[s][0] = [across(x, 2 * s) for x in own]
+        gathered[s][0][early(s)] = across(own[early(s)], 2 * s)
     solved = lax.dot_general(
         vectors_t, inverse_lower_factors, (((2,), (2,)), ((0,), (0,))), precision=HIGHEST
     )
@@ -173,9 +176,10 @@
 
     near = [cores] + [across(cores, 2 * s) for s in range(1, lines)]
 
-    arrived, near = after(([gathered[s][0] for s in single], near))
+    arrived, near, own = after(([gathered[s][0][early(s)] for s in single], near, own))
     for s, x in zip(single, arrived):
-        gathered[s][0] = x
+        gathered[s][0][early(s)] = x
+        gathered[s][0][1 - early(s)] = across(own[1 - early(s)], 2 * s)
     several = sorted((s for s in range(1, lines) if s not in single), key=lambda s: bin(s).count("1"))
     for s in several:
         low, high = s & -s, 1 << (s.bit_length() - 1)
@@ -183,6 +187,12 @@
             across(gathered[s ^ high][0][0], 2 * high),
             across(gathered[s ^ low][0][1], 2 * low),
         ]
+
+    arrived, near, everywhere[0] = after(
+        ([gathered[s][0] for s in range(1, lines)], near, everywhere[0])
+    )
+    for s, x in zip(range(1, lines), arrived):
+        gathered[s][0] = x
     far = across(jnp.concatenate(near), 1)
     blocks = diagonal_blocks(col.astype(jnp.int32).reshape(1), slot_of_panel, near, far)
 
@@ -195,35 +205,25 @@
             parts = [(x, half) for x in whole for half in range(2)]
         return scale_into(place, parts, blocks, s, left, depth)
 
+    def exchange(number):
+        chunk = lax.all_to_all(everywhere[number], "col", split_axis=0, concat_axis=0, tiled=True)
+        return chunk.reshape(depth, -1)
+
+    chunks = [exchange(0)]
+
     left = None
-    for s in [0] + single:
+    for s in range(lines - 1):
         left = scale(s, left)
-
-    def exchange(number):
-        source, first, count = CHUNKS[number]
-        sent = everywhere[source]
-        if GATHERS[source][1] != count:
-            at = (first - GATHERS[source][0]) * eighth
-            sent = sent[:, :, at : at + count * eighth]
-        chunk = lax.all_to_all(sent, "col", split_axis=0, concat_axis=0, tiled=True)
-        return chunk.reshape(depth, -1)
-
-    arrived, left, everywhere[0] = after(([gathered[s][0] for s in several], left, everywhere[0]))
-    chunks = [exchange(0)]
-    for s, x in zip(several, arrived):
-        gathered[s][0] = x
-    for s in several:
-        left = scale(s, left)
+    everywhere[1], left = after((everywhere[1], left))
+    chunks.append(exchange(1))
+    left = scale(lines - 1, left)
 
     updated = None
-    for number, (_, first, _) in enumerate(CHUNKS):
-        if number + 1 < len(CHUNKS):
-            source = CHUNKS[number + 1][0]
-            if updated is None:
-                everywhere[source], left = after((everywhere[source], left))
-            else:
-                everywhere[source], updated = after((everywhere[source], updated))
-            chunks.append(exchange(number + 1))
+    for number, (first, _) in enumerate(CHUNKS):
+        later = number + 1
+        if 1 < later < len(CHUNKS):
+            everywhere[later], updated = after((everywhere[later], updated))
+            chunks.append(exchange(later))
         updated = update_chunk(first * eighth, trailing, left, chunks[number], updated)
     return updated
 

time: 246 us -> 247 us (level)
  waiting for transfers between devices: 92.7 us -> 80.9 us
  Pallas kernels: 98.3 us -> 105 us
  starting transfers between devices: 31.1 us -> 35.5 us
    all_gather x3 -> x4, waiting for transfers between devices: 28.4 us -> 16.2 us  [body(): lax.all_gather(column_chunk(*g), 'row', axis=0, tiled=True)]
    all_to_all x3 -> x4, waiting for transfers between devices: 8.56 us -> 0.01 us  [exchange(): lax.all_to_all(everywhere[number], 'col', split_axis=0, concat_axis=0, ti...]
    pallas_call x3 -> x4, Pallas kernels: 72.4 us -> 79.4 us  [update_chunk(): pl.pallas_call(update_kernel, grid=(height // tile,), in_specs=[here, sid...]
    ppermute x17, waiting for transfers between devices: 50.2 us -> 55.1 us  [across(): return lax.ppermute(x, 'col', [(i, i ^ bits) for i in range(columns)])]
    ppermute x2, waiting for transfers between devices: 5.42 us -> 9.62 us  [along(): return lax.ppermute(x, 'row', moves)]
    all_to_all x3 -> x4, starting transfers between devices: 12.7 us -> 16.8 us  [exchange(): lax.all_to_all(everywhere[number], 'col', split_axis=0, concat_axis=0, ti...]
    unnamed x16 -> x34, local copies, waits for them, and re-layouts: 2.21 us -> 4.74 us
  transfers between devices with their start and end apart: 25 -> 27, of which waited for: 16 -> 14; matrix products, arithmetic and copies ran while one was open for 2% -> 2% of each run, Pallas kernels for 32% -> 38%
where the time goes in v6:
time: 247 us; the launch traced here: 246 us
  Pallas kernels  105 us (43%)
  waiting for transfers between devices  80.9 us (33%)
  starting transfers between devices  35.5 us (14%)
  between operations  13.4 us (5%)
  local copies, waits for them, and re-layouts  7.51 us (3%)
  other arithmetic  3.4 us (1%)
    pallas_call x4, Pallas kernels, update_chunk(): pl.pallas_call(update_kernel, grid=(height // tile,), in_specs=[here, sid...  79.4 us
    ppermute x17, waiting for transfers between devices, across(): return lax.ppermute(x, 'col', [(i, i ^ bits) for i in range(columns)])  55.1 us
    pallas_call x4, Pallas kernels, scale_into(): pl.pallas_call(scale_kernel, grid_spec=pltpu.PrefetchScalarGridSpec(num_s...  24.6 us
    all_to_all x4, starting transfers between devices, exchange(): lax.all_to_all(everywhere[number], 'col', split_axis=0, concat_axis=0, ti...  16.8 us
    all_gather x4, waiting for transfers between devices, body(): lax.all_gather(column_chunk(*g), 'row', axis=0, tiled=True)  16.2 us
    ppermute x17, starting transfers between devices, across(): return lax.ppermute(x, 'col', [(i, i ^ bits) for i in range(columns)])  14.1 us
    ppermute x2, waiting for transfers between devices, along(): return lax.ppermute(x, 'row', moves)  9.62 us
  transfers between devices with their start and end apart: 27, of which 14 were waited for; matrix products, arithmetic and copies ran while one was open for 2% of the time, Pallas kernels for 38%

profile of v6, /device:TPU:0, one launch (start us, length us, event | category | flops | bytes accessed | tf_op | source)
XLA Modules:
  0.0 246.4 jit_solution(16197327109056552334)
XLA Ops:
  6.5 1.4 slice_bitcast_fusion.3
  8.0 0.8 pad_maximum_fusion.1
  8.9 1.2 slice_bitcast_fusion.1
  10.1 1.0 pad_maximum_fusion
  11.2 3.0 %collective-permute-start = (f32[64,4096]{1,0:T(8,128)S(1)}, f32[64,4096]{1,0:T(8,128)S(1)}, u32[]{:S(2)}, u32[]{:S(2)}) collective-permute-start(f32[64,4096]{1,0:T(8,128)S(1)} %get-tuple-element.41), channel_id=1, source_target_pairs={{0,2},{1,3},{2,0},{3,1},{4,6},{5,7},{6,4},{7,5},{8,10},{9,11},{10,... | collective-permute-start | bytes 3145736 | tf_op jit(solution)/shard_map/ppermute | solution.py:141
  14.2 1.5 collective-permute-start.1
  15.8 0.7 fusion.1
  16.7 1.6 collective-permute-start.2
  18.3 2.7 %collective-permute-done.2 = f32[2,64,64]{2,1,0:T(8,128)S(1)} collective-permute-done((f32[2,64,64]{2,1,0:T(8,128)S(1)}, f32[2,64,64]{2,1,0:T(8,128)S(1)}, u32[]{:S(2)}, u32[]{:S(2)}) %collective-permute-start.2) | collective-permute-done | bytes 32800 | tf_op jit(solution)/shard_map/ppermute | solution.py:144
  21.0 2.7 %collective-permute-start.3 = (f32[2,64,64]{2,1,0:T(8,128)S(1)}, f32[2,64,64]{2,1,0:T(8,128)S(1)}, u32[]{:S(2)}, u32[]{:S(2)}) collective-permute-start(f32[2,64,64]{2,1,0:T(8,128)S(1)} %add.7), channel_id=1, source_target_pairs={{0,16},{8,24},{16,0},{24,8},{1,17},{9,25},{17,1},{25,9},{2,18},{10... | collective-permute-start | bytes 98312 | tf_op jit(solution)/shard_map/ppermute | solution.py:144
  23.7 6.9 %collective-permute-done.3 = f32[2,64,64]{2,1,0:T(8,128)S(1)} collective-permute-done((f32[2,64,64]{2,1,0:T(8,128)S(1)}, f32[2,64,64]{2,1,0:T(8,128)S(1)}, u32[]{:S(2)}, u32[]{:S(2)}) %collective-permute-start.3) | collective-permute-done | bytes 32800 | tf_op jit(solution)/shard_map/ppermute | solution.py:144
  30.6 0.4 collective-permute-start.4
  31.1 3.1 %collective-permute-start.6 = (f32[2,64,64]{2,1,0:T(8,128)S(1)}, f32[2,64,64]{2,1,0:T(8,128)S(1)}, u32[]{:S(2)}, u32[]{:S(2)}) collective-permute-start(f32[2,64,64]{2,1,0:T(8,128)S(1)} %add.8.refs_0_), channel_id=1, source_target_pairs={{0,6},{1,7},{2,4},{3,5},{4,2},{5,3},{6,0},{7,1},{8,14},{9,15},{10,... | collective-permute-start | bytes 98312 | tf_op jit(solution)/shard_map/ppermute | solution.py:141
  34.2 5.3 %collective-permute-done.4.refs_1_ = f32[2,64,64]{2,1,0:T(8,128)S(1)} collective-permute-done((f32[2,64,64]{2,1,0:T(8,128)S(1)}, f32[2,64,64]{2,1,0:T(8,128)S(1)}, u32[]{:S(2)}, u32[]{:S(2)}) %collective-permute-start.4) | collective-permute-done | bytes 32800 | tf_op jit(solution)/shard_map/ppermute | solution.py:141
  39.5 2.2 collective-permute-done.5.refs_2_
  41.7 1.3 collective-permute-start.10
  43.0 0.8 collective-permute-start.9
  43.8 1.5 collective-permute-start.7
  45.3 0.5 collective-permute-start.8
  45.8 22.0 %collective-permute-done.10.refs_1_ = f32[64,4096]{1,0:T(8,128)S(1)} collective-permute-done((f32[64,4096]{1,0:T(8,128)S(1)}, f32[64,4096]{1,0:T(8,128)S(1)}, u32[]{:S(2)}, u32[]{:S(2)}) %collective-permute-start.10) | collective-permute-done | bytes 1048608 | tf_op jit(solution)/shard_map/ppermute | solution.py:141
  67.9 1.2 collective-permute-done.9.refs_0_
  69.1 19.0 %collective-permute-done.7.refs_1_ = f32[64,4096]{1,0:T(8,128)S(1)} collective-permute-done((f32[64,4096]{1,0:T(8,128)S(1)}, f32[64,4096]{1,0:T(8,128)S(1)}, u32[]{:S(2)}, u32[]{:S(2)}) %collective-permute-start.7) | collective-permute-done | bytes 1048608 | tf_op jit(solution)/shard_map/ppermute | solution.py:141
  88.1 1.0 copy-done.13
  89.4 4.4 %all-to-all-start.1 = ((f32[8,128,512]{2,1,0:T(8,128)}), f32[8,128,512]{2,1,0:T(8,128)}, u32[]{:S(2)}, u32[]{:S(2)}) async-start(f32[8,128,512]{2,1,0:T(8,128)} %all-gather.5.cloned.1.call-done), calls=%async_computation.1 | async-start | bytes 4194304 | tf_op jit(solution)/shard_map/all_to_all | solution.py:209
  93.9 0.4 collective-permute-start.13
  95.0 0.6 collective-permute-done.13.refs_4_
  95.8 0.8 pad_maximum_fusion.2
  96.7 0.8 shard_map.55.refs_4_
  97.5 6.4 %shard_map.56 = (bf16[4096,1024]{1,0:T(8,128)(2,1)}, bf16[4096,1024]{1,0:T(8,128)(2,1)}) custom-call(s32[1]{0:T(128)} %bitcast.8.place, f32[128,4096]{1,0:T(8,128)S(1)} %copy-done.2, f32[128,4096]{1,0:T(8,128)S(1)} %copy-done.2, f32[128,4096]{1,0:T(8,128)} %collective-permute-done.18.refs_2_.refs_3_, f32[128,4096]{1,0:T(8,128)} %collective-permute-done.18.refs_2_.refs_3_, ...), custom_call_target="tpu_custom_call" | custom-call | flops 1 | bytes 1 | tf_op jit(solution)/shard_map/pallas_call | solution.py:42
  103.9 6.1 %shard_map.57 = (bf16[4096,1024]{1,0:T(8,128)(2,1)}, bf16[4096,1024]{1,0:T(8,128)(2,1)}) custom-call(s32[1]{0:T(128)} %bitcast.7.place, f32[64,4096]{1,0:T(8,128)S(1)} %copy-done.8, f32[64,4096]{1,0:T(8,128)S(1)} %copy-done.14, f32[64,4096]{1,0:T(8,128)} %collective-permute-done.16.refs_2_, ...), custom_call_target="tpu_custom_call", output_to_operand_aliasing={{0}: (6, {}), {1}: (7, {})} | custom-call | flops 1 | bytes 1 | tf_op jit(solution)/shard_map/pallas_call | solution.py:42
  110.0 6.1 %shard_map.58 = (bf16[4096,1024]{1,0:T(8,128)(2,1)}, bf16[4096,1024]{1,0:T(8,128)(2,1)}) custom-call(s32[1]{0:T(128)} %bitcast.6.place, f32[64,4096]{1,0:T(8,128)} %collective-permute-done.8.refs_0_, f32[64,4096]{1,0:T(8,128)S(1)} %copy-done.6, f32[64,4096]{1,0:T(8,128)} %collective-permute-done.14.refs_2_, ...), custom_call_target="tpu_custom_call", output_to_operand_aliasing={{0}: (6, {}), {1}: (7, {})} | custom-call | flops 1 | bytes 1 | tf_op jit(solution)/shard_map/pallas_call | solution.py:42
  116.1 8.3 %all-gather.7.cloned.1.call-done = f32[8,128,768]{2,1,0:T(8,128)} async-done(((f32[2,128,768]{2,1,0:T(8,128)}), f32[8,128,768]{2,1,0:T(8,128)}) %all-gather.7.cloned.1.call-update) | async-done | bytes 3145744 | tf_op jit(solution)/shard_map/all_gather | solution.py:157
  124.4 4.4 %all-to-all-start = ((f32[8,128,768]{2,1,0:T(8,128)}), f32[8,128,768]{2,1,0:T(8,128)}, u32[]{:S(2)}, u32[]{:S(2)}) async-start(f32[8,128,768]{2,1,0:T(8,128)} %all-gather.7.cloned.1.call-done), calls=%async_computation | async-start | bytes 6291456 | tf_op jit(solution)/shard_map/all_to_all | solution.py:209
  129.5 2.9 %collective-permute-done.11.refs_2_ = f32[64,4096]{1,0:T(8,128)} collective-permute-done((f32[64,4096]{1,0:T(8,128)}, f32[64,4096]{1,0:T(8,128)}, u32[]{:S(2)}, u32[]{:S(2)}) %collective-permute-start.11) | collective-permute-done | bytes 1048608 | tf_op jit(solution)/shard_map/ppermute | solution.py:141
  132.3 1.5 collective-permute-done.12.refs_3_
  133.8 1.2 copy-done.4
  135.1 1.2 copy-done.10
  136.3 1.2 copy-done.12
  137.5 6.0 %shard_map.59 = (bf16[4096,1024]{1,0:T(8,128)(2,1)}, bf16[4096,1024]{1,0:T(8,128)(2,1)}) custom-call(s32[1]{0:T(128)} %bitcast.place, f32[64,4096]{1,0:T(8,128)S(1)} %copy-done.12, f32[64,4096]{1,0:T(8,128)S(1)} %copy-done.10, f32[64,4096]{1,0:T(8,128)} %collective-permute-done.11.refs_2_, ...), custom_call_target="tpu_custom_call", output_to_operand_aliasing={{0}: (6, {}), {1}: (7, {})} | custom-call | flops 1 | bytes 1 | tf_op jit(solution)/shard_map/pallas_call | solution.py:42
  143.5 20.3 %shard_map.60.refs_0_ = f32[4096,2048]{1,0:T(8,128)} custom-call(f32[4096,2048]{1,0:T(8,128)} %trailing.7, bf16[4096,1024]{1,0:T(8,128)(2,1)} %get-tuple-element.65.hi, bf16[4096,1024]{1,0:T(8,128)(2,1)} %get-tuple-element.66.lo, f32[1024,512]{1,0:T(8,128)} %bitcast.14.right), custom_call_target="tpu_custom_call" | custom-call | flops 1 | bytes 1 | tf_op jit(solution)/shard_map/pallas_call | solution.py:117
  163.8 6.8 %all-gather.11.cloned.1.call-done = f32[8,128,512]{2,1,0:T(8,128)} async-done(((f32[2,128,512]{2,1,0:T(8,128)}), f32[8,128,512]{2,1,0:T(8,128)}) %all-gather.11.cloned.1.call-update) | async-done | bytes 2097168 | tf_op jit(solution)/shard_map/all_gather | solution.py:157
  170.6 4.4 %all-to-all-start.3 = ((f32[8,128,512]{2,1,0:T(8,128)}), f32[8,128,512]{2,1,0:T(8,128)}, u32[]{:S(2)}, u32[]{:S(2)}) async-start(f32[8,128,512]{2,1,0:T(8,128)} %all-gather.11.cloned.1.call-done), calls=%async_computation.3 | async-start | bytes 4194304 | tf_op jit(solution)/shard_map/all_to_all | solution.py:209
  175.3 0.7 pad_maximum_fusion.4
  176.0 27.2 %shard_map.61.refs_0_ = f32[4096,2048]{1,0:T(8,128)} custom-call(f32[4096,2048]{1,0:T(8,128)} %trailing.7, bf16[4096,1024]{1,0:T(8,128)(2,1)} %get-tuple-element.65.hi, bf16[4096,1024]{1,0:T(8,128)(2,1)} %get-tuple-element.66.lo, f32[1024,768]{1,0:T(8,128)} %bitcast.11.right, f32[4096,2048]{1,0:T(8,128)} %shard_map.60.refs_0_), custom_call_target="tpu_custom_call", output_to_operand_aliasing={{}: (4, {})} | custom-call | flops 1 | bytes 1 | tf_op jit(solution)/shard_map/pallas_call | solution.py:117
  203.2 1.0 all-gather.9.cloned.1.call-done
  204.2 3.7 %all-to-all-start.2 = ((f32[8,128,256]{2,1,0:T(8,128)}), f32[8,128,256]{2,1,0:T(8,128)S(1)}, u32[]{:S(2)}, u32[]{:S(2)}) async-start(f32[8,128,256]{2,1,0:T(8,128)} %all-gather.9.cloned.1.call-done), calls=%async_computation.2 | async-start | bytes 2097152 | tf_op jit(solution)/shard_map/all_to_all | solution.py:209
  207.9 19.6 %shard_map.62.refs_0_ = f32[4096,2048]{1,0:T(8,128)} custom-call(f32[4096,2048]{1,0:T(8,128)} %trailing.7, bf16[4096,1024]{1,0:T(8,128)(2,1)} %get-tuple-element.65.hi, bf16[4096,1024]{1,0:T(8,128)(2,1)} %get-tuple-element.66.lo, f32[1024,512]{1,0:T(8,128)} %bitcast.16.right, f32[4096,2048]{1,0:T(8,128)} %shard_map.61.refs_0_), custom_call_target="tpu_custom_call", output_to_operand_aliasing={{}: (4, {})} | custom-call | flops 1 | bytes 1 | tf_op jit(solution)/shard_map/pallas_call | solution.py:117
  227.5 12.4 %shard_map.63 = f32[4096,2048]{1,0:T(8,128)} custom-call(f32[4096,2048]{1,0:T(8,128)} %trailing.7, bf16[4096,1024]{1,0:T(8,128)(2,1)} %get-tuple-element.65.hi, bf16[4096,1024]{1,0:T(8,128)(2,1)} %get-tuple-element.66.lo, f32[1024,256]{1,0:T(8,128)S(1)} %bitcast.29, f32[4096,2048]{1,0:T(8,128)} %shard_map.62.refs_0_), custom_call_target="tpu_custom_call", output_to_operand_aliasing={{}: (4, {})} | custom-call | flops 1 | bytes 1 | tf_op jit(solution)/shard_map/pallas_call | solution.py:117
  (66 shorter events, 2.7 us)
Async XLA Ops:
  6.5 9.2 %copy-start = (f32[2,128,512]{2,1,0:T(8,128)S(1)}, f32[2,128,512]{2,1,0:T(8,128)}, u32[]{:S(2)}) copy-start(f32[2,128,512]{2,1,0:T(8,128)} %param.8) | copy-start | bytes 1572868
  6.5 4.6 %copy-start.2 = (f32[128,4096]{1,0:T(8,128)S(1)}, f32[128,4096]{1,0:T(8,128)}, u32[]{:S(2)}) copy-start(f32[128,4096]{1,0:T(8,128)} %refs_1_.1) | copy-start | bytes 6291460
  6.5 9.2 %copy-start.16 = (f32[2,64,512]{2,1,0:T(8,128)S(1)}, f32[2,64,512]{2,1,0:T(8,128)}, u32[]{:S(2)}) copy-start(f32[2,64,512]{2,1,0:T(8,128)} %param.7) | copy-start | bytes 786436
  6.5 82.9 %all-gather.5.cloned.1.call-start = ((), (), s32[]{:S(2)}) async-start(), calls=%async_computation.4 | async-start | bytes 2621440 | tf_op jit(solution)/shard_map/all_gather | solution.py:157
  8.8 87.8 %copy-start.15 = (s32[16]{0:T(128)S(1)}, s32[16]{0:T(128)}, u32[]{:S(2)}) copy-start(s32[16]{0:T(128)} %slots.1) | copy-start | bytes 196
  8.9 115.6 %all-gather.7.cloned.1.call-start = ((), (), s32[]{:S(2)}) async-start(), calls=%async_computation.5 | async-start | bytes 3932160 | tf_op jit(solution)/shard_map/all_gather | solution.py:157
  11.2 30.4 %collective-permute-start = (f32[64,4096]{1,0:T(8,128)S(1)}, f32[64,4096]{1,0:T(8,128)S(1)}, u32[]{:S(2)}, u32[]{:S(2)}) collective-permute-start(f32[64,4096]{1,0:T(8,128)S(1)} %get-tuple-element.41), channel_id=1, source_target_pairs={{0,2},{1,3},{2,0},{3,1},{4,6},{5,7},{6,4},{7,5},{8,10},{9,11},{10,... | collective-permute-start | bytes 3145736 | tf_op jit(solution)/shard_map/ppermute | solution.py:141
  14.2 27.4 %collective-permute-start.1 = (f32[64,4096]{1,0:T(8,128)S(1)}, f32[64,4096]{1,0:T(8,128)S(1)}, u32[]{:S(2)}, u32[]{:S(2)}) collective-permute-start(f32[64,4096]{1,0:T(8,128)S(1)} %get-tuple-element.40), channel_id=1, source_target_pairs={{0,4},{1,5},{2,6},{3,7},{4,0},{5,1},{6,2},{7,3},{8,12},{9,13},{10,... | collective-permute-start | bytes 3145736 | tf_op jit(solution)/shard_map/ppermute | solution.py:141
  16.7 4.3 %collective-permute-start.2 = (f32[2,64,64]{2,1,0:T(8,128)S(1)}, f32[2,64,64]{2,1,0:T(8,128)S(1)}, u32[]{:S(2)}, u32[]{:S(2)}) collective-permute-start(f32[2,64,64]{2,1,0:T(8,128)S(1)} %fusion.2), channel_id=1, source_target_pairs={{0,8},{8,0},{16,24},{24,16},{1,9},{9,1},{17,25},{25,17},{2,10},{10... | collective-permute-start | bytes 98312 | tf_op jit(solution)/shard_map/ppermute | solution.py:144
  21.0 9.6 %collective-permute-start.3 = (f32[2,64,64]{2,1,0:T(8,128)S(1)}, f32[2,64,64]{2,1,0:T(8,128)S(1)}, u32[]{:S(2)}, u32[]{:S(2)}) collective-permute-start(f32[2,64,64]{2,1,0:T(8,128)S(1)} %add.7), channel_id=1, source_target_pairs={{0,16},{8,24},{16,0},{24,8},{1,17},{9,25},{17,1},{25,9},{2,18},{10... | collective-permute-start | bytes 98312 | tf_op jit(solution)/shard_map/ppermute | solution.py:144
  30.6 8.9 %collective-permute-start.4 = (f32[2,64,64]{2,1,0:T(8,128)S(1)}, f32[2,64,64]{2,1,0:T(8,128)S(1)}, u32[]{:S(2)}, u32[]{:S(2)}) collective-permute-start(f32[2,64,64]{2,1,0:T(8,128)S(1)} %add.8.refs_0_), channel_id=1, source_target_pairs={{0,2},{1,3},{2,0},{3,1},{4,6},{5,7},{6,4},{7,5},{8,10},{9,11},{10,... | collective-permute-start | bytes 98312 | tf_op jit(solution)/shard_map/ppermute | solution.py:141
  31.0 10.6 %collective-permute-start.5 = (f32[2,64,64]{2,1,0:T(8,128)S(1)}, f32[2,64,64]{2,1,0:T(8,128)S(1)}, u32[]{:S(2)}, u32[]{:S(2)}) collective-permute-start(f32[2,64,64]{2,1,0:T(8,128)S(1)} %add.8.refs_0_), channel_id=1, source_target_pairs={{0,4},{1,5},{2,6},{3,7},{4,0},{5,1},{6,2},{7,3},{8,12},{9,13},{10,... | collective-permute-start | bytes 98312 | tf_op jit(solution)/shard_map/ppermute | solution.py:141
  31.1 10.6 %collective-permute-start.6 = (f32[2,64,64]{2,1,0:T(8,128)S(1)}, f32[2,64,64]{2,1,0:T(8,128)S(1)}, u32[]{:S(2)}, u32[]{:S(2)}) collective-permute-start(f32[2,64,64]{2,1,0:T(8,128)S(1)} %add.8.refs_0_), channel_id=1, source_target_pairs={{0,6},{1,7},{2,4},{3,5},{4,2},{5,3},{6,0},{7,1},{8,14},{9,15},{10,... | collective-permute-start | bytes 98312 | tf_op jit(solution)/shard_map/ppermute | solution.py:141
  41.7 26.2 %copy-start.7 = (f32[64,4096]{1,0:T(8,128)}, f32[64,4096]{1,0:T(8,128)S(1)}, u32[]{:S(2)}) copy-start(f32[64,4096]{1,0:T(8,128)S(1)} %collective-permute-done.refs_0_) | copy-start | bytes 3145732
  41.7 3.6 %copy-start.5 = (f32[64,4096]{1,0:T(8,128)}, f32[64,4096]{1,0:T(8,128)S(1)}, u32[]{:S(2)}) copy-start(f32[64,4096]{1,0:T(8,128)S(1)} %collective-permute-done.1.refs_1_) | copy-start | bytes 3145732
  41.7 26.2 %collective-permute-start.10 = (f32[64,4096]{1,0:T(8,128)S(1)}, f32[64,4096]{1,0:T(8,128)S(1)}, u32[]{:S(2)}, u32[]{:S(2)}) collective-permute-start(f32[64,4096]{1,0:T(8,128)S(1)} %collective-permute-done.1.refs_1_), channel_id=1, source_target_pairs={{0,2},{1,3},{2,0},{3,1},{4,6},{5,7},{6,4},{7,5},{8,10},{9,11},{10,... | collective-permute-start | bytes 3145736 | tf_op jit(solution)/shard_map/ppermute | solution.py:141
  43.0 26.1 %collective-permute-start.9 = (f32[64,4096]{1,0:T(8,128)S(1)}, f32[64,4096]{1,0:T(8,128)S(1)}, u32[]{:S(2)}, u32[]{:S(2)}) collective-permute-start(f32[64,4096]{1,0:T(8,128)S(1)} %collective-permute-done.refs_0_), channel_id=1, source_target_pairs={{0,4},{1,5},{2,6},{3,7},{4,0},{5,1},{6,2},{7,3},{8,12},{9,13},{10,... | collective-permute-start | bytes 3145736 | tf_op jit(solution)/shard_map/ppermute | solution.py:141
  43.8 44.3 %collective-permute-start.7 = (f32[64,4096]{1,0:T(8,128)S(1)}, f32[64,4096]{1,0:T(8,128)S(1)}, u32[]{:S(2)}, u32[]{:S(2)}) collective-permute-start(f32[64,4096]{1,0:T(8,128)S(1)} %get-tuple-element.40), channel_id=1, source_target_pairs={{0,2},{1,3},{2,0},{3,1},{4,6},{5,7},{6,4},{7,5},{8,10},{9,11},{10,... | collective-permute-start | bytes 3145736 | tf_op jit(solution)/shard_map/ppermute | solution.py:141
  45.3 44.1 %collective-permute-start.8 = (f32[64,4096]{1,0:T(8,128)S(1)}, f32[64,4096]{1,0:T(8,128)}, u32[]{:S(2)}, u32[]{:S(2)}) collective-permute-start(f32[64,4096]{1,0:T(8,128)S(1)} %get-tuple-element.41), channel_id=1, source_target_pairs={{0,4},{1,5},{2,6},{3,7},{4,0},{5,1},{6,2},{7,3},{8,12},{9,13},{10,... | collective-permute-start | bytes 3145736 | tf_op jit(solution)/shard_map/ppermute | solution.py:141
  45.8 51.7 %collective-permute-start.18 = (f32[128,4096]{1,0:T(8,128)S(1)}, f32[128,4096]{1,0:T(8,128)}, u32[]{:S(2)}, u32[]{:S(2)}) collective-permute-start(f32[128,4096]{1,0:T(8,128)S(1)} %copy-done.2), channel_id=1, source_target_pairs={{0,1},{1,0},{2,3},{3,2},{4,5},{5,4},{6,7},{7,6},{8,9},{9,8},{10,11... | collective-permute-start | bytes 6291464 | tf_op jit(solution)/shard_map/ppermute | solution.py:141
  67.9 1.2 copy-start.9
  69.1 19.0 %copy-start.11 = (f32[64,4096]{1,0:T(8,128)}, f32[64,4096]{1,0:T(8,128)S(1)}, u32[]{:S(2)}) copy-start(f32[64,4096]{1,0:T(8,128)S(1)} %collective-permute-done.9.refs_0_) | copy-start | bytes 3145732
  88.1 1.0 copy-start.13
  89.4 35.0 %all-to-all-start.1 = ((f32[8,128,512]{2,1,0:T(8,128)}), f32[8,128,512]{2,1,0:T(8,128)}, u32[]{:S(2)}, u32[]{:S(2)}) async-start(f32[8,128,512]{2,1,0:T(8,128)} %all-gather.5.cloned.1.call-done), calls=%async_computation.1 | async-start | bytes 4194304 | tf_op jit(solution)/shard_map/all_to_all | solution.py:209
  93.8 76.8 %all-gather.11.cloned.1.call-start = ((), (), s32[]{:S(2)}) async-start(), calls=%async_computation.7 | async-start | bytes 2621440 | tf_op jit(solution)/shard_map/all_gather | solution.py:157
  93.9 1.7 collective-permute-start.13
  94.3 9.6 %collective-permute-start.16 = (f32[64,4096]{1,0:T(8,128)}, f32[64,4096]{1,0:T(8,128)}, u32[]{:S(2)}, u32[]{:S(2)}) collective-permute-start(f32[64,4096]{1,0:T(8,128)} %copy-done.7), channel_id=1, source_target_pairs={{0,1},{1,0},{2,3},{3,2},{4,5},{5,4},{6,7},{7,6},{8,9},{9,8},{10,11... | collective-permute-start | bytes 3145736 | tf_op jit(solution)/shard_map/ppermute | solution.py:141
  94.5 9.4 %collective-permute-start.17 = (f32[64,4096]{1,0:T(8,128)}, f32[64,4096]{1,0:T(8,128)}, u32[]{:S(2)}, u32[]{:S(2)}) collective-permute-start(f32[64,4096]{1,0:T(8,128)} %copy-done.13), channel_id=1, source_target_pairs={{0,1},{1,0},{2,3},{3,2},{4,5},{5,4},{6,7},{7,6},{8,9},{9,8},{10,11... | collective-permute-start | bytes 3145736 | tf_op jit(solution)/shard_map/ppermute | solution.py:141
  94.8 15.2 %collective-permute-start.14 = (f32[64,4096]{1,0:T(8,128)}, f32[64,4096]{1,0:T(8,128)}, u32[]{:S(2)}, u32[]{:S(2)}) collective-permute-start(f32[64,4096]{1,0:T(8,128)} %collective-permute-done.8.refs_0_), channel_id=1, source_target_pairs={{0,1},{1,0},{2,3},{3,2},{4,5},{5,4},{6,7},{7,6},{8,9},{9,8},{10,11... | collective-permute-start | bytes 3145736 | tf_op jit(solution)/shard_map/ppermute | solution.py:141
  95.6 14.4 %collective-permute-start.15 = (f32[64,4096]{1,0:T(8,128)}, f32[64,4096]{1,0:T(8,128)}, u32[]{:S(2)}, u32[]{:S(2)}) collective-permute-start(f32[64,4096]{1,0:T(8,128)} %copy-done.5), channel_id=1, source_target_pairs={{0,1},{1,0},{2,3},{3,2},{4,5},{5,4},{6,7},{7,6},{8,9},{9,8},{10,11... | collective-permute-start | bytes 3145736 | tf_op jit(solution)/shard_map/ppermute | solution.py:141
  96.7 7.2 %copy-start.8 = (f32[64,4096]{1,0:T(8,128)S(1)}, f32[64,4096]{1,0:T(8,128)}, u32[]{:S(2)}) copy-start(f32[64,4096]{1,0:T(8,128)} %copy-done.7) | copy-start | bytes 3145732
  96.7 7.2 %copy-start.14 = (f32[64,4096]{1,0:T(8,128)S(1)}, f32[64,4096]{1,0:T(8,128)}, u32[]{:S(2)}) copy-start(f32[64,4096]{1,0:T(8,128)} %copy-done.13) | copy-start | bytes 3145732
  97.5 12.5 %copy-start.3 = (f32[4,256,256]{2,1,0:T(8,128)}, f32[4,256,256]{2,1,0:T(8,128)S(1)}, u32[]{:S(2)}) copy-start(f32[4,256,256]{2,1,0:T(8,128)S(1)} %shard_map.55.refs_4_) | copy-start | bytes 3145732
  103.9 6.1 %copy-start.6 = (f32[64,4096]{1,0:T(8,128)S(1)}, f32[64,4096]{1,0:T(8,128)}, u32[]{:S(2)}) copy-start(f32[64,4096]{1,0:T(8,128)} %copy-done.5) | copy-start | bytes 3145732
  124.4 46.2 %all-to-all-start = ((f32[8,128,768]{2,1,0:T(8,128)}), f32[8,128,768]{2,1,0:T(8,128)}, u32[]{:S(2)}, u32[]{:S(2)}) async-start(f32[8,128,768]{2,1,0:T(8,128)} %all-gather.7.cloned.1.call-done), calls=%async_computation | async-start | bytes 6291456 | tf_op jit(solution)/shard_map/all_to_all | solution.py:209
  128.9 3.4 %collective-permute-start.11 = (f32[64,4096]{1,0:T(8,128)}, f32[64,4096]{1,0:T(8,128)}, u32[]{:S(2)}, u32[]{:S(2)}) collective-permute-start(f32[64,4096]{1,0:T(8,128)} %copy-done.11), channel_id=1, source_target_pairs={{0,1},{1,0},{2,3},{3,2},{4,5},{5,4},{6,7},{7,6},{8,9},{9,8},{10,11... | collective-permute-start | bytes 3145736 | tf_op jit(solution)/shard_map/ppermute | solution.py:141
  129.3 4.6 %collective-permute-start.12 = (f32[64,4096]{1,0:T(8,128)}, f32[64,4096]{1,0:T(8,128)}, u32[]{:S(2)}, u32[]{:S(2)}) collective-permute-start(f32[64,4096]{1,0:T(8,128)} %copy-done.9), channel_id=1, source_target_pairs={{0,1},{1,0},{2,3},{3,2},{4,5},{5,4},{6,7},{7,6},{8,9},{9,8},{10,11... | collective-permute-start | bytes 3145736 | tf_op jit(solution)/shard_map/ppermute | solution.py:141
  133.8 1.2 copy-start.4
  135.1 1.2 copy-start.10
  136.3 1.2 copy-start.12
  170.6 33.6 %all-to-all-start.3 = ((f32[8,128,512]{2,1,0:T(8,128)}), f32[8,128,512]{2,1,0:T(8,128)}, u32[]{:S(2)}, u32[]{:S(2)}) async-start(f32[8,128,512]{2,1,0:T(8,128)} %all-gather.11.cloned.1.call-done), calls=%async_computation.3 | async-start | bytes 4194304 | tf_op jit(solution)/shard_map/all_to_all | solution.py:209
  175.0 29.2 %all-gather.9.cloned.1.call-start = ((), (), s32[]{:S(2)}) async-start(), calls=%async_computation.6 | async-start | bytes 1310720 | tf_op jit(solution)/shard_map/all_gather | solution.py:157
  204.2 23.3 %all-to-all-start.2 = ((f32[8,128,256]{2,1,0:T(8,128)}), f32[8,128,256]{2,1,0:T(8,128)S(1)}, u32[]{:S(2)}, u32[]{:S(2)}) async-start(f32[8,128,256]{2,1,0:T(8,128)} %all-gather.9.cloned.1.call-done), calls=%async_computation.2 | async-start | bytes 2097152 | tf_op jit(solution)/shard_map/all_to_all | solution.py:209
  227.5 12.4 %copy-start.1 = (f32[2,128,512]{2,1,0:T(8,128)S(1)}, f32[2,128,512]{2,1,0:T(8,128)}, u32[]{:S(2)}) copy-start(f32[2,128,512]{2,1,0:T(8,128)} %param.8) | copy-start | bytes 1572868
Sparse Core Ops, SparseCore 0:
  9.0 51.2 all-gather.4
  61.9 62.5 all-gather.6
  126.0 44.5 all-gather.10
  177.1 27.0 all-gather.8
